TPU v7x, 128 devices: a whole 4x4x4 slice. The times are simulated.
128 devices in a mesh: cp: 32 (over z, x, core), hd: 4 (over y).
Axes of the slice: x: 4, y: 4, z: 4, core: 2. Of those that a mesh axis runs over, the one named last changes fastest.
Arguments:
- queries: bfloat16 [8192, 8192], P(('cp', 'hd')), may hold values from -3 to 3
- keys: bfloat16 [8192, 1024], P(('cp', 'hd')), may hold values from -3 to 3
- values: bfloat16 [8192, 1024], P(('cp', 'hd')), may hold values from -4 to 4
- fwd_out: bfloat16 [8192, 8192], P(('cp', 'hd')), may hold values from -4 to 4
- out_grad: bfloat16 [8192, 8192], P(('cp', 'hd')), may hold values from -4 to 4
- log_norm: float32 [8192, 64], P('cp', 'hd'), may hold values from 4 to 7
- doc_bounds: int32 [12], replicated, may hold values from 0 to 8192, as said below
- span_plan: int32 [32, 2], replicated, may hold values from 0 to 63, as said below
- read_lists: int32 [32, 2, 16], P('cp'), may hold values from -1 to 63, as said below
Outputs:
- grad_queries: bfloat16 [8192, 8192], P(('cp', 'hd'))
- grad_keys: bfloat16 [8192, 1024], P(('cp', 'hd'))
- grad_values: bfloat16 [8192, 1024], P(('cp', 'hd'))
Inputs may be any that keep to these rules, and one draw needn't show every extreme that they name: `doc_bounds`: rises from 0 to 8192; the first document has 127 tokens, the second exactly 1794, every later one 512 to 1794. `span_plan`: every span stands in exactly one slot. `read_lists`: for the span c in slot j of rank r: the spans from the one holding the start of the document of c's first token up to c, ascending, then -1 in the remaining entries; the number of spans is at most 16, and exactly 16 for span 16 - 1.
All inputs are finite; a program needn't handle non-finite values.
Results may differ from a plain program's by a relative error of at most 0.0054.
Values may be sent and summed in bfloat16 or wider, within the bound.
No kernel may reach another device: no remote copies, remote signals or barrier semaphores. Data moves between devices by JAX's collectives and lax.ppermute only.
A program may use at most 128 MiB of HBM per device.

v0:
```python
import jax
import jax.numpy as jnp
from jax import lax
from jax.sharding import PartitionSpec as P

HEAD_DIM = 128
SPAN = 128


def doc_index(bounds, places):
    return jnp.sum((bounds[None, 1:] <= places[:, None]).astype(jnp.int32), axis=1)


def tile_core(
    query_tile,
    grad_tile,
    lse_tile,
    delta_tile,
    query_place,
    query_doc,
    key_tile,
    value_tile,
    key_place,
    key_doc,
    is_live,
):
    factor = HEAD_DIM ** (-0.5)
    scores = (
        jnp.einsum("qgrd,kgd->grqk", query_tile, key_tile, preferred_element_type=jnp.float32)
        * factor
    )
    allowed = (
        (key_place[None, :] <= query_place[:, None])
        & (key_doc[None, :] == query_doc[:, None])
        & is_live
    )
    shifted = jnp.where(allowed, scores - lse_tile[..., None], 0.0)
    probs = jnp.where(allowed, jnp.exp(shifted), 0.0)
    dprob = jnp.einsum("qgrd,kgd->grqk", grad_tile, value_tile, preferred_element_type=jnp.float32)
    dscore = (probs * (dprob - delta_tile[..., None]) * factor).astype(jnp.bfloat16)
    return (probs.astype(jnp.bfloat16), dscore)


def add_rows(buffer, addend, first_row):
    current = lax.dynamic_slice_in_dim(buffer, first_row, addend.shape[0], 0)
    return lax.dynamic_update_slice_in_dim(buffer, current + addend, first_row, 0)


def shards(queries, keys, values, fwd_out, out_grad, log_norm, doc_bounds, span_plan, read_lists):
    cp_index = lax.axis_index("cp")
    query_local, key_local, value_local, output_local, grad_local = (
        lax.all_to_all(queries, "hd", split_axis=1, concat_axis=0, tiled=True),
        lax.all_to_all(keys, "hd", split_axis=1, concat_axis=0, tiled=True),
        lax.all_to_all(values, "hd", split_axis=1, concat_axis=0, tiled=True),
        lax.all_to_all(fwd_out, "hd", split_axis=1, concat_axis=0, tiled=True),
        lax.all_to_all(out_grad, "hd", split_axis=1, concat_axis=0, tiled=True),
    )
    weighted = output_local.astype(jnp.float32) * grad_local.astype(jnp.float32)
    delta = jnp.sum(weighted.reshape(weighted.shape[0], -1, HEAD_DIM), axis=2)
    row_total = query_local.shape[0]
    spans_here = row_total // SPAN
    kv_width = key_local.shape[1]
    kv_groups = kv_width // HEAD_DIM
    repeat = query_local.shape[1] // kv_width
    keys_all, values_all = (
        lax.all_gather(key_local, "cp", axis=0, tiled=True),
        lax.all_gather(value_local, "cp", axis=0, tiled=True),
    )
    gathered_rows = keys_all.shape[0]
    plan_flat = span_plan.reshape(-1)
    slot_range = jnp.arange(plan_flat.shape[0], dtype=jnp.int32)
    my_spans = lax.dynamic_slice_in_dim(span_plan, cp_index, 1, 0)[0]
    read_table = read_lists[0]
    live_table = read_table >= 0
    matches = plan_flat[None, None, :] == read_table[:, :, None]
    found_slots = jnp.sum(jnp.where(matches, slot_range, 0), axis=2)
    slot_table = jnp.where(live_table, found_slots, -1)
    offsets = lax.iota(jnp.int32, SPAN)
    lse_all = log_norm.reshape(spans_here, SPAN, kv_groups, repeat).transpose(0, 2, 3, 1)
    delta_all = delta.reshape(spans_here, SPAN, kv_groups, repeat).transpose(0, 2, 3, 1)

    def query_side(span_pos):
        query_tile = query_local[span_pos * SPAN : (span_pos + 1) * SPAN].reshape(
            SPAN, kv_groups, repeat, HEAD_DIM
        )
        grad_tile = grad_local[span_pos * SPAN : (span_pos + 1) * SPAN].reshape(
            SPAN, kv_groups, repeat, HEAD_DIM
        )
        query_place = my_spans[span_pos] * SPAN + offsets
        return (
            query_tile,
            grad_tile,
            lse_all[span_pos],
            delta_all[span_pos],
            query_place,
            doc_index(doc_bounds, query_place),
        )

    def kv_side(span_id, slot_now):
        first_row = jnp.maximum(slot_now, 0) * SPAN
        key_tile = lax.dynamic_slice_in_dim(keys_all, first_row, SPAN, 0).reshape(
            SPAN, kv_groups, HEAD_DIM
        )
        value_tile = lax.dynamic_slice_in_dim(values_all, first_row, SPAN, 0).reshape(
            SPAN, kv_groups, HEAD_DIM
        )
        key_place = span_id * SPAN + offsets
        return (key_tile, value_tile, key_place, doc_index(doc_bounds, key_place), slot_now >= 0)

    sides = [query_side(span_pos) for span_pos in range(spans_here)]
    grad_pieces = []
    zero_query = jnp.zeros((SPAN, kv_groups, repeat, HEAD_DIM), jnp.float32)
    empty_buffer = jnp.zeros((gathered_rows, kv_width), jnp.float32)
    sums_k, sums_v = (empty_buffer, empty_buffer)
    for span_pos in range(spans_here):

        def joint_step(entry_pos, carry, fixed=sides[span_pos], span_pos=span_pos):
            acc_query, acc_key, acc_value = carry
            slot_now = slot_table[span_pos, entry_pos]
            key_tile, value_tile, key_place, key_doc, is_live = kv_side(
                read_table[span_pos, entry_pos], slot_now
            )
            probs, dscore = tile_core(*fixed, key_tile, value_tile, key_place, key_doc, is_live)
            acc_query = acc_query + jnp.einsum(
                "grqk,kgd->qgrd", dscore, key_tile, preferred_element_type=jnp.float32
            )
            part_key = jnp.einsum(
                "grqk,qgrd->kgd", dscore, fixed[0], preferred_element_type=jnp.float32
            ).reshape(SPAN, kv_width)
            part_value = jnp.einsum(
                "grqk,qgrd->kgd", probs, fixed[1], preferred_element_type=jnp.float32
            ).reshape(SPAN, kv_width)
            first_row = jnp.maximum(slot_now, 0) * SPAN
            return (
                acc_query,
                add_rows(acc_key, part_key, first_row),
                add_rows(acc_value, part_value, first_row),
            )

        result = lax.fori_loop(0, read_table.shape[1], joint_step, (zero_query, sums_k, sums_v))
        grad_part, sums_k, sums_v = result
        grad_pieces.append(grad_part)
    grad_key, grad_value = (
        lax.psum_scatter(sums_k, "cp", scatter_dimension=0, tiled=True),
        lax.psum_scatter(sums_v, "cp", scatter_dimension=0, tiled=True),
    )
    grad_query = jnp.concatenate(grad_pieces, axis=0).reshape(row_total, -1).astype(jnp.bfloat16)
    grad_queries, grad_keys, grad_values = (
        lax.all_to_all(grad_query, "hd", split_axis=0, concat_axis=1, tiled=True),
        lax.all_to_all(
            grad_key.astype(jnp.bfloat16), "hd", split_axis=0, concat_axis=1, tiled=True
        ),
        lax.all_to_all(
            grad_value.astype(jnp.bfloat16), "hd", split_axis=0, concat_axis=1, tiled=True
        ),
    )
    return (grad_queries, grad_keys, grad_values)


def solution(mesh):
    in_specs = (
        P(("cp", "hd"), None),
        P(("cp", "hd"), None),
        P(("cp", "hd"), None),
        P(("cp", "hd"), None),
        P(("cp", "hd"), None),
        P("cp", "hd"),
        P(),
        P(),
        P("cp", None, None),
    )
    out_specs = (P(("cp", "hd"), None), P(("cp", "hd"), None), P(("cp", "hd"), None))
    return jax.shard_map(shards, mesh=mesh, in_specs=in_specs, out_specs=out_specs, check_vma=False)
```

profile of v0, /device:TPU:0, one launch (start us, length us, event | category | flops | bytes accessed | tf_op | source)
XLA Modules:
  0.0 686.1 jit_solution(1670976854283357632)
XLA Ops:
  8.2 10.4 %all_to_all.137 = bf16[64,4,256]{2,0,1:T(8,128)(2,1)} all-to-all(bf16[64,4,256]{2,0,1:T(8,128)(2,1)S(1)} %bitcast.309), channel_id=1, replica_groups=mesh['cp'=32,'hd'=4] {'hd'}, dimensions={1} | all-to-all | bytes 262144 | tf_op jit(solution)/shard_map/all_to_all | solution.py:53
  19.7 9.0 %all_to_all.138 = bf16[64,4,256]{2,0,1:T(8,128)(2,1)} all-to-all(bf16[64,4,256]{2,0,1:T(8,128)(2,1)S(1)} %bitcast.310), channel_id=1, replica_groups=mesh['cp'=32,'hd'=4] {'hd'}, dimensions={1} | all-to-all | bytes 262144 | tf_op jit(solution)/shard_map/all_to_all | solution.py:54
  31.0 3.5 all-to-all-start.3
  42.1 5.2 all-to-all-done.3
  47.3 3.5 all-to-all-start.4
  51.1 11.2 %all-to-all-done.4 = bf16[64,4,2048]{2,0,1:T(8,128)(2,1)S(1)} async-done(((bf16[64,4,2048]{2,0,1:T(8,128)(2,1)}), bf16[64,4,2048]{2,0,1:T(8,128)(2,1)S(1)}, u32[]{:S(2)}, u32[]{:S(2)}) %all-to-all-start.4) | async-done | bytes 1048608 | tf_op jit(solution)/shard_map/all_to_all | solution.py:55
  62.4 4.3 all-to-all-start.1
  71.8 5.8 all-to-all-done.1
  83.3 6.4 copy.198
  89.8 23.8 %all-gather.5.cloned.1.call-done = bf16[8192,256]{1,0:T(8,128)(2,1)} async-done(((bf16[256,256]{1,0:T(8,128)(2,1)}), bf16[8192,256]{1,0:T(8,128)(2,1)}) %all-gather.5.cloned.1.call-update) | async-done | bytes 4194320 | tf_op jit(solution)/shard_map/all_gather | solution.py:67
  113.6 6.4 copy.201
  119.9 4.2 broadcast_in_dim.93
  124.1 4.2 broadcast_in_dim.93.clone
  128.4 202.3 %while.36 = (s32[]{:T(128)}, f32[128,2,8,128]{0,3,2,1:T(8,128)}, f32[8192,256]{0,1:T(8,128)}, f32[8192,256]{0,1:T(8,128)}, s32[2,16]{1,0:T(2,128)S(1)}, /*index=...) while((s32[]{:T(128)}, f32[128,2,8,128]{0,3,2,1:T(8,128)}, ...), condition=%wide.region_5.6_spmd.clone, body=%wide.region_3.5_spmd.clone.sunk | while | flops 338563328 | bytes 10473899 | solution.py:140
  150.1 2.5 fusion.109
  330.7 138.9 %while.37 = (s32[]{:T(128)}, f32[128,2,8,128]{0,3,2,1:T(8,128)S(1)}, f32[8192,256]{0,1:T(8,128)}, f32[8192,256]{0,1:T(8,128)}, s32[2,16]{1,0:T(2,128)S(1)}, /*in...) while((s32[]{:T(128)}, ...), condition=%wide.region_9.10_spmd.clone, body=%wide.region_7.9_spmd.clone.sunk | while | flops 338563328 | bytes 10473899 | solution.py:140
  469.6 9.0 %copy.212 = f32[8192,256]{1,0:T(8,128)} copy(f32[8192,256]{0,1:T(8,128)} %get-tuple-element.529) | data formatting | bytes 16777216 | tf_op jit(solution)/shard_map/while | solution.py:140
  478.7 9.0 %copy.214 = f32[8192,256]{1,0:T(8,128)} copy(f32[8192,256]{0,1:T(8,128)} %get-tuple-element.530) | data formatting | bytes 16777216 | tf_op jit(solution)/shard_map/while | solution.py:140
  491.6 4.2 all-to-all-start.5
  495.8 75.1 %reduce-scatter.3.cloned.1.call-done = f32[256,256]{1,0:T(8,128)} async-done(((f32[8192,256]{1,0:T(8,128)}), f32[256,256]{1,0:T(8,128)}) %reduce-scatter.3.cloned.1.call-update) | async-done | bytes 262160 | tf_op jit(solution)/shard_map/reduce_scatter | solution.py:144
  572.5 4.3 all-to-all-start.6
  576.8 90.2 %reduce-scatter.5.cloned.1.call-done = f32[256,256]{1,0:T(8,128)} async-done(((f32[8192,256]{1,0:T(8,128)}), f32[256,256]{1,0:T(8,128)}) %reduce-scatter.5.cloned.1.call-update) | async-done | bytes 262160 | tf_op jit(solution)/shard_map/reduce_scatter | solution.py:145
  668.7 4.3 all-to-all-start.7
  674.7 4.2 all-to-all-done.7
  (544 shorter events, 328.4 us)
Async XLA Ops:
  7.2 33.9 %copy-start.1 = (bf16[64,8192]{1,0:T(8,128)(2,1)S(1)}, bf16[64,8192]{1,0:T(8,128)(2,1)}, u32[]{:S(2)}) copy-start(bf16[64,8192]{1,0:T(8,128)(2,1)} %param.13) | copy-start | bytes 3145732
  7.2 34.9 %copy-start.2 = (f32[256,16]{0,1:T(8,128)S(1)}, f32[256,16]{0,1:T(8,128)}, u32[]{:S(2)}) copy-start(f32[256,16]{0,1:T(8,128)} %param.18) | copy-start | bytes 49156
  7.2 43.7 %copy-start.3 = (s32[1,2,16]{2,1,0:T(2,128)S(1)}, s32[1,2,16]{2,1,0:T(2,128)}, u32[]{:S(2)}) copy-start(s32[1,2,16]{2,1,0:T(2,128)} %param.21) | copy-start | bytes 388
  7.2 76.1 %all-gather.3.cloned.1.call-start = ((), (), s32[]{:S(2)}) async-start(), calls=%async_computation.10 | async-start | bytes 4325376 | tf_op jit(solution)/shard_map/all_gather | solution.py:66
  18.7 94.9 %all-gather.5.cloned.1.call-start = ((), (), s32[]{:S(2)}) async-start(), calls=%async_computation.11 | async-start | bytes 4325376 | tf_op jit(solution)/shard_map/all_gather | solution.py:67
  31.0 16.3 %all-to-all-start.3 = ((bf16[64,4,2048]{2,0,1:T(8,128)(2,1)}), bf16[64,4,2048]{2,0,1:T(8,128)(2,1)S(1)}, u32[]{:S(2)}, u32[]{:S(2)}) async-start(bf16[64,4,2048]{2,0,1:T(8,128)(2,1)} %bitcast.203), calls=%async_computation.3 | async-start | bytes 2097152 | tf_op jit(solution)/shard_map/all_to_all | solution.py:56
  47.3 15.0 %all-to-all-start.4 = ((bf16[64,4,2048]{2,0,1:T(8,128)(2,1)}), bf16[64,4,2048]{2,0,1:T(8,128)(2,1)S(1)}, u32[]{:S(2)}, u32[]{:S(2)}) async-start(bf16[64,4,2048]{2,0,1:T(8,128)(2,1)} %bitcast.202), calls=%async_computation.4 | async-start | bytes 2097152 | tf_op jit(solution)/shard_map/all_to_all | solution.py:55
  62.4 15.2 %all-to-all-start.1 = ((bf16[64,4,2048]{2,0,1:T(8,128)(2,1)}), bf16[64,4,2048]{2,0,1:T(8,128)(2,1)}, u32[]{:S(2)}, u32[]{:S(2)}) async-start(bf16[64,4,2048]{2,0,1:T(8,128)(2,1)} %bitcast.204), calls=%async_computation.1 | async-start | bytes 2097152 | tf_op jit(solution)/shard_map/all_to_all | solution.py:52
  66.6 504.3 %reduce-scatter.3.cloned.1.call-start = ((), (), s32[]{:S(2)}) async-start(), calls=%async_computation.12 | async-start | bytes 8650752 | tf_op jit(solution)/shard_map/reduce_scatter | solution.py:144
  119.9 8.4 %copy-start.4 = (s32[12]{0:T(128)S(1)}, s32[12]{0:T(128)}, u32[]{:S(2)}) copy-start(s32[12]{0:T(128)} %param.19) | copy-start | bytes 148
  478.6 188.4 %reduce-scatter.5.cloned.1.call-start = ((), (), s32[]{:S(2)}) async-start(), calls=%async_computation.13 | async-start | bytes 8650752 | tf_op jit(solution)/shard_map/reduce_scatter | solution.py:145
  487.7 1.3 copy-start
  491.6 81.0 %all-to-all-start.5 = ((bf16[4,64,2048]{2,1,0:T(8,128)(2,1)}), bf16[4,64,2048]{2,1,0:T(8,128)(2,1)S(1)}, u32[]{:S(2)}, u32[]{:S(2)}) async-start(bf16[4,64,2048]{2,1,0:T(8,128)(2,1)} %convert_element_type.77), calls=%async_computation.5 | async-start | bytes 2097152 | tf_op jit(solution)/shard_map/all_to_all | solution.py:149
  572.5 96.1 %all-to-all-start.6 = ((bf16[4,64,256]{2,1,0:T(8,128)(2,1)}), bf16[4,64,256]{2,1,0:T(8,128)(2,1)S(1)}, u32[]{:S(2)}, u32[]{:S(2)}) async-start(bf16[4,64,256]{2,1,0:T(8,128)(2,1)} %bitcast.17), calls=%async_computation.7 | async-start | bytes 262144 | tf_op jit(solution)/shard_map/all_to_all | solution.py:150
  668.7 10.3 %all-to-all-start.7 = ((bf16[4,64,256]{2,1,0:T(8,128)(2,1)}), bf16[4,64,256]{2,1,0:T(8,128)(2,1)S(1)}, u32[]{:S(2)}, u32[]{:S(2)}) async-start(bf16[4,64,256]{2,1,0:T(8,128)(2,1)} %bitcast.19), calls=%async_computation.9 | async-start | bytes 262144 | tf_op jit(solution)/shard_map/all_to_all | solution.py:153
Sparse Core Ops, SparseCore 0:
  18.8 46.7 all-gather.2
  67.8 45.6 all-gather.4
  478.7 92.1 reduce-scatter.2
  574.9 92.0 reduce-scatter.4
where the time goes:
time: 694 us; the launch traced here: 686 us
  waiting for transfers between devices  216 us (31%)
  other arithmetic  127 us (18%)
  matrix products  122 us (18%)
  local copies, waits for them, and re-layouts  121 us (17%)
  loops' own time  41.7 us (6%)
  starting transfers between devices  24.3 us (4%)
  blocking collectives  19.5 us (3%)
  between operations  15.2 us (2%)
    reduce_scatter x1, waiting for transfers between devices, shards(): lax.psum_scatter(sums_v, 'cp', scatter_dimension=0, tiled=True)  90.2 us
    reduce_scatter x1, waiting for transfers between devices, shards(): lax.psum_scatter(sums_k, 'cp', scatter_dimension=0, tiled=True)  75.1 us
    dynamic_update_slice x32, other arithmetic, add_rows(): lax.dynamic_update_slice_in_dim(buffer, current + addend, first_row, 0)  55.4 us
    dot_general x32, matrix products, joint_step(): jnp.einsum('grqk,kgd->qgrd', dscore, key_tile, preferred_element_type=jnp...  45.5 us
    another operation x2, loops' own time, shards(): lax.fori_loop(0, read_table.shape[1], joint_step, (zero_query, sums_k, su...  41.7 us
    dot_general x32, matrix products, tile_core(): jnp.einsum('qgrd,kgd->grqk', query_tile, key_tile, preferred_element_type...  30.3 us
    dynamic_slice x32, local copies, waits for them, and re-layouts, kv_side(): lax.dynamic_slice_in_dim(values_all, first_row, SPAN, 0)  27.3 us
    dynamic_slice x32, local copies, waits for them, and re-layouts, kv_side(): lax.dynamic_slice_in_dim(keys_all, first_row, SPAN, 0)  27.2 us
  transfers between devices with their start and end apart: 10, of which 7 were waited for; matrix products, arithmetic and copies ran while one was open for 6% of the time, Pallas kernels for 0%

commit v1 on v0

v1 whole, which is shorter than its diff:
```python
import jax
import jax.numpy as jnp
from jax import lax
from jax.experimental import pallas as pl
from jax.experimental.pallas import tpu as pltpu
from jax.sharding import Mesh, PartitionSpec as P

HEAD_DIM = 128
SPAN = 128
HALF = 64
SLAB = 2048
LANES = 512
PACKED = 528
ROWS = ("z", "x", "c", "y")
MIB = 1024 * 1024


def dot(a, b, ca, cb):
    return lax.dot_general(a, b, (((ca,), (cb,)), ((), ())), preferred_element_type=jnp.float32)


def pack_kv_kernel(keys_ref, values_ref, out_ref):
    for x in range(4):
        for y in range(4):
            cols = slice((2 * y + x // 2) * HEAD_DIM, (2 * y + x // 2 + 1) * HEAD_DIM)
            out_ref[x, 0, y] = keys_ref[:, cols]
            out_ref[x, 1, y] = values_ref[:, cols]


def pack_q_kernel(queries_ref, grad_ref, fwd_ref, out_ref):
    row = lax.broadcasted_iota(jnp.int32, (16, HEAD_DIM), 0)
    for x in range(4):
        delta = jnp.zeros((16, HALF), jnp.float32)
        for h in range(4):
            cols = slice((x * 4 + h) * HEAD_DIM, (x * 4 + h + 1) * HEAD_DIM)
            grad = grad_ref[:, cols]
            out_ref[x, 0, h * HALF : (h + 1) * HALF] = queries_ref[:, cols]
            out_ref[x, 0, 256 + h * HALF : 256 + (h + 1) * HALF] = grad
            product = grad.astype(jnp.float32) * fwd_ref[:, cols].astype(jnp.float32)
            high = product.astype(jnp.bfloat16)
            low = (product - high.astype(jnp.float32)).astype(jnp.bfloat16)
            pick = (row == h).astype(jnp.bfloat16)
            delta = delta + dot(pick, high, 1, 1) + dot(pick, low, 1, 1)
        high = delta.astype(jnp.bfloat16)
        low = (delta - high.astype(jnp.float32)).astype(jnp.bfloat16)
        out_ref[x, 0, 512:PACKED] = jnp.concatenate([high, low], axis=1)


def unpack_q_kernel(in_ref, out_ref):
    for x in range(4):
        for h in range(4):
            cols = slice((x * 4 + h) * HEAD_DIM, (x * 4 + h + 1) * HEAD_DIM)
            out_ref[:, cols] = in_ref[x, 0, h * HALF : (h + 1) * HALF]


def unpack_kv_kernel(in_ref, keys_ref, values_ref):
    for g in range(8):
        cols = slice(g * HEAD_DIM, (g + 1) * HEAD_DIM)
        y, x = g // 2, 2 * (g % 2)
        for c, out_ref in ((0, keys_ref), (1, values_ref)):
            total = in_ref[x, c, y].astype(jnp.float32) + in_ref[x + 1, c, y].astype(jnp.float32)
            out_ref[:, cols] = total.astype(jnp.bfloat16)


PIECES = ((0, SLAB), (SLAB, SLAB), (2 * SLAB, SLAB // 2), (2 * SLAB + SLAB // 2, SLAB // 2), (3 * SLAB, SLAB))


def main_kernel(where_ref, plan_ref, bounds_ref, packed_ref, lse_ref, delta_ref, *rest):
    mine = rest[0:5]
    other = rest[5:10]
    dq_ref = rest[10]
    keep = rest[11:16]
    send = rest[16:21]
    key_ref, value_ref, dk_ref, dv_ref, dq_sum, slot_ref, sems = rest[21:]
    z, c = where_ref[0], where_ref[1]
    factor = HEAD_DIM ** (-0.5)

    def fetch(first, second):
        copies = []
        for i, (start, size) in enumerate(PIECES):
            rows = pl.ds(start, size)
            copies.append(pltpu.make_async_copy(mine[i], first.at[rows], sems.at[i]))
            copies.append(pltpu.make_async_copy(other[i], second.at[rows], sems.at[5 + i]))
        for copy in copies:
            copy.start()
        return copies

    def fetch_all(first, second):
        copies = fetch(first, second)
        for copy in copies:
            copy.wait()

    dk_ref[...] = jnp.zeros_like(dk_ref)
    dv_ref[...] = jnp.zeros_like(dv_ref)

    def note_slot(slot, carry):
        slot_ref[plan_ref[slot]] = slot
        return carry

    lax.fori_loop(0, 64, note_slot, 0)

    @pl.when(c == 0)
    def _():
        fetch_all(key_ref, value_ref)

    @pl.when(c == 1)
    def _():
        fetch_all(value_ref, key_ref)

    lane = lax.broadcasted_iota(jnp.int32, (1, LANES), 1)
    within = (lane // 256) * HALF + lane % HALF
    row = lax.broadcasted_iota(jnp.int32, (SPAN, LANES), 0)

    def first_row(span):
        slot = slot_ref[span]
        slab = lax.rem(lax.shift_right_logical(slot, 4) - z + 4, 4)
        return pl.multiple_of(slab * SLAB + (slot & 15) * SPAN, SPAN)

    def query_span(s, carry):
        span = plan_ref[(z * 4 + lax.shift_right_logical(s, 1)) * 4 + c * 2 + (s & 1)]
        last = span * SPAN + within
        first = jnp.zeros_like(last)
        first_doc = jnp.int32(0)
        for i in range(1, 12):
            bound = bounds_ref[i]
            first = jnp.where(bound <= last, jnp.maximum(first, bound), first)
            first_doc = jnp.where(bound <= span * SPAN, jnp.maximum(first_doc, bound), first_doc)
        begin = lax.shift_right_logical(first_doc, 7)
        count = span - begin + 1
        queries = jnp.concatenate([packed_ref[2 * s, 0:256], packed_ref[2 * s + 1, 0:256]], axis=0)
        grads = jnp.concatenate([packed_ref[2 * s, 256:512], packed_ref[2 * s + 1, 256:512]], axis=0)
        lse = lse_ref[pl.ds(s, 1), :]
        delta = delta_ref[pl.ds(s, 1), :]
        dq_sum[...] = jnp.zeros_like(dq_sum)

        def pair(i, carry):
            span_a = begin + 2 * i
            has_b = span_a < span
            span_b = jnp.where(has_b, span_a + 1, span_a)
            base_a = span_a * SPAN
            base_b = jnp.where(has_b, span_b * SPAN, 8192)
            row_a = first_row(span_a)
            row_b = first_row(span_b)
            key = jnp.concatenate([key_ref[pl.ds(row_a, SPAN), :], key_ref[pl.ds(row_b, SPAN), :]], axis=0)
            value = jnp.concatenate([value_ref[pl.ds(row_a, SPAN), :], value_ref[pl.ds(row_b, SPAN), :]], axis=0)
            allowed = jnp.concatenate(
                [
                    (row >= first - base_a) & (row <= last - base_a),
                    (row >= first - base_b) & (row <= last - base_b),
                ],
                axis=0,
            )
            scores = dot(key, queries, 1, 1)
            probs = jnp.where(allowed, jnp.exp(scores * factor - lse), 0.0)
            dprob = dot(value, grads, 1, 1)
            dscore = (probs * (dprob - delta)).astype(jnp.bfloat16)
            part_v = dot(probs.astype(jnp.bfloat16), grads, 1, 0)
            part_k = dot(dscore, queries, 1, 0)
            dq_sum[...] += dot(dscore, key, 0, 0)
            dk_ref[pl.ds(row_a, SPAN), :] += part_k[:SPAN]
            dv_ref[pl.ds(row_a, SPAN), :] += part_v[:SPAN]
            dk_ref[pl.ds(row_b, SPAN), :] += part_k[SPAN:]
            dv_ref[pl.ds(row_b, SPAN), :] += part_v[SPAN:]
            return carry

        lax.fori_loop(0, lax.shift_right_logical(count + 1, 1), pair, 0)
        dq = (dq_sum[...] * factor).astype(jnp.bfloat16)
        dq_ref[2 * s] = dq[:256]
        dq_ref[2 * s + 1] = dq[256:]
        return carry

    lax.fori_loop(0, 8, query_span, 0)

    def write(key_outs, value_outs):
        for i, (start, size) in enumerate(PIECES):
            for j in range(0, size, 512):
                rows = slice(start + j, start + j + 512)
                key_outs[i][j : j + 512] = (dk_ref[rows] * factor).astype(jnp.bfloat16)
                value_outs[i][j : j + 512] = dv_ref[rows].astype(jnp.bfloat16)

    @pl.when(c == 0)
    def _():
        write(keep, send)

    @pl.when(c == 1)
    def _():
        write(send, keep)


def shift(array, axis, by):
    return lax.ppermute(array, axis, [(i, (i + by) % 4) for i in range(4)])


def swap(array):
    return lax.ppermute(array, "c", [(0, 1), (1, 0)])


def exchange(array, axes):
    return lax.all_to_all(array, axes, 0, 0, tiled=True)


def shards(queries, keys, values, fwd_out, out_grad, log_norm, doc_bounds, span_plan, read_lists):
    bf16 = jnp.bfloat16
    vmem = pl.BlockSpec(memory_space=pltpu.VMEM)
    smem = pl.BlockSpec(memory_space=pltpu.SMEM)
    anywhere = pl.BlockSpec(memory_space=pl.ANY)
    z, x, c = lax.axis_index("z"), lax.axis_index("x"), lax.axis_index("c")

    kv_out = pl.pallas_call(
        pack_kv_kernel,
        out_shape=jax.ShapeDtypeStruct((4, 2, 4, HALF, HEAD_DIM), bf16),
        in_specs=[vmem, vmem],
        out_specs=vmem,
        name="pack_kv",
    )(keys, values)
    block = exchange(kv_out.reshape(32, HALF, HEAD_DIM), ("x", "c", "y")).reshape(SLAB, HEAD_DIM)

    wide = pl.BlockSpec((HALF, 16 * HEAD_DIM), lambda y: (0, y))
    q_out = pl.pallas_call(
        pack_q_kernel,
        grid=(4,),
        out_shape=jax.ShapeDtypeStruct((4, 4, PACKED, HEAD_DIM), bf16),
        in_specs=[wide, wide, wide],
        out_specs=pl.BlockSpec((4, 1, PACKED, HEAD_DIM), lambda y: (0, y, 0, 0)),
        name="pack_q",
    )(queries, out_grad, fwd_out)
    packed = exchange(q_out.reshape(16, PACKED, HEAD_DIM), ("x", "y"))

    all_lse = lax.all_gather(log_norm.T, "x", axis=0, tiled=False)
    lse = lax.dynamic_slice_in_dim(all_lse, x * 4, 4, 1)
    lse = lse.reshape(4, 4, 2, 2, HALF).transpose(0, 2, 3, 1, 4).reshape(8, LANES)

    from_next = shift(block, "z", -1)
    from_last = shift(block, "z", 1)
    far_a = shift(from_next[: SLAB // 2], "z", -1)
    far_b = shift(from_last[SLAB // 2 :], "z", 1)
    mine = [block, from_next, far_a, far_b, from_last]
    other = [swap(part) for part in mine]

    delta = packed[:, 512:516, :HALF].astype(jnp.float32) + packed[:, 512:516, HALF:].astype(jnp.float32)
    delta = delta.reshape(8, LANES)

    where = jnp.stack([z, c]).astype(jnp.int32)
    pieces = [jax.ShapeDtypeStruct((size, HEAD_DIM), bf16) for _, size in PIECES]
    outs = pl.pallas_call(
        main_kernel,
        out_shape=[jax.ShapeDtypeStruct((16, 256, HEAD_DIM), bf16)] + pieces + pieces,
        in_specs=[smem, smem, smem, vmem, vmem, vmem] + [anywhere] * 10,
        out_specs=[vmem] * 11,
        scratch_shapes=[
            pltpu.VMEM((4 * SLAB, HEAD_DIM), bf16),
            pltpu.VMEM((4 * SLAB, HEAD_DIM), bf16),
            pltpu.VMEM((4 * SLAB, HEAD_DIM), jnp.float32),
            pltpu.VMEM((4 * SLAB, HEAD_DIM), jnp.float32),
            pltpu.VMEM((LANES, HEAD_DIM), jnp.float32),
            pltpu.SMEM((64,), jnp.int32),
            pltpu.SemaphoreType.DMA((10,)),
        ],
        compiler_params=pltpu.CompilerParams(vmem_limit_bytes=48 * MIB),
        name="tiles",
    )(where, span_plan.reshape(-1), doc_bounds, packed, lse, delta, *mine, *other)
    dq, keep, send = outs[0], outs[1:6], outs[6:11]

    dq_back = exchange(dq, ("x", "y")).reshape(4, 4, 256, HEAD_DIM)
    grad_queries = pl.pallas_call(
        unpack_q_kernel,
        grid=(4,),
        out_shape=jax.ShapeDtypeStruct((HALF, 64 * HEAD_DIM), bf16),
        in_specs=[pl.BlockSpec((4, 1, 256, HEAD_DIM), lambda y: (0, y, 0, 0))],
        out_specs=wide,
        name="unpack_q",
    )(dq_back)

    f32 = jnp.float32
    got = [swap(part) for part in send]
    far_a = (keep[2].astype(f32) + got[2].astype(f32)).astype(bf16)
    far_b = (keep[3].astype(f32) + got[3].astype(f32)).astype(bf16)
    via_next = shift(far_a, "z", 1)
    via_last = shift(far_b, "z", -1)
    half = SLAB // 2
    to_next = keep[1].astype(f32) + got[1].astype(f32)
    to_next = jnp.concatenate([to_next[:half] + via_next.astype(f32), to_next[half:]], axis=0).astype(bf16)
    to_last = keep[4].astype(f32) + got[4].astype(f32)
    to_last = jnp.concatenate([to_last[:half], to_last[half:] + via_last.astype(f32)], axis=0).astype(bf16)
    near = shift(to_next, "z", 1).astype(f32) + shift(to_last, "z", -1).astype(f32)
    total = (keep[0].astype(f32) + got[0].astype(f32) + near).astype(bf16)
    kv_back = exchange(total.reshape(32, HALF, HEAD_DIM), ("x", "c", "y"))
    grad_keys, grad_values = pl.pallas_call(
        unpack_kv_kernel,
        out_shape=[jax.ShapeDtypeStruct((HALF, 8 * HEAD_DIM), bf16)] * 2,
        in_specs=[vmem],
        out_specs=[vmem, vmem],
        name="unpack_kv",
    )(kv_back.reshape(4, 2, 4, HALF, HEAD_DIM))
    return (grad_queries, grad_keys, grad_values)


def solution(mesh):
    fine = Mesh(mesh.devices.reshape(4, 4, 2, 4), ROWS)
    rows = P(ROWS, None)
    cp = ("z", "x", "c")
    in_specs = (rows, rows, rows, rows, rows, P(cp, "y"), P(), P(), P(cp, None, None))
    return jax.shard_map(shards, mesh=fine, in_specs=in_specs, out_specs=(rows, rows, rows), check_vma=False)
```

time: 694 us -> 148 us (0.21)
  waiting for transfers between devices: 216 us -> 48.2 us
  matrix products: 122 us -> 0 us
  other arithmetic: 127 us -> 5.24 us
  local copies, waits for them, and re-layouts: 121 us -> 2.14 us
  loops' own time: 41.7 us -> 0 us
  Pallas kernels: 0 us -> 38.8 us
  between operations: 15.2 us -> 0.88 us
  starting transfers between devices: 24.3 us -> 36.6 us
    reduce_scatter x2 -> x0, waiting for transfers between devices: 165 us -> none  [the longest x1 90.2 us: shards(): lax.psum_scatter(sums_v, 'cp', scatter_dimension=0, tiled=True)]
    dot_general x160 -> x0, matrix products: 122 us -> none  [the longest x32 45.5 us: joint_step(): jnp.einsum('grqk,kgd->qgrd', dscore, key_tile, preferred_element_type=jnp...]
    dynamic_update_slice x32 -> x0, other arithmetic: 55.4 us -> none  [add_rows(): lax.dynamic_update_slice_in_dim(buffer, current + addend, first_row, 0)]
    dynamic_slice x65 -> x1, local copies, waits for them, and re-layouts: 55.2 us -> 0.01 us  [shards(): lse = lax.dynamic_slice_in_dim(all_lse, x * 4, 4, 1)]
    another operation x2 -> x0, loops' own time: 41.7 us -> none  [shards(): lax.fori_loop(0, read_table.shape[1], joint_step, (zero_query, sums_k, su...]
    pallas_call x0 -> x5, Pallas kernels: none -> 38.8 us  [the longest x1 26.9 us: shards(): pl.pallas_call(main_kernel, out_shape=[jax.ShapeDtypeStruct((16, 256, HEA...]
    ppermute x0 -> x18, waiting for transfers between devices: none -> 24.4 us  [the longest x8 23 us: shift(): return lax.ppermute(array, axis, [(i, (i + by) % 4) for i in range(4)])]
    all_gather x2 -> x0, waiting for transfers between devices: 23.8 us -> none  [the longest x1 23.8 us: shards(): lax.all_gather(value_local, 'cp', axis=0, tiled=True)]
  transfers between devices with their start and end apart: 10 -> 22, of which waited for: 7 -> 9; matrix products, arithmetic and copies ran while one was open for 6% -> 4% of each run, Pallas kernels for 0% -> 6%
where the time goes in v1:
time: 148 us; the launch traced here: 146 us
  waiting for transfers between devices  48.2 us (33%)
  Pallas kernels  38.8 us (26%)
  starting transfers between devices  36.6 us (25%)
  blocking collectives  14.3 us (10%)
  other arithmetic  5.24 us (4%)
  local copies, waits for them, and re-layouts  2.14 us (1%)
    pallas_call x1, Pallas kernels, shards(): pl.pallas_call(main_kernel, out_shape=[jax.ShapeDtypeStruct((16, 256, HEA...  26.9 us
    all_to_all x4, waiting for transfers between devices, exchange(): return lax.all_to_all(array, axes, 0, 0, tiled=True)  23.8 us
    ppermute x8, waiting for transfers between devices, shift(): return lax.ppermute(array, axis, [(i, (i + by) % 4) for i in range(4)])  23 us
    all_to_all x4, starting transfers between devices, exchange(): return lax.all_to_all(array, axes, 0, 0, tiled=True)  21.1 us
    all_gather x1, blocking collectives, shards(): all_lse = lax.all_gather(log_norm.T, 'x', axis=0, tiled=False)  14.3 us
    ppermute x8, starting transfers between devices, shift(): return lax.ppermute(array, axis, [(i, (i + by) % 4) for i in range(4)])  13.2 us
    pallas_call x1, Pallas kernels, shards(): pl.pallas_call(pack_q_kernel, grid=(4,), out_shape=jax.ShapeDtypeStruct((...  4.91 us
    pallas_call x1, Pallas kernels, shards(): pl.pallas_call(unpack_q_kernel, grid=(4,), out_shape=jax.ShapeDtypeStruct...  3.43 us
  transfers between devices with their start and end apart: 22, of which 9 were waited for; matrix products, arithmetic and copies ran while one was open for 4% of the time, Pallas kernels for 6%

profile of v1, /device:TPU:0, one launch (start us, length us, event | category | flops | bytes accessed | tf_op | source)
XLA Modules:
  0.0 146.2 jit_solution(16255237424865718790)
XLA Ops:
  0.6 1.8 %pack_kv.1 = bf16[4,2,4,64,128]{4,3,2,1,0:T(8,128)(2,1)} custom-call(bf16[64,1024]{1,0:T(8,128)(2,1)} %keys_ref.1, bf16[64,1024]{1,0:T(8,128)(2,1)} %values_ref.1), custom_call_target="tpu_custom_call" | custom-call | tf_op jit(solution)/shard_map/pack_kv/pallas_call | solution.py:209
  2.5 7.4 %all-to-all-start.1 = ((bf16[32,64,128]{2,1,0:T(8,128)(2,1)}), bf16[32,64,128]{2,1,0:T(8,128)(2,1)S(1)}, u32[]{:S(2)}, u32[]{:S(2)}) async-start(bf16[32,64,128]{2,1,0:T(8,128)(2,1)} %bitcast.18), calls=%async_computation.1 | async-start | bytes 1048576 | tf_op jit(solution)/shard_map/all_to_all | solution.py:199
  9.9 4.9 %pack_q.1 = bf16[4,4,528,128]{3,2,1,0:T(8,128)(2,1)} custom-call(bf16[64,8192]{1,0:T(8,128)(2,1)} %queries_ref.1, bf16[64,8192]{1,0:T(8,128)(2,1)} %grad_ref.1, bf16[64,8192]{1,0:T(8,128)(2,1)} %fwd_ref.1), custom_call_target="tpu_custom_call" | custom-call | tf_op jit(solution)/shard_map/pack_q/pallas_call | solution.py:219
  14.8 6.9 %all-to-all-done.1 = bf16[32,64,128]{2,1,0:T(8,128)(2,1)S(1)} async-done(((bf16[32,64,128]{2,1,0:T(8,128)(2,1)}), bf16[32,64,128]{2,1,0:T(8,128)(2,1)S(1)}, u32[]{:S(2)}, u32[]{:S(2)}) %all-to-all-start.1) | async-done | bytes 524320 | tf_op jit(solution)/shard_map/all_to_all | solution.py:199
  21.7 4.6 %all-to-all-start = ((bf16[16,528,128]{2,1,0:T(8,128)(2,1)}), bf16[16,528,128]{2,1,0:T(8,128)(2,1)}, u32[]{:S(2)}, u32[]{:S(2)}) async-start(bf16[16,528,128]{2,1,0:T(8,128)(2,1)} %bitcast.15), calls=%async_computation | async-start | bytes 4325376 | tf_op jit(solution)/shard_map/all_to_all | solution.py:199
  26.2 2.0 %collective-permute-start.2 = (bf16[2048,128]{1,0:T(8,128)(2,1)S(1)}, bf16[2048,128]{1,0:T(8,128)(2,1)S(1)}, u32[]{:S(2)}, u32[]{:S(2)}) collective-permute-start(bf16[2048,128]{1,0:T(8,128)(2,1)S(1)} %bitcast.11), channel_id=1, source_target_pairs={{0,32},{32,64},{64,96},{96,0},{1,33},{33,65},{65,97},{97,1},{2,34}... | collective-permute-start | bytes 1572872 | tf_op jit(solution)/shard_map/ppermute | solution.py:191
  28.2 2.2 %collective-permute-start = (bf16[2048,128]{1,0:T(8,128)(2,1)S(1)}, bf16[2048,128]{1,0:T(8,128)(2,1)S(1)}, u32[]{:S(2)}, u32[]{:S(2)}) collective-permute-start(bf16[2048,128]{1,0:T(8,128)(2,1)S(1)} %bitcast.12), channel_id=1, source_target_pairs={{0,96},{32,0},{64,32},{96,64},{1,97},{33,1},{65,33},{97,65},{2,98}... | collective-permute-start | bytes 1572872 | tf_op jit(solution)/shard_map/ppermute | solution.py:191
  30.4 11.5 %collective-permute-done.2.rest_4_ = bf16[2048,128]{1,0:T(8,128)(2,1)S(1)} collective-permute-done((bf16[2048,128]{1,0:T(8,128)(2,1)S(1)}, bf16[2048,128]{1,0:T(8,128)(2,1)S(1)}, u32[]{:S(2)}, u32[]{:S(2)}) %collective-permute-start.2) | collective-permute-done | bytes 524320 | tf_op jit(solution)/shard_map/ppermute | solution.py:191
  42.1 3.3 %collective-permute-start.1 = (bf16[1024,128]{1,0:T(8,128)(2,1)S(1)}, bf16[1024,128]{1,0:T(8,128)(2,1)S(1)}, u32[]{:S(2)}, u32[]{:S(2)}) collective-permute-start(bf16[1024,128]{1,0:T(8,128)(2,1)S(1)} %slice.36), channel_id=1, source_target_pairs={{0,96},{32,0},{64,32},{96,64},{1,97},{33,1},{65,33},{97,65},{2,98}... | collective-permute-start | bytes 786440 | tf_op jit(solution)/shard_map/ppermute | solution.py:191
  45.9 14.3 %all-gather = f32[64,256]{1,0:T(8,128)S(1)} all-gather(f32[16,256]{1,0:T(8,128)S(1)} %bitcast.21), channel_id=2, replica_groups=mesh['z'=4,'x'=4,'c'=2,'y'=4] {'x'}, dimensions={0}, use_global_device_ids=true | all-gather | bytes 81920 | tf_op jit(solution)/shard_map/all_gather | solution.py:229
  61.3 0.9 convert_add_fusion.2
  63.1 26.9 %tiles.1 = (bf16[16,256,128]{2,1,0:T(8,128)(2,1)}, bf16[2048,128]{1,0:T(8,128)(2,1)S(1)}, bf16[2048,128]{1,0:T(8,128)(2,1)S(1)}, bf16[1024,128]{1,0:T(8,128)(2,1...) custom-call(s32[2]{0:T(128)S(1)} %pad_add_fusion.where_ref, ...), custom_call_target="tpu_custom_call" | custom-call | tf_op jit(solution)/shard_map/tiles/pallas_call | solution.py:245
  91.8 1.0 collective-permute-done.15
  92.8 2.3 %collective-permute-start.16 = (bf16[1024,128]{1,0:T(8,128)(2,1)S(1)}, bf16[1024,128]{1,0:T(8,128)(2,1)S(1)}, u32[]{:S(2)}, u32[]{:S(2)}) collective-permute-start(bf16[1024,128]{1,0:T(8,128)(2,1)S(1)} %add_convert_fusion.1), channel_id=1, source_target_pairs={{0,96},{32,0},{64,32},{96,64},{1,97},{33,1},{65,33},{97,65},{2,98}... | collective-permute-start | bytes 786440 | tf_op jit(solution)/shard_map/ppermute | solution.py:191
  95.3 6.0 %collective-permute-done.12 = bf16[1024,128]{1,0:T(8,128)(2,1)S(1)} collective-permute-done((bf16[1024,128]{1,0:T(8,128)(2,1)S(1)}, bf16[1024,128]{1,0:T(8,128)(2,1)S(1)}, u32[]{:S(2)}, u32[]{:S(2)}) %collective-permute-start.12) | collective-permute-done | bytes 262176 | tf_op jit(solution)/shard_map/ppermute | solution.py:191
  103.3 3.2 %collective-permute-start.17 = (bf16[2048,128]{1,0:T(8,128)(2,1)}, bf16[2048,128]{1,0:T(8,128)(2,1)S(1)}, u32[]{:S(2)}, u32[]{:S(2)}) collective-permute-start(bf16[2048,128]{1,0:T(8,128)(2,1)} %pad_maximum_fusion.1), channel_id=1, source_target_pairs={{0,96},{32,0},{64,32},{96,64},{1,97},{33,1},{65,33},{97,65},{2,98}... | collective-permute-start | bytes 1572872 | tf_op jit(solution)/shard_map/ppermute | solution.py:191
  106.5 5.3 %all-to-all-start.2 = ((bf16[16,256,128]{2,1,0:T(8,128)(2,1)}), bf16[16,256,128]{2,1,0:T(8,128)(2,1)S(1)}, u32[]{:S(2)}, u32[]{:S(2)}) async-start(bf16[16,256,128]{2,1,0:T(8,128)(2,1)} %get-tuple-element.16), calls=%async_computation.2 | async-start | bytes 2097152 | tf_op jit(solution)/shard_map/all_to_all | solution.py:199
  111.8 5.1 %collective-permute-done.13 = bf16[2048,128]{1,0:T(8,128)(2,1)} collective-permute-done((bf16[2048,128]{1,0:T(8,128)(2,1)}, bf16[2048,128]{1,0:T(8,128)(2,1)}, u32[]{:S(2)}, u32[]{:S(2)}) %collective-permute-start.13) | collective-permute-done | bytes 524320 | tf_op jit(solution)/shard_map/ppermute | solution.py:191
  117.2 2.1 %add_convert_fusion = bf16[2048,128]{1,0:T(8,128)(2,1)} fusion(bf16[2048,128]{1,0:T(8,128)(2,1)S(1)} %collective-permute-done.17, bf16[2048,128]{1,0:T(8,128)(2,1)} %collective-permute-done.13, bf16[2048,128]{1,0:T(8,128)(2,1)S(1)} %collective-permute-done.9, bf16[2048,128]{1,0:T(8,128)(2,1)S(1)} %get-tuple-element.17), kind=kLoop, calls=%fused_computation | loop fusion | flops 2097152 | bytes 2621440 | tf_op jit(solution)/shard_map/convert_element_type | solution.py:286
  119.3 8.6 %all-to-all-done.2 = bf16[16,256,128]{2,1,0:T(8,128)(2,1)S(1)} async-done(((bf16[16,256,128]{2,1,0:T(8,128)(2,1)}), bf16[16,256,128]{2,1,0:T(8,128)(2,1)S(1)}, u32[]{:S(2)}, u32[]{:S(2)}) %all-to-all-start.2) | async-done | bytes 1048608 | tf_op jit(solution)/shard_map/all_to_all | solution.py:199
  127.9 3.9 %all-to-all-start.3 = ((bf16[32,64,128]{2,1,0:T(8,128)(2,1)}), bf16[32,64,128]{2,1,0:T(8,128)(2,1)S(1)}, u32[]{:S(2)}, u32[]{:S(2)}) async-start(bf16[32,64,128]{2,1,0:T(8,128)(2,1)} %bitcast.9), calls=%async_computation.3 | async-start | bytes 1048576 | tf_op jit(solution)/shard_map/all_to_all | solution.py:199
  131.8 3.4 %unpack_q.1 = bf16[64,8192]{1,0:T(8,128)(2,1)} custom-call(bf16[4,4,256,128]{3,2,1,0:T(8,128)(2,1)} %bitcast.16), custom_call_target="tpu_custom_call" | custom-call | tf_op jit(solution)/shard_map/unpack_q/pallas_call | solution.py:265
  135.3 8.3 %all-to-all-done.3 = bf16[32,64,128]{2,1,0:T(8,128)(2,1)S(1)} async-done(((bf16[32,64,128]{2,1,0:T(8,128)(2,1)}), bf16[32,64,128]{2,1,0:T(8,128)(2,1)S(1)}, u32[]{:S(2)}, u32[]{:S(2)}) %all-to-all-start.3) | async-done | bytes 524320 | tf_op jit(solution)/shard_map/all_to_all | solution.py:199
  144.4 1.8 %unpack_kv.1 = (bf16[64,1024]{1,0:T(8,128)(2,1)}, bf16[64,1024]{1,0:T(8,128)(2,1)}) custom-call(bf16[4,2,4,64,128]{4,3,2,1,0:T(8,128)(2,1)} %bitcast.17), custom_call_target="tpu_custom_call" | custom-call | tf_op jit(solution)/shard_map/unpack_kv/pallas_call | solution.py:288
  (64 shorter events, 7.6 us)
Async XLA Ops:
  2.5 19.2 %all-to-all-start.1 = ((bf16[32,64,128]{2,1,0:T(8,128)(2,1)}), bf16[32,64,128]{2,1,0:T(8,128)(2,1)S(1)}, u32[]{:S(2)}, u32[]{:S(2)}) async-start(bf16[32,64,128]{2,1,0:T(8,128)(2,1)} %bitcast.18), calls=%async_computation.1 | async-start | bytes 1048576 | tf_op jit(solution)/shard_map/all_to_all | solution.py:199
  21.7 39.3 %copy-start.7 = (s32[32,2]{0,1:T(2,128)S(1)}, s32[32,2]{0,1:T(2,128)}, u32[]{:S(2)}) copy-start(s32[32,2]{0,1:T(2,128)} %param.16) | copy-start | bytes 772
  21.7 41.5 %copy-start = (s32[12]{0:T(128)S(1)}, s32[12]{0:T(128)}, u32[]{:S(2)}) copy-start(s32[12]{0:T(128)} %bounds_ref.1) | copy-start | bytes 148
  21.7 39.7 %all-to-all-start = ((bf16[16,528,128]{2,1,0:T(8,128)(2,1)}), bf16[16,528,128]{2,1,0:T(8,128)(2,1)}, u32[]{:S(2)}, u32[]{:S(2)}) async-start(bf16[16,528,128]{2,1,0:T(8,128)(2,1)} %bitcast.15), calls=%async_computation | async-start | bytes 4325376 | tf_op jit(solution)/shard_map/all_to_all | solution.py:199
  26.2 15.7 %collective-permute-start.2 = (bf16[2048,128]{1,0:T(8,128)(2,1)S(1)}, bf16[2048,128]{1,0:T(8,128)(2,1)S(1)}, u32[]{:S(2)}, u32[]{:S(2)}) collective-permute-start(bf16[2048,128]{1,0:T(8,128)(2,1)S(1)} %bitcast.11), channel_id=1, source_target_pairs={{0,32},{32,64},{64,96},{96,0},{1,33},{33,65},{65,97},{97,1},{2,34}... | collective-permute-start | bytes 1572872 | tf_op jit(solution)/shard_map/ppermute | solution.py:191
  28.2 13.8 %collective-permute-start = (bf16[2048,128]{1,0:T(8,128)(2,1)S(1)}, bf16[2048,128]{1,0:T(8,128)(2,1)S(1)}, u32[]{:S(2)}, u32[]{:S(2)}) collective-permute-start(bf16[2048,128]{1,0:T(8,128)(2,1)S(1)} %bitcast.12), channel_id=1, source_target_pairs={{0,96},{32,0},{64,32},{96,64},{1,97},{33,1},{65,33},{97,65},{2,98}... | collective-permute-start | bytes 1572872 | tf_op jit(solution)/shard_map/ppermute | solution.py:191
  42.0 18.3 %collective-permute-start.3 = (bf16[1024,128]{1,0:T(8,128)(2,1)S(1)}, bf16[1024,128]{1,0:T(8,128)(2,1)S(1)}, u32[]{:S(2)}, u32[]{:S(2)}) collective-permute-start(bf16[1024,128]{1,0:T(8,128)(2,1)S(1)} %slice.37), channel_id=1, source_target_pairs={{0,32},{32,64},{64,96},{96,0},{1,33},{33,65},{65,97},{97,1},{2,34}... | collective-permute-start | bytes 786440 | tf_op jit(solution)/shard_map/ppermute | solution.py:191
  42.1 18.2 %collective-permute-start.1 = (bf16[1024,128]{1,0:T(8,128)(2,1)S(1)}, bf16[1024,128]{1,0:T(8,128)(2,1)S(1)}, u32[]{:S(2)}, u32[]{:S(2)}) collective-permute-start(bf16[1024,128]{1,0:T(8,128)(2,1)S(1)} %slice.36), channel_id=1, source_target_pairs={{0,96},{32,0},{64,32},{96,64},{1,97},{33,1},{65,33},{97,65},{2,98}... | collective-permute-start | bytes 786440 | tf_op jit(solution)/shard_map/ppermute | solution.py:191
  45.4 16.9 %collective-permute-start.4 = (bf16[2048,128]{1,0:T(8,128)(2,1)S(1)}, bf16[2048,128]{1,0:T(8,128)(2,1)S(1)}, u32[]{:S(2)}, u32[]{:S(2)}) collective-permute-start(bf16[2048,128]{1,0:T(8,128)(2,1)S(1)} %bitcast.13), channel_id=1, source_target_pairs={{0,4},{4,0},{1,5},{5,1},{2,6},{6,2},{3,7},{7,3},{8,12},{12,8},{9,1... | collective-permute-start | bytes 1572872 | tf_op jit(solution)/shard_map/ppermute | solution.py:195
  45.4 17.0 %collective-permute-start.8 = (bf16[2048,128]{1,0:T(8,128)(2,1)S(1)}, bf16[2048,128]{1,0:T(8,128)(2,1)}, u32[]{:S(2)}, u32[]{:S(2)}) collective-permute-start(bf16[2048,128]{1,0:T(8,128)(2,1)S(1)} %collective-permute-done.2.rest_4_), channel_id=1, source_target_pairs={{0,4},{4,0},{1,5},{5,1},{2,6},{6,2},{3,7},{7,3},{8,12},{12,8},{9,1... | collective-permute-start | bytes 1572872 | tf_op jit(solution)/shard_map/ppermute | solution.py:195
  45.9 17.2 %collective-permute-start.5 = (bf16[2048,128]{1,0:T(8,128)(2,1)S(1)}, bf16[2048,128]{1,0:T(8,128)(2,1)}, u32[]{:S(2)}, u32[]{:S(2)}) collective-permute-start(bf16[2048,128]{1,0:T(8,128)(2,1)S(1)} %collective-permute-done.rest_1_), channel_id=1, source_target_pairs={{0,4},{4,0},{1,5},{5,1},{2,6},{6,2},{3,7},{7,3},{8,12},{12,8},{9,1... | collective-permute-start | bytes 1572872 | tf_op jit(solution)/shard_map/ppermute | solution.py:195
  60.2 2.1 %collective-permute-start.7 = (bf16[1024,128]{1,0:T(8,128)(2,1)S(1)}, bf16[1024,128]{1,0:T(8,128)(2,1)S(1)}, u32[]{:S(2)}, u32[]{:S(2)}) collective-permute-start(bf16[1024,128]{1,0:T(8,128)(2,1)S(1)} %collective-permute-done.3.rest_3_), channel_id=1, source_target_pairs={{0,4},{4,0},{1,5},{5,1},{2,6},{6,2},{3,7},{7,3},{8,12},{12,8},{9,1... | collective-permute-start | bytes 786440 | tf_op jit(solution)/shard_map/ppermute | solution.py:195
  60.3 2.0 %collective-permute-start.6 = (bf16[1024,128]{1,0:T(8,128)(2,1)S(1)}, bf16[1024,128]{1,0:T(8,128)(2,1)S(1)}, u32[]{:S(2)}, u32[]{:S(2)}) collective-permute-start(bf16[1024,128]{1,0:T(8,128)(2,1)S(1)} %collective-permute-done.1.rest_2_), channel_id=1, source_target_pairs={{0,4},{4,0},{1,5},{5,1},{2,6},{6,2},{3,7},{7,3},{8,12},{12,8},{9,1... | collective-permute-start | bytes 786440 | tf_op jit(solution)/shard_map/ppermute | solution.py:195
  90.0 1.6 %collective-permute-start.11 = (bf16[1024,128]{1,0:T(8,128)(2,1)S(1)}, bf16[1024,128]{1,0:T(8,128)(2,1)S(1)}, u32[]{:S(2)}, u32[]{:S(2)}) collective-permute-start(bf16[1024,128]{1,0:T(8,128)(2,1)S(1)} %get-tuple-element.22), channel_id=1, source_target_pairs={{0,4},{4,0},{1,5},{5,1},{2,6},{6,2},{3,7},{7,3},{8,12},{12,8},{9,1... | collective-permute-start | bytes 786440 | tf_op jit(solution)/shard_map/ppermute | solution.py:195
  90.2 5.0 %collective-permute-start.10 = (bf16[2048,128]{1,0:T(8,128)(2,1)S(1)}, bf16[2048,128]{1,0:T(8,128)(2,1)S(1)}, u32[]{:S(2)}, u32[]{:S(2)}) collective-permute-start(bf16[2048,128]{1,0:T(8,128)(2,1)S(1)} %get-tuple-element.20), channel_id=1, source_target_pairs={{0,4},{4,0},{1,5},{5,1},{2,6},{6,2},{3,7},{7,3},{8,12},{12,8},{9,1... | collective-permute-start | bytes 1572872 | tf_op jit(solution)/shard_map/ppermute | solution.py:195
  90.6 2.1 %collective-permute-start.15 = (bf16[1024,128]{1,0:T(8,128)(2,1)S(1)}, bf16[1024,128]{1,0:T(8,128)(2,1)S(1)}, u32[]{:S(2)}, u32[]{:S(2)}) collective-permute-start(bf16[1024,128]{1,0:T(8,128)(2,1)S(1)} %get-tuple-element.26), channel_id=1, source_target_pairs={{0,4},{4,0},{1,5},{5,1},{2,6},{6,2},{3,7},{7,3},{8,12},{12,8},{9,1... | collective-permute-start | bytes 786440 | tf_op jit(solution)/shard_map/ppermute | solution.py:195
  90.7 21.1 %collective-permute-start.9 = (bf16[2048,128]{1,0:T(8,128)(2,1)S(1)}, bf16[2048,128]{1,0:T(8,128)(2,1)S(1)}, u32[]{:S(2)}, u32[]{:S(2)}) collective-permute-start(bf16[2048,128]{1,0:T(8,128)(2,1)S(1)} %get-tuple-element.18), channel_id=1, source_target_pairs={{0,4},{4,0},{1,5},{5,1},{2,6},{6,2},{3,7},{7,3},{8,12},{12,8},{9,1... | collective-permute-start | bytes 1572872 | tf_op jit(solution)/shard_map/ppermute | solution.py:195
  91.1 11.1 %collective-permute-start.14 = (bf16[2048,128]{1,0:T(8,128)(2,1)S(1)}, bf16[2048,128]{1,0:T(8,128)(2,1)S(1)}, u32[]{:S(2)}, u32[]{:S(2)}) collective-permute-start(bf16[2048,128]{1,0:T(8,128)(2,1)S(1)} %get-tuple-element.24), channel_id=1, source_target_pairs={{0,4},{4,0},{1,5},{5,1},{2,6},{6,2},{3,7},{7,3},{8,12},{12,8},{9,1... | collective-permute-start | bytes 1572872 | tf_op jit(solution)/shard_map/ppermute | solution.py:195
  91.7 9.6 %collective-permute-start.12 = (bf16[1024,128]{1,0:T(8,128)(2,1)S(1)}, bf16[1024,128]{1,0:T(8,128)(2,1)S(1)}, u32[]{:S(2)}, u32[]{:S(2)}) collective-permute-start(bf16[1024,128]{1,0:T(8,128)(2,1)S(1)} %add_convert_fusion.2), channel_id=1, source_target_pairs={{0,32},{32,64},{64,96},{96,0},{1,33},{33,65},{65,97},{97,1},{2,34}... | collective-permute-start | bytes 786440 | tf_op jit(solution)/shard_map/ppermute | solution.py:191
  92.8 9.6 %collective-permute-start.16 = (bf16[1024,128]{1,0:T(8,128)(2,1)S(1)}, bf16[1024,128]{1,0:T(8,128)(2,1)S(1)}, u32[]{:S(2)}, u32[]{:S(2)}) collective-permute-start(bf16[1024,128]{1,0:T(8,128)(2,1)S(1)} %add_convert_fusion.1), channel_id=1, source_target_pairs={{0,96},{32,0},{64,32},{96,64},{1,97},{33,1},{65,33},{97,65},{2,98}... | collective-permute-start | bytes 786440 | tf_op jit(solution)/shard_map/ppermute | solution.py:191
  102.2 14.7 %collective-permute-start.13 = (bf16[2048,128]{1,0:T(8,128)(2,1)}, bf16[2048,128]{1,0:T(8,128)(2,1)}, u32[]{:S(2)}, u32[]{:S(2)}) collective-permute-start(bf16[2048,128]{1,0:T(8,128)(2,1)} %pad_maximum_fusion), channel_id=1, source_target_pairs={{0,32},{32,64},{64,96},{96,0},{1,33},{33,65},{65,97},{97,1},{2,34}... | collective-permute-start | bytes 1572872 | tf_op jit(solution)/shard_map/ppermute | solution.py:191
  103.3 13.9 %collective-permute-start.17 = (bf16[2048,128]{1,0:T(8,128)(2,1)}, bf16[2048,128]{1,0:T(8,128)(2,1)S(1)}, u32[]{:S(2)}, u32[]{:S(2)}) collective-permute-start(bf16[2048,128]{1,0:T(8,128)(2,1)} %pad_maximum_fusion.1), channel_id=1, source_target_pairs={{0,96},{32,0},{64,32},{96,64},{1,97},{33,1},{65,33},{97,65},{2,98}... | collective-permute-start | bytes 1572872 | tf_op jit(solution)/shard_map/ppermute | solution.py:191
  106.5 21.4 %all-to-all-start.2 = ((bf16[16,256,128]{2,1,0:T(8,128)(2,1)}), bf16[16,256,128]{2,1,0:T(8,128)(2,1)S(1)}, u32[]{:S(2)}, u32[]{:S(2)}) async-start(bf16[16,256,128]{2,1,0:T(8,128)(2,1)} %get-tuple-element.16), calls=%async_computation.2 | async-start | bytes 2097152 | tf_op jit(solution)/shard_map/all_to_all | solution.py:199
  127.9 15.7 %all-to-all-start.3 = ((bf16[32,64,128]{2,1,0:T(8,128)(2,1)}), bf16[32,64,128]{2,1,0:T(8,128)(2,1)S(1)}, u32[]{:S(2)}, u32[]{:S(2)}) async-start(bf16[32,64,128]{2,1,0:T(8,128)(2,1)} %bitcast.9), calls=%async_computation.3 | async-start | bytes 1048576 | tf_op jit(solution)/shard_map/all_to_all | solution.py:199
  (6 other events, 71.2 us)

commit v2 on v1

v2 whole, which is shorter than its diff:
```python
import jax
import jax.numpy as jnp
from jax import lax
from jax.experimental import pallas as pl
from jax.experimental.pallas import tpu as pltpu
from jax.sharding import Mesh, PartitionSpec as P

HEAD_DIM = 128
SPAN = 128
HALF = 64
LANES = 512
PACKED = 528
ROWS = ("z", "x", "c", "y")
MIB = 1024 * 1024


def dot(a, b, ca, cb):
    return lax.dot_general(a, b, (((ca,), (cb,)), ((), ())), preferred_element_type=jnp.float32)


def pack_kv_kernel(keys_ref, values_ref, out_ref):
    for z in range(4):
        for y in range(4):
            cols = slice((2 * y + z // 2) * HEAD_DIM, (2 * y + z // 2 + 1) * HEAD_DIM)
            out_ref[z, y, 0] = keys_ref[:, cols]
            out_ref[z, y, 1] = values_ref[:, cols]


def pack_q_kernel(queries_ref, grad_ref, fwd_ref, out_ref):
    row = lax.broadcasted_iota(jnp.int32, (16, HEAD_DIM), 0)
    for z in range(4):
        delta = jnp.zeros((16, HEAD_DIM), jnp.float32)
        for pair in range(2):
            products = []
            for h in (2 * pair, 2 * pair + 1):
                cols = slice((z * 4 + h) * HEAD_DIM, (z * 4 + h + 1) * HEAD_DIM)
                grad = grad_ref[:, cols]
                out_ref[z, 0, h * HALF : (h + 1) * HALF] = queries_ref[:, cols]
                out_ref[z, 0, 256 + h * HALF : 256 + (h + 1) * HALF] = grad
                products.append(grad.astype(jnp.float32) * fwd_ref[:, cols].astype(jnp.float32))
            product = jnp.concatenate(products, axis=0)
            high = product.astype(jnp.bfloat16)
            low = (product - high.astype(jnp.float32)).astype(jnp.bfloat16)
            pick = ((row == pair) | (row == pair + 2)).astype(jnp.bfloat16)
            delta = delta + dot(pick, high, 1, 1) + dot(pick, low, 1, 1)
        high = delta.astype(jnp.bfloat16).astype(jnp.float32)
        out_ref[z, 0, 512:PACKED] = jnp.where(row < 2, high, delta - high).astype(jnp.bfloat16)


def unpack_q_kernel(in_ref, out_ref):
    for z in range(4):
        for h in range(4):
            cols = slice((z * 4 + h) * HEAD_DIM, (z * 4 + h + 1) * HEAD_DIM)
            out_ref[:, cols] = in_ref[z, 0, h * HALF : (h + 1) * HALF]


def unpack_kv_kernel(in_ref, keys_ref, values_ref):
    for g in range(8):
        cols = slice(g * HEAD_DIM, (g + 1) * HEAD_DIM)
        y, z = g // 2, 2 * (g % 2)
        for i, out_ref in ((0, keys_ref), (1, values_ref)):
            total = in_ref[z, y, i].astype(jnp.float32) + in_ref[z + 1, y, i].astype(jnp.float32)
            out_ref[:, cols] = total.astype(jnp.bfloat16)


PIECES = ((0, 0, 16), (1, 0, 16), (2, 0, 8), (2, 8, 8), (3, 0, 16))
GROUP = 2
MOST = 72


def tiles_kernel(where_ref, plan_ref, bounds_ref, packed_ref, lse_ref, *rest):
    mine, other, dq_ref, keep, send, rest = rest[:5], rest[5:10], rest[10], rest[11:16], rest[16:21], rest[21:]
    kv_ref, dkv_ref, dq_sum, slot_ref, step_ref, base_ref, chunk_ref, lanes_ref, sums_ref, *buffers, sems = rest
    z, x, c = where_ref[0], where_ref[1], where_ref[2]
    factor = HEAD_DIM ** (-0.5)

    copies = []
    for i, (slab, chunk, chunks) in enumerate(PIECES):
        for core, sources in enumerate((mine, other)):
            rows = pl.ds(slab * 32 + core * 16 + chunk, chunks)
            copies.append(pltpu.make_async_copy(sources[i], kv_ref.at[rows], sems.at[2 * i + core]))
    for copy in copies:
        copy.start()

    def note_slot(slot, carry):
        slot_ref[plan_ref[slot]] = slot
        return carry

    lax.fori_loop(0, 64, note_slot, 0)
    dkv_ref[...] = jnp.zeros_like(dkv_ref)
    dq_sum[...] = jnp.zeros_like(dq_sum)
    for buffer in buffers[2:]:
        buffer[...] = jnp.zeros_like(buffer)

    lane = lax.broadcasted_iota(jnp.int32, (1, LANES), 1)
    within = (lane // 256) * HALF + lane % HALF
    row = lax.broadcasted_iota(jnp.int32, (SPAN, LANES), 0)

    steps = jnp.int32(0)
    for s in range(8):
        span = plan_ref[(s // 2) * 16 + x * 4 + c * 2 + s % 2]
        last = span * SPAN + within
        first = jnp.zeros_like(last)
        first_doc = jnp.int32(0)
        for i in range(1, 12):
            bound = bounds_ref[i]
            first = jnp.where(bound <= last, jnp.maximum(first, bound), first)
            first_doc = jnp.where(bound <= span * SPAN, jnp.maximum(first_doc, bound), first_doc)
        lanes_ref[s, 0:1] = first
        lanes_ref[s, 1:2] = last
        parts = [packed_ref[2 * s + i, 512:PACKED].astype(jnp.float32) for i in range(2)]
        sums_ref[s, 0:1] = lse_ref[pl.ds(((s // 2 - z) & 3) * 2 + s % 2, 1), :]
        sums_ref[s, 1:2] = jnp.concatenate(
            [part[h : h + 1] + part[h + 2 : h + 3] for part in parts for h in range(2)], axis=1
        )

        def note_span(i, carry, s=s, begin=lax.shift_right_logical(first_doc, 7), span=span, steps=steps):
            key_span = jnp.minimum(begin + i, span)
            slot = slot_ref[key_span]
            slab = (lax.shift_right_logical(slot, 2) - x) & 3
            core = (lax.shift_right_logical(slot, 1) & 1) ^ c
            step_ref[steps + lax.shift_right_logical(i, 1)] = s
            base_ref[2 * steps + i] = jnp.where(begin + i <= span, key_span * SPAN, 8192)
            chunk_ref[2 * steps + i] = (
                slab * 32 + core * 16 + lax.shift_right_logical(slot, 4) * 4 + (slot & 1) * 2
            )
            return carry

        pairs = lax.shift_right_logical(span - lax.shift_right_logical(first_doc, 7) + 2, 1)
        lax.fori_loop(0, 2 * pairs, note_span, 0)
        steps = steps + pairs
    for i in range(2):
        step_ref[steps + i] = 7
    for i in range(4):
        base_ref[2 * steps + i] = 8192
        chunk_ref[2 * steps + i] = 0
    for copy in copies:
        copy.wait()

    def operand(s, start):
        return jnp.concatenate([packed_ref[2 * s + i, start : start + 256] for i in range(2)], axis=0)

    def tile(step, i):
        chunks = [chunk_ref[2 * step + j] for j in range(GROUP)]
        return jnp.concatenate([kv_ref[pl.ds(r, 2), i].reshape(SPAN, HEAD_DIM) for r in chunks], axis=0)

    def scores_stage(step, probs_ref, dscore_ref):
        s = step_ref[step]
        first, last = lanes_ref[s, 0:1], lanes_ref[s, 1:2]
        lse, delta = sums_ref[s, 0:1], sums_ref[s, 1:2]
        masks = []
        for j in range(GROUP):
            base = base_ref[2 * step + j]
            masks.append((row >= first - base) & (row <= last - base))
        allowed = jnp.concatenate(masks, axis=0)
        scores = dot(tile(step, 0), operand(s, 0), 1, 1)
        probs = jnp.where(allowed, jnp.exp(scores * factor - lse), 0.0)
        dprob = dot(tile(step, 1), operand(s, 256), 1, 1)
        probs_ref[...] = probs.astype(jnp.bfloat16)
        dscore_ref[...] = (probs * (dprob - delta)).astype(jnp.bfloat16)

    def sums_stage(step, probs_ref, dscore_ref):
        s = step_ref[step]
        probs, dscore = probs_ref[...], dscore_ref[...]
        part_v = dot(probs, operand(s, 256), 1, 0)
        part_k = dot(dscore, operand(s, 0), 1, 0)
        dq_sum[s] += dot(tile(step, 0), dscore, 0, 0)
        for i, part in ((0, part_k), (1, part_v)):
            part = part.reshape(2 * GROUP, HALF, HEAD_DIM)
            for j in range(GROUP):
                dkv_ref[pl.ds(chunk_ref[2 * step + j], 2), i] += part[2 * j : 2 * j + 2]

    def two_steps(i, carry):
        step = 2 * i
        scores_stage(step, buffers[0], buffers[1])
        sums_stage(jnp.maximum(step - 1, 0), buffers[2], buffers[3])
        scores_stage(step + 1, buffers[2], buffers[3])
        sums_stage(step, buffers[0], buffers[1])
        return carry

    loops = lax.shift_right_logical(steps + 1, 1)
    lax.fori_loop(0, loops, two_steps, 0)
    sums_stage(jnp.maximum(2 * loops - 1, 0), buffers[2], buffers[3])

    for i in range(16):
        rows = slice((i % 2) * 256, (i % 2) * 256 + 256)
        dq_ref[i] = jnp.transpose(dq_sum[i // 2, :, rows] * factor).astype(jnp.bfloat16)
    for i, (slab, chunk, chunks) in enumerate(PIECES):
        for core, outs in enumerate((keep, send)):
            start = slab * 32 + core * 16 + chunk
            for j in range(0, chunks, 4):
                rows = slice(start + j, start + j + 4)
                outs[i][j : j + 4, 0] = (dkv_ref[rows, 0] * factor).astype(jnp.bfloat16)
                outs[i][j : j + 4, 1] = dkv_ref[rows, 1].astype(jnp.bfloat16)


def tiles(where, plan, bounds, packed, lse, mine, other):
    bf16, f32 = jnp.bfloat16, jnp.float32
    vmem = pl.BlockSpec(memory_space=pltpu.VMEM)
    smem = pl.BlockSpec(memory_space=pltpu.SMEM)
    anywhere = pl.BlockSpec(memory_space=pl.ANY)
    parts = [jax.ShapeDtypeStruct((chunks, 2, HALF, HEAD_DIM), bf16) for _, _, chunks in PIECES]
    outs = pl.pallas_call(
        tiles_kernel,
        out_shape=[jax.ShapeDtypeStruct((16, 256, HEAD_DIM), bf16)] + parts + parts,
        in_specs=[smem, smem, smem, vmem, vmem] + [anywhere] * 10,
        out_specs=[vmem] * 11,
        scratch_shapes=[
            pltpu.VMEM((128, 2, HALF, HEAD_DIM), bf16),
            pltpu.VMEM((128, 2, HALF, HEAD_DIM), f32),
            pltpu.VMEM((8, HEAD_DIM, LANES), f32),
            pltpu.SMEM((64,), jnp.int32),
            pltpu.SMEM((MOST,), jnp.int32),
            pltpu.SMEM((2 * MOST,), jnp.int32),
            pltpu.SMEM((2 * MOST,), jnp.int32),
            pltpu.VMEM((8, 2, LANES), jnp.int32),
            pltpu.VMEM((8, 2, LANES), f32),
        ]
        + [pltpu.VMEM((GROUP * SPAN, LANES), bf16)] * 4
        + [pltpu.SemaphoreType.DMA((10,))],
        compiler_params=pltpu.CompilerParams(vmem_limit_bytes=26 * MIB),
        name="tiles",
    )(where, plan, bounds, packed, lse, *mine, *other)
    return outs[0], outs[1:6], outs[6:11]


def shift(array, axis, by):
    return lax.ppermute(array, axis, [(i, (i + by) % 4) for i in range(4)])


def swap(array):
    return lax.ppermute(array, "c", [(0, 1), (1, 0)])


def exchange(array):
    return lax.all_to_all(array, ("z", "y"), 0, 0, tiled=True)


def shards(queries, keys, values, fwd_out, out_grad, log_norm, doc_bounds, span_plan, read_lists):
    bf16 = jnp.bfloat16
    f32 = jnp.float32
    vmem = pl.BlockSpec(memory_space=pltpu.VMEM)
    z, x = lax.axis_index("z"), lax.axis_index("x")
    c = lax.axis_index("c")

    kv_out = pl.pallas_call(
        pack_kv_kernel,
        out_shape=jax.ShapeDtypeStruct((4, 4, 2, HALF, HEAD_DIM), bf16),
        in_specs=[vmem, vmem],
        out_specs=vmem,
        name="pack_kv",
    )(keys, values)
    block = exchange(kv_out.reshape(16, 2, HALF, HEAD_DIM))

    wide = pl.BlockSpec((HALF, 16 * HEAD_DIM), lambda y: (0, y))
    q_out = pl.pallas_call(
        pack_q_kernel,
        grid=(4,),
        out_shape=jax.ShapeDtypeStruct((4, 4, PACKED, HEAD_DIM), bf16),
        in_specs=[wide, wide, wide],
        out_specs=pl.BlockSpec((4, 1, PACKED, HEAD_DIM), lambda y: (0, y, 0, 0)),
        name="pack_q",
    )(queries, out_grad, fwd_out)
    norms = log_norm.reshape(2, 2, HALF, 4, 4).transpose(3, 0, 1, 4, 2).reshape(4, 2, LANES)
    to = [lax.dynamic_index_in_dim(norms, (z + k) % 4, 0, keepdims=False) for k in range(4)]
    lse = jnp.concatenate(
        [to[0], shift(to[3], "z", -1), shift(to[2], "z", 2), shift(to[1], "z", 1)], axis=0
    )
    q_out, lse = lax.optimization_barrier((q_out, lse))
    packed = exchange(q_out.reshape(16, PACKED, HEAD_DIM))

    from_next = shift(block, "x", -1)
    from_last = shift(block, "x", 1)
    far_a = shift(from_next[:8], "x", -1)
    far_b = shift(from_last[8:], "x", 1)

    where = jnp.stack([z, x, c]).astype(jnp.int32)
    mine = [block, from_next, far_a, far_b, from_last]
    other = [swap(part) for part in mine]
    dq, keep, send = tiles(where, span_plan.reshape(-1), doc_bounds, packed, lse, mine, other)

    got = [swap(part) for part in send]
    sums = [a.astype(f32) + b.astype(f32) for a, b in zip(keep, got)]
    via_next = shift(sums[2].astype(bf16), "x", 1).astype(f32)
    via_last = shift(sums[3].astype(bf16), "x", -1).astype(f32)
    to_next = jnp.concatenate([sums[1][:8] + via_next, sums[1][8:]], axis=0).astype(bf16)
    to_last = jnp.concatenate([sums[4][:8], sums[4][8:] + via_last], axis=0).astype(bf16)
    dq, sums[1], sums[4] = lax.optimization_barrier((dq, sums[1], sums[4]))
    dq_back = exchange(dq).reshape(4, 4, 256, HEAD_DIM)
    grad_queries = pl.pallas_call(
        unpack_q_kernel,
        grid=(4,),
        out_shape=jax.ShapeDtypeStruct((HALF, 64 * HEAD_DIM), bf16),
        in_specs=[pl.BlockSpec((4, 1, 256, HEAD_DIM), lambda y: (0, y, 0, 0))],
        out_specs=wide,
        compiler_params=pltpu.CompilerParams(vmem_limit_bytes=6 * MIB),
        name="unpack_q",
    )(dq_back)

    near = shift(to_next, "x", 1).astype(f32) + shift(to_last, "x", -1).astype(f32)
    kv_back = exchange((sums[0] + near).astype(bf16))
    grad_keys, grad_values = pl.pallas_call(
        unpack_kv_kernel,
        out_shape=[jax.ShapeDtypeStruct((HALF, 8 * HEAD_DIM), bf16)] * 2,
        in_specs=[vmem],
        out_specs=[vmem, vmem],
        compiler_params=pltpu.CompilerParams(vmem_limit_bytes=4 * MIB),
        name="unpack_kv",
    )(kv_back.reshape(4, 4, 2, HALF, HEAD_DIM))
    return (grad_queries, grad_keys, grad_values)


def solution(mesh):
    fine = Mesh(mesh.devices.reshape(4, 4, 2, 4), ROWS)
    rows = P(ROWS, None)
    cp = ("z", "x", "c")
    in_specs = (rows, rows, rows, rows, rows, P(cp, "y"), P(), P(), P(cp, None, None))
    return jax.shard_map(shards, mesh=fine, in_specs=in_specs, out_specs=(rows, rows, rows), check_vma=False)
```

time: 148 us -> 126 us (0.85)
  blocking collectives: 14.3 us -> 0 us
  Pallas kernels: 38.8 us -> 25.4 us
  starting transfers between devices: 36.6 us -> 44 us
    all_gather x1 -> x0, blocking collectives: 14.3 us -> none  [shards(): all_lse = lax.all_gather(log_norm.T, 'x', axis=0, tiled=False)]
    pallas_call x2, Pallas kernels: 28.7 us -> 18.1 us  [the longest x1 16.3 us: tiles(): pl.pallas_call(tiles_kernel, out_shape=[jax.ShapeDtypeStruct((16, 256, HE...]
    all_to_all x4, waiting for transfers between devices: 23.8 us -> 15.2 us  [exchange(): return lax.all_to_all(array, ('z', 'y'), 0, 0, tiled=True)]
    ppermute x8 -> x11, waiting for transfers between devices: 23 us -> 29.6 us  [shift(): return lax.ppermute(array, axis, [(i, (i + by) % 4) for i in range(4)])]
    ppermute x8 -> x11, starting transfers between devices: 13.2 us -> 19.4 us  [shift(): return lax.ppermute(array, axis, [(i, (i + by) % 4) for i in range(4)])]
    pallas_call x1, Pallas kernels: 3.43 us -> 1.67 us  [shards(): pl.pallas_call(unpack_q_kernel, grid=(4,), out_shape=jax.ShapeDtypeStruct...]
    all_to_all x4, starting transfers between devices: 21.1 us -> 22.9 us  [exchange(): return lax.all_to_all(array, ('z', 'y'), 0, 0, tiled=True)]
    unnamed x17 -> x11, local copies, waits for them, and re-layouts: 1.66 us -> 0.11 us
  transfers between devices with their start and end apart: 22 -> 25, of which waited for: 9 -> 12; matrix products, arithmetic and copies ran while one was open for 4% -> 6% of each run, Pallas kernels for 6% -> 5%
where the time goes in v2:
time: 126 us; the launch traced here: 124 us
  waiting for transfers between devices  46.9 us (37%)
  starting transfers between devices  44 us (35%)
  Pallas kernels  25.4 us (20%)
  other arithmetic  4.74 us (4%)
  local copies, waits for them, and re-layouts  2.21 us (2%)
    ppermute x11, waiting for transfers between devices, shift(): return lax.ppermute(array, axis, [(i, (i + by) % 4) for i in range(4)])  29.6 us
    all_to_all x4, starting transfers between devices, exchange(): return lax.all_to_all(array, ('z', 'y'), 0, 0, tiled=True)  22.9 us
    ppermute x11, starting transfers between devices, shift(): return lax.ppermute(array, axis, [(i, (i + by) % 4) for i in range(4)])  19.4 us
    pallas_call x1, Pallas kernels, tiles(): pl.pallas_call(tiles_kernel, out_shape=[jax.ShapeDtypeStruct((16, 256, HE...  16.3 us
    all_to_all x4, waiting for transfers between devices, exchange(): return lax.all_to_all(array, ('z', 'y'), 0, 0, tiled=True)  15.2 us
    pallas_call x1, Pallas kernels, shards(): pl.pallas_call(pack_q_kernel, grid=(4,), out_shape=jax.ShapeDtypeStruct((...  4.79 us
  transfers between devices with their start and end apart: 25, of which 12 were waited for; matrix products, arithmetic and copies ran while one was open for 6% of the time, Pallas kernels for 5%

profile of v2, /device:TPU:0, one launch (start us, length us, event | category | flops | bytes accessed | tf_op | source)
XLA Modules:
  0.0 124.2 jit_solution(1841629946965914232)
XLA Ops:
  0.6 1.8 %pack_kv.1 = bf16[4,4,2,64,128]{4,3,2,1,0:T(8,128)(2,1)} custom-call(bf16[64,1024]{1,0:T(8,128)(2,1)} %keys_ref.1, bf16[64,1024]{1,0:T(8,128)(2,1)} %values_ref.1), custom_call_target="tpu_custom_call" | custom-call | tf_op jit(solution)/shard_map/pack_kv/pallas_call | solution.py:246
  2.5 8.1 %all-to-all-start.1 = ((bf16[16,2,64,128]{3,2,1,0:T(8,128)(2,1)}), bf16[16,2,64,128]{3,2,1,0:T(8,128)(2,1)S(1)}, u32[]{:S(2)}, u32[]{:S(2)}) async-start(bf16[16,2,64,128]{3,2,1,0:T(8,128)(2,1)} %bitcast.21), calls=%async_computation.1 | async-start | bytes 1048576 | tf_op jit(solution)/shard_map/all_to_all | solution.py:236
  11.6 1.9 %collective-permute-start.2 = (f32[2,512]{1,0:T(2,128)S(1)}, f32[2,512]{1,0:T(2,128)S(1)}, u32[]{:S(2)}, u32[]{:S(2)}) collective-permute-start(f32[2,512]{1,0:T(2,128)S(1)} %get-tuple-element.36), channel_id=1, source_target_pairs={{0,32},{32,64},{64,96},{96,0},{1,33},{33,65},{65,97},{97,1},{2,34}... | collective-permute-start | bytes 12296 | tf_op jit(solution)/shard_map/ppermute | solution.py:228
  13.6 2.7 %collective-permute-start.1 = (f32[2,512]{1,0:T(2,128)S(1)}, f32[2,512]{1,0:T(2,128)S(1)}, u32[]{:S(2)}, u32[]{:S(2)}) collective-permute-start(f32[2,512]{1,0:T(2,128)S(1)} %get-tuple-element.37), channel_id=1, source_target_pairs={{0,64},{32,96},{64,0},{96,32},{1,65},{33,97},{65,1},{97,33},{2,66}... | collective-permute-start | bytes 12296 | tf_op jit(solution)/shard_map/ppermute | solution.py:228
  17.7 4.8 %pack_q.1 = bf16[4,4,528,128]{3,2,1,0:T(8,128)(2,1)} custom-call(bf16[64,8192]{1,0:T(8,128)(2,1)} %queries_ref.1, bf16[64,8192]{1,0:T(8,128)(2,1)} %grad_ref.1, bf16[64,8192]{1,0:T(8,128)(2,1)} %fwd_ref.1), custom_call_target="tpu_custom_call" | custom-call | tf_op jit(solution)/shard_map/pack_q/pallas_call | solution.py:256
  22.6 4.4 %all-to-all-start = ((bf16[16,528,128]{2,1,0:T(8,128)(2,1)}), bf16[16,528,128]{2,1,0:T(8,128)(2,1)S(1)}, u32[]{:S(2)}, u32[]{:S(2)}) async-start(bf16[16,528,128]{2,1,0:T(8,128)(2,1)} %bitcast.20), calls=%async_computation | async-start | bytes 4325376 | tf_op jit(solution)/shard_map/all_to_all | solution.py:236
  26.9 1.6 %collective-permute-start.5 = (bf16[16,2,64,128]{3,2,1,0:T(8,128)(2,1)S(1)}, bf16[16,2,64,128]{3,2,1,0:T(8,128)(2,1)S(1)}, u32[]{:S(2)}, u32[]{:S(2)}) collective-permute-start(bf16[16,2,64,128]{3,2,1,0:T(8,128)(2,1)S(1)} %all-to-all-done.1.rest_0_), channel_id=1, source_target_pairs={{0,8},{8,16},{16,24},{24,0},{1,9},{9,17},{17,25},{25,1},{2,10},{10... | collective-permute-start | bytes 1572872 | tf_op jit(solution)/shard_map/ppermute | solution.py:228
  28.5 1.7 %collective-permute-start.3 = (bf16[16,2,64,128]{3,2,1,0:T(8,128)(2,1)S(1)}, bf16[16,2,64,128]{3,2,1,0:T(8,128)(2,1)}, u32[]{:S(2)}, u32[]{:S(2)}) collective-permute-start(bf16[16,2,64,128]{3,2,1,0:T(8,128)(2,1)S(1)} %all-to-all-done.1.rest_0_), channel_id=1, source_target_pairs={{0,24},{8,0},{16,8},{24,16},{1,25},{9,1},{17,9},{25,17},{2,26},{10... | collective-permute-start | bytes 1572872 | tf_op jit(solution)/shard_map/ppermute | solution.py:228
  30.2 10.0 %collective-permute-done.5.rest_4_ = bf16[16,2,64,128]{3,2,1,0:T(8,128)(2,1)S(1)} collective-permute-done((bf16[16,2,64,128]{3,2,1,0:T(8,128)(2,1)S(1)}, bf16[16,2,64,128]{3,2,1,0:T(8,128)(2,1)S(1)}, u32[]{:S(2)}, u32[]{:S(2)}) %collective-permute-start.5) | collective-permute-done | bytes 524320 | tf_op jit(solution)/shard_map/ppermute | solution.py:228
  41.5 3.0 %collective-permute-start.4 = (bf16[8,2,64,128]{3,2,1,0:T(8,128)(2,1)S(1)}, bf16[8,2,64,128]{3,2,1,0:T(8,128)(2,1)}, u32[]{:S(2)}, u32[]{:S(2)}) collective-permute-start(bf16[8,2,64,128]{3,2,1,0:T(8,128)(2,1)S(1)} %slice.26), channel_id=1, source_target_pairs={{0,24},{8,0},{16,8},{24,16},{1,25},{9,1},{17,9},{25,17},{2,26},{10... | collective-permute-start | bytes 786440 | tf_op jit(solution)/shard_map/ppermute | solution.py:228
  45.1 2.8 %collective-permute-done.6.rest_3_ = bf16[8,2,64,128]{3,2,1,0:T(8,128)(2,1)S(1)} collective-permute-done((bf16[8,2,64,128]{3,2,1,0:T(8,128)(2,1)S(1)}, bf16[8,2,64,128]{3,2,1,0:T(8,128)(2,1)S(1)}, u32[]{:S(2)}, u32[]{:S(2)}) %collective-permute-start.6) | collective-permute-done | bytes 262176 | tf_op jit(solution)/shard_map/ppermute | solution.py:228
  50.3 6.5 %all-to-all-done.packed_ref = bf16[16,528,128]{2,1,0:T(8,128)(2,1)S(1)} async-done(((bf16[16,528,128]{2,1,0:T(8,128)(2,1)}), bf16[16,528,128]{2,1,0:T(8,128)(2,1)S(1)}, u32[]{:S(2)}, u32[]{:S(2)}) %all-to-all-start) | async-done | bytes 2162720 | tf_op jit(solution)/shard_map/all_to_all | solution.py:236
  56.8 16.3 %tiles.1 = (bf16[16,256,128]{2,1,0:T(8,128)(2,1)S(1)}, bf16[16,2,64,128]{3,2,1,0:T(8,128)(2,1)S(1)}, bf16[16,2,64,128]{3,2,1,0:T(8,128)(2,1)S(1)}, bf16[8,2,64,1...) custom-call(s32[3]{0:T(128)S(1)} %pad_add_fusion.where_ref, ...), custom_call_target="tpu_custom_call" | custom-call | tf_op jit(solution)/shard_map/tiles/pallas_call | solution.py:203
  74.8 1.5 %collective-permute-start.16 = (bf16[8,2,64,128]{3,2,1,0:T(8,128)(2,1)S(1)}, bf16[8,2,64,128]{3,2,1,0:T(8,128)(2,1)S(1)}, u32[]{:S(2)}, u32[]{:S(2)}) collective-permute-start(bf16[8,2,64,128]{3,2,1,0:T(8,128)(2,1)S(1)} %add_convert_fusion.2), channel_id=1, source_target_pairs={{0,8},{8,16},{16,24},{24,0},{1,9},{9,17},{17,25},{25,1},{2,10},{10... | collective-permute-start | bytes 786440 | tf_op jit(solution)/shard_map/ppermute | solution.py:228
  76.4 1.9 %collective-permute-start.19 = (bf16[8,2,64,128]{3,2,1,0:T(8,128)(2,1)S(1)}, bf16[8,2,64,128]{3,2,1,0:T(8,128)(2,1)}, u32[]{:S(2)}, u32[]{:S(2)}) collective-permute-start(bf16[8,2,64,128]{3,2,1,0:T(8,128)(2,1)S(1)} %add_convert_fusion.1), channel_id=1, source_target_pairs={{0,24},{8,0},{16,8},{24,16},{1,25},{9,1},{17,9},{25,17},{2,26},{10... | collective-permute-start | bytes 786440 | tf_op jit(solution)/shard_map/ppermute | solution.py:228
  78.5 5.9 %collective-permute-done.16 = bf16[8,2,64,128]{3,2,1,0:T(8,128)(2,1)S(1)} collective-permute-done((bf16[8,2,64,128]{3,2,1,0:T(8,128)(2,1)S(1)}, bf16[8,2,64,128]{3,2,1,0:T(8,128)(2,1)S(1)}, u32[]{:S(2)}, u32[]{:S(2)}) %collective-permute-start.16) | collective-permute-done | bytes 262176 | tf_op jit(solution)/shard_map/ppermute | solution.py:228
  85.8 3.8 %all-to-all-start.2 = ((bf16[16,256,128]{2,1,0:T(8,128)(2,1)}), bf16[16,256,128]{2,1,0:T(8,128)(2,1)S(1)}, u32[]{:S(2)}, u32[]{:S(2)}) async-start(bf16[16,256,128]{2,1,0:T(8,128)(2,1)} %copy-done), calls=%async_computation.2 | async-start | bytes 2097152 | tf_op jit(solution)/shard_map/all_to_all | solution.py:236
  90.8 3.1 %collective-permute-start.20 = (bf16[16,2,64,128]{3,2,1,0:T(8,128)(2,1)S(1)}, bf16[16,2,64,128]{3,2,1,0:T(8,128)(2,1)S(1)}, u32[]{:S(2)}, u32[]{:S(2)}) collective-permute-start(bf16[16,2,64,128]{3,2,1,0:T(8,128)(2,1)S(1)} %pad_maximum_fusion.1), channel_id=1, source_target_pairs={{0,24},{8,0},{16,8},{24,16},{1,25},{9,1},{17,9},{25,17},{2,26},{10... | collective-permute-start | bytes 1572872 | tf_op jit(solution)/shard_map/ppermute | solution.py:228
  93.8 6.2 %collective-permute-done.17 = bf16[16,2,64,128]{3,2,1,0:T(8,128)(2,1)} collective-permute-done((bf16[16,2,64,128]{3,2,1,0:T(8,128)(2,1)}, bf16[16,2,64,128]{3,2,1,0:T(8,128)(2,1)}, u32[]{:S(2)}, u32[]{:S(2)}) %collective-permute-start.17) | collective-permute-done | bytes 524320 | tf_op jit(solution)/shard_map/ppermute | solution.py:228
  100.0 4.2 %collective-permute-done.20 = bf16[16,2,64,128]{3,2,1,0:T(8,128)(2,1)S(1)} collective-permute-done((bf16[16,2,64,128]{3,2,1,0:T(8,128)(2,1)S(1)}, bf16[16,2,64,128]{3,2,1,0:T(8,128)(2,1)S(1)}, u32[]{:S(2)}, u32[]{:S(2)}) %collective-permute-start.20) | collective-permute-done | bytes 524320 | tf_op jit(solution)/shard_map/ppermute | solution.py:228
  104.2 2.2 %add_convert_fusion = bf16[16,2,64,128]{3,2,1,0:T(8,128)(2,1)} fusion(bf16[16,2,64,128]{3,2,1,0:T(8,128)(2,1)S(1)} %collective-permute-done.20, bf16[16,2,64,128]{3,2,1,0:T(8,128)(2,1)} %collective-permute-done.17, bf16[16,2,64,128]{3,2,1,0:T(8,128)(2,1)S(1)} %collective-permute-done.14, bf16[16,2,64,128]{3,2,1,0:T(8,128)(2,1)S(1)} %copy-done.2), kind=kLoop, calls=%fused_computation | loop fusion | flops 2097152 | bytes 2621440 | tf_op jit(solution)/shard_map/convert_element_type | solution.py:301
  106.7 6.6 %all-to-all-start.3 = ((bf16[16,2,64,128]{3,2,1,0:T(8,128)(2,1)}), bf16[16,2,64,128]{3,2,1,0:T(8,128)(2,1)S(1)}, u32[]{:S(2)}, u32[]{:S(2)}) async-start(bf16[16,2,64,128]{3,2,1,0:T(8,128)(2,1)} %add_convert_fusion), calls=%async_computation.3 | async-start | bytes 1048576 | tf_op jit(solution)/shard_map/all_to_all | solution.py:236
  113.3 1.7 %unpack_q.1 = bf16[64,8192]{1,0:T(8,128)(2,1)} custom-call(bf16[4,4,256,128]{3,2,1,0:T(8,128)(2,1)S(1)} %bitcast.18), custom_call_target="tpu_custom_call" | custom-call | tf_op jit(solution)/shard_map/unpack_q/pallas_call | solution.py:290
  114.9 8.5 %all-to-all-done.3 = bf16[16,2,64,128]{3,2,1,0:T(8,128)(2,1)S(1)} async-done(((bf16[16,2,64,128]{3,2,1,0:T(8,128)(2,1)}), bf16[16,2,64,128]{3,2,1,0:T(8,128)(2,1)S(1)}, u32[]{:S(2)}, u32[]{:S(2)}) %all-to-all-start.3) | async-done | bytes 524320 | tf_op jit(solution)/shard_map/all_to_all | solution.py:236
  (62 shorter events, 12.2 us)
Async XLA Ops:
  2.5 20.1 %all-to-all-start.1 = ((bf16[16,2,64,128]{3,2,1,0:T(8,128)(2,1)}), bf16[16,2,64,128]{3,2,1,0:T(8,128)(2,1)S(1)}, u32[]{:S(2)}, u32[]{:S(2)}) async-start(bf16[16,2,64,128]{3,2,1,0:T(8,128)(2,1)} %bitcast.21), calls=%async_computation.1 | async-start | bytes 1048576 | tf_op jit(solution)/shard_map/all_to_all | solution.py:236
  11.6 10.9 %collective-permute-start.2 = (f32[2,512]{1,0:T(2,128)S(1)}, f32[2,512]{1,0:T(2,128)S(1)}, u32[]{:S(2)}, u32[]{:S(2)}) collective-permute-start(f32[2,512]{1,0:T(2,128)S(1)} %get-tuple-element.36), channel_id=1, source_target_pairs={{0,32},{32,64},{64,96},{96,0},{1,33},{33,65},{65,97},{97,1},{2,34}... | collective-permute-start | bytes 12296 | tf_op jit(solution)/shard_map/ppermute | solution.py:228
  13.6 8.9 %collective-permute-start.1 = (f32[2,512]{1,0:T(2,128)S(1)}, f32[2,512]{1,0:T(2,128)S(1)}, u32[]{:S(2)}, u32[]{:S(2)}) collective-permute-start(f32[2,512]{1,0:T(2,128)S(1)} %get-tuple-element.37), channel_id=1, source_target_pairs={{0,64},{32,96},{64,0},{96,32},{1,65},{33,97},{65,1},{97,33},{2,66}... | collective-permute-start | bytes 12296 | tf_op jit(solution)/shard_map/ppermute | solution.py:228
  16.2 6.3 %collective-permute-start = (f32[2,512]{1,0:T(2,128)S(1)}, f32[2,512]{1,0:T(2,128)S(1)}, u32[]{:S(2)}, u32[]{:S(2)}) collective-permute-start(f32[2,512]{1,0:T(2,128)S(1)} %get-tuple-element.38), channel_id=1, source_target_pairs={{0,96},{32,0},{64,32},{96,64},{1,97},{33,1},{65,33},{97,65},{2,98}... | collective-permute-start | bytes 12296 | tf_op jit(solution)/shard_map/ppermute | solution.py:228
  22.6 34.2 %all-to-all-start = ((bf16[16,528,128]{2,1,0:T(8,128)(2,1)}), bf16[16,528,128]{2,1,0:T(8,128)(2,1)S(1)}, u32[]{:S(2)}, u32[]{:S(2)}) async-start(bf16[16,528,128]{2,1,0:T(8,128)(2,1)} %bitcast.20), calls=%async_computation | async-start | bytes 4325376 | tf_op jit(solution)/shard_map/all_to_all | solution.py:236
  26.9 13.3 %collective-permute-start.5 = (bf16[16,2,64,128]{3,2,1,0:T(8,128)(2,1)S(1)}, bf16[16,2,64,128]{3,2,1,0:T(8,128)(2,1)S(1)}, u32[]{:S(2)}, u32[]{:S(2)}) collective-permute-start(bf16[16,2,64,128]{3,2,1,0:T(8,128)(2,1)S(1)} %all-to-all-done.1.rest_0_), channel_id=1, source_target_pairs={{0,8},{8,16},{16,24},{24,0},{1,9},{9,17},{17,25},{25,1},{2,10},{10... | collective-permute-start | bytes 1572872 | tf_op jit(solution)/shard_map/ppermute | solution.py:228
  28.5 12.1 %collective-permute-start.3 = (bf16[16,2,64,128]{3,2,1,0:T(8,128)(2,1)S(1)}, bf16[16,2,64,128]{3,2,1,0:T(8,128)(2,1)}, u32[]{:S(2)}, u32[]{:S(2)}) collective-permute-start(bf16[16,2,64,128]{3,2,1,0:T(8,128)(2,1)S(1)} %all-to-all-done.1.rest_0_), channel_id=1, source_target_pairs={{0,24},{8,0},{16,8},{24,16},{1,25},{9,1},{17,9},{25,17},{2,26},{10... | collective-permute-start | bytes 1572872 | tf_op jit(solution)/shard_map/ppermute | solution.py:228
  30.2 18.5 %collective-permute-start.7 = (bf16[16,2,64,128]{3,2,1,0:T(8,128)(2,1)S(1)}, bf16[16,2,64,128]{3,2,1,0:T(8,128)(2,1)}, u32[]{:S(2)}, u32[]{:S(2)}) collective-permute-start(bf16[16,2,64,128]{3,2,1,0:T(8,128)(2,1)S(1)} %all-to-all-done.1.rest_0_), channel_id=1, source_target_pairs={{0,4},{4,0},{1,5},{5,1},{2,6},{6,2},{3,7},{7,3},{8,12},{12,8},{9,1... | collective-permute-start | bytes 1572872 | tf_op jit(solution)/shard_map/ppermute | solution.py:232
  40.2 7.7 %collective-permute-start.6 = (bf16[8,2,64,128]{3,2,1,0:T(8,128)(2,1)S(1)}, bf16[8,2,64,128]{3,2,1,0:T(8,128)(2,1)S(1)}, u32[]{:S(2)}, u32[]{:S(2)}) collective-permute-start(bf16[8,2,64,128]{3,2,1,0:T(8,128)(2,1)S(1)} %slice.27), channel_id=1, source_target_pairs={{0,8},{8,16},{16,24},{24,0},{1,9},{9,17},{17,25},{25,1},{2,10},{10... | collective-permute-start | bytes 786440 | tf_op jit(solution)/shard_map/ppermute | solution.py:228
  41.5 6.9 %collective-permute-start.4 = (bf16[8,2,64,128]{3,2,1,0:T(8,128)(2,1)S(1)}, bf16[8,2,64,128]{3,2,1,0:T(8,128)(2,1)}, u32[]{:S(2)}, u32[]{:S(2)}) collective-permute-start(bf16[8,2,64,128]{3,2,1,0:T(8,128)(2,1)S(1)} %slice.26), channel_id=1, source_target_pairs={{0,24},{8,0},{16,8},{24,16},{1,25},{9,1},{17,9},{25,17},{2,26},{10... | collective-permute-start | bytes 786440 | tf_op jit(solution)/shard_map/ppermute | solution.py:228
  44.6 5.0 %collective-permute-start.11 = (bf16[16,2,64,128]{3,2,1,0:T(8,128)(2,1)S(1)}, bf16[16,2,64,128]{3,2,1,0:T(8,128)(2,1)}, u32[]{:S(2)}, u32[]{:S(2)}) collective-permute-start(bf16[16,2,64,128]{3,2,1,0:T(8,128)(2,1)S(1)} %collective-permute-done.5.rest_4_), channel_id=1, source_target_pairs={{0,4},{4,0},{1,5},{5,1},{2,6},{6,2},{3,7},{7,3},{8,12},{12,8},{9,1... | collective-permute-start | bytes 1572872 | tf_op jit(solution)/shard_map/ppermute | solution.py:232
  44.6 5.8 %collective-permute-start.8 = (bf16[16,2,64,128]{3,2,1,0:T(8,128)(2,1)}, bf16[16,2,64,128]{3,2,1,0:T(8,128)(2,1)}, u32[]{:S(2)}, u32[]{:S(2)}) collective-permute-start(bf16[16,2,64,128]{3,2,1,0:T(8,128)(2,1)} %collective-permute-done.3.rest_1_), channel_id=1, source_target_pairs={{0,4},{4,0},{1,5},{5,1},{2,6},{6,2},{3,7},{7,3},{8,12},{12,8},{9,1... | collective-permute-start | bytes 1572872 | tf_op jit(solution)/shard_map/ppermute | solution.py:232
  47.9 1.7 %collective-permute-start.10 = (bf16[8,2,64,128]{3,2,1,0:T(8,128)(2,1)S(1)}, bf16[8,2,64,128]{3,2,1,0:T(8,128)(2,1)}, u32[]{:S(2)}, u32[]{:S(2)}) collective-permute-start(bf16[8,2,64,128]{3,2,1,0:T(8,128)(2,1)S(1)} %collective-permute-done.6.rest_3_), channel_id=1, source_target_pairs={{0,4},{4,0},{1,5},{5,1},{2,6},{6,2},{3,7},{7,3},{8,12},{12,8},{9,1... | collective-permute-start | bytes 786440 | tf_op jit(solution)/shard_map/ppermute | solution.py:232
  48.5 1.9 %collective-permute-start.9 = (bf16[8,2,64,128]{3,2,1,0:T(8,128)(2,1)}, bf16[8,2,64,128]{3,2,1,0:T(8,128)(2,1)}, u32[]{:S(2)}, u32[]{:S(2)}) collective-permute-start(bf16[8,2,64,128]{3,2,1,0:T(8,128)(2,1)} %collective-permute-done.4.rest_2_), channel_id=1, source_target_pairs={{0,4},{4,0},{1,5},{5,1},{2,6},{6,2},{3,7},{7,3},{8,12},{12,8},{9,1... | collective-permute-start | bytes 786440 | tf_op jit(solution)/shard_map/ppermute | solution.py:232
  73.2 5.1 %collective-permute-start.12 = (bf16[16,2,64,128]{3,2,1,0:T(8,128)(2,1)S(1)}, bf16[16,2,64,128]{3,2,1,0:T(8,128)(2,1)S(1)}, u32[]{:S(2)}, u32[]{:S(2)}) collective-permute-start(bf16[16,2,64,128]{3,2,1,0:T(8,128)(2,1)S(1)} %get-tuple-element.23), channel_id=1, source_target_pairs={{0,4},{4,0},{1,5},{5,1},{2,6},{6,2},{3,7},{7,3},{8,12},{12,8},{9,1... | collective-permute-start | bytes 1572872 | tf_op jit(solution)/shard_map/ppermute | solution.py:232
  73.7 2.6 %collective-permute-start.18 = (bf16[8,2,64,128]{3,2,1,0:T(8,128)(2,1)S(1)}, bf16[8,2,64,128]{3,2,1,0:T(8,128)(2,1)S(1)}, u32[]{:S(2)}, u32[]{:S(2)}) collective-permute-start(bf16[8,2,64,128]{3,2,1,0:T(8,128)(2,1)S(1)} %get-tuple-element.32), channel_id=1, source_target_pairs={{0,4},{4,0},{1,5},{5,1},{2,6},{6,2},{3,7},{7,3},{8,12},{12,8},{9,1... | collective-permute-start | bytes 786440 | tf_op jit(solution)/shard_map/ppermute | solution.py:232
  73.8 11.8 %collective-permute-start.13 = (bf16[16,2,64,128]{3,2,1,0:T(8,128)(2,1)S(1)}, bf16[16,2,64,128]{3,2,1,0:T(8,128)(2,1)S(1)}, u32[]{:S(2)}, u32[]{:S(2)}) collective-permute-start(bf16[16,2,64,128]{3,2,1,0:T(8,128)(2,1)S(1)} %get-tuple-element.25), channel_id=1, source_target_pairs={{0,4},{4,0},{1,5},{5,1},{2,6},{6,2},{3,7},{7,3},{8,12},{12,8},{9,1... | collective-permute-start | bytes 1572872 | tf_op jit(solution)/shard_map/ppermute | solution.py:232
  74.2 19.6 %collective-permute-start.14 = (bf16[16,2,64,128]{3,2,1,0:T(8,128)(2,1)}, bf16[16,2,64,128]{3,2,1,0:T(8,128)(2,1)S(1)}, u32[]{:S(2)}, u32[]{:S(2)}) collective-permute-start(bf16[16,2,64,128]{3,2,1,0:T(8,128)(2,1)} %get-tuple-element.28), channel_id=1, source_target_pairs={{0,4},{4,0},{1,5},{5,1},{2,6},{6,2},{3,7},{7,3},{8,12},{12,8},{9,1... | collective-permute-start | bytes 1572872 | tf_op jit(solution)/shard_map/ppermute | solution.py:232
  74.8 9.6 %collective-permute-start.16 = (bf16[8,2,64,128]{3,2,1,0:T(8,128)(2,1)S(1)}, bf16[8,2,64,128]{3,2,1,0:T(8,128)(2,1)S(1)}, u32[]{:S(2)}, u32[]{:S(2)}) collective-permute-start(bf16[8,2,64,128]{3,2,1,0:T(8,128)(2,1)S(1)} %add_convert_fusion.2), channel_id=1, source_target_pairs={{0,8},{8,16},{16,24},{24,0},{1,9},{9,17},{17,25},{25,1},{2,10},{10... | collective-permute-start | bytes 786440 | tf_op jit(solution)/shard_map/ppermute | solution.py:228
  76.4 13.2 %collective-permute-start.19 = (bf16[8,2,64,128]{3,2,1,0:T(8,128)(2,1)S(1)}, bf16[8,2,64,128]{3,2,1,0:T(8,128)(2,1)}, u32[]{:S(2)}, u32[]{:S(2)}) collective-permute-start(bf16[8,2,64,128]{3,2,1,0:T(8,128)(2,1)S(1)} %add_convert_fusion.1), channel_id=1, source_target_pairs={{0,24},{8,0},{16,8},{24,16},{1,25},{9,1},{17,9},{25,17},{2,26},{10... | collective-permute-start | bytes 786440 | tf_op jit(solution)/shard_map/ppermute | solution.py:228
  85.4 14.7 %collective-permute-start.17 = (bf16[16,2,64,128]{3,2,1,0:T(8,128)(2,1)}, bf16[16,2,64,128]{3,2,1,0:T(8,128)(2,1)}, u32[]{:S(2)}, u32[]{:S(2)}) collective-permute-start(bf16[16,2,64,128]{3,2,1,0:T(8,128)(2,1)} %pad_maximum_fusion), channel_id=1, source_target_pairs={{0,8},{8,16},{16,24},{24,0},{1,9},{9,17},{17,25},{25,1},{2,10},{10... | collective-permute-start | bytes 1572872 | tf_op jit(solution)/shard_map/ppermute | solution.py:228
  85.8 20.9 %all-to-all-start.2 = ((bf16[16,256,128]{2,1,0:T(8,128)(2,1)}), bf16[16,256,128]{2,1,0:T(8,128)(2,1)S(1)}, u32[]{:S(2)}, u32[]{:S(2)}) async-start(bf16[16,256,128]{2,1,0:T(8,128)(2,1)} %copy-done), calls=%async_computation.2 | async-start | bytes 2097152 | tf_op jit(solution)/shard_map/all_to_all | solution.py:236
  90.8 13.4 %collective-permute-start.20 = (bf16[16,2,64,128]{3,2,1,0:T(8,128)(2,1)S(1)}, bf16[16,2,64,128]{3,2,1,0:T(8,128)(2,1)S(1)}, u32[]{:S(2)}, u32[]{:S(2)}) collective-permute-start(bf16[16,2,64,128]{3,2,1,0:T(8,128)(2,1)S(1)} %pad_maximum_fusion.1), channel_id=1, source_target_pairs={{0,24},{8,0},{16,8},{24,16},{1,25},{9,1},{17,9},{25,17},{2,26},{10... | collective-permute-start | bytes 1572872 | tf_op jit(solution)/shard_map/ppermute | solution.py:228
  106.7 16.7 %all-to-all-start.3 = ((bf16[16,2,64,128]{3,2,1,0:T(8,128)(2,1)}), bf16[16,2,64,128]{3,2,1,0:T(8,128)(2,1)S(1)}, u32[]{:S(2)}, u32[]{:S(2)}) async-start(bf16[16,2,64,128]{3,2,1,0:T(8,128)(2,1)} %add_convert_fusion), calls=%async_computation.3 | async-start | bytes 1048576 | tf_op jit(solution)/shard_map/all_to_all | solution.py:236
  (6 other events, 103.0 us)

commit v3 on v2

v3 whole, which is shorter than its diff:
```python
import functools

import jax
import jax.numpy as jnp
from jax import lax
from jax.experimental import pallas as pl
from jax.experimental.pallas import tpu as pltpu
from jax.sharding import Mesh, PartitionSpec as P

HEAD_DIM = 128
SPAN = 128
HALF = 64
LANES = 512
PACKED = 272
ROWS = ("z", "x", "c", "y")
MIB = 1024 * 1024


def dot(a, b, ca, cb):
    return lax.dot_general(a, b, (((ca,), (cb,)), ((), ())), preferred_element_type=jnp.float32)


def pack_kv_kernel(keys_ref, values_ref, out_ref):
    for z in range(4):
        for y in range(4):
            cols = slice((2 * y + z // 2) * HEAD_DIM, (2 * y + z // 2 + 1) * HEAD_DIM)
            out_ref[z, y, 0] = keys_ref[:, cols]
            out_ref[z, y, 1] = values_ref[:, cols]


def pack_q_kernel(queries_ref, grad_ref, fwd_ref, out_ref):
    row = lax.broadcasted_iota(jnp.int32, (16, HEAD_DIM), 0)
    pick = (row < 2).astype(jnp.bfloat16)
    for z in range(4):
        for pair in range(2):
            cols = [slice((z * 4 + 2 * pair + i) * HEAD_DIM, (z * 4 + 2 * pair + i + 1) * HEAD_DIM) for i in range(2)]
            lanes = slice(pair * HEAD_DIM, (pair + 1) * HEAD_DIM)
            query = jnp.concatenate([queries_ref[:, col] for col in cols], axis=0)
            grad = jnp.concatenate([grad_ref[:, col] for col in cols], axis=0)
            fwd = jnp.concatenate([fwd_ref[:, col] for col in cols], axis=0)
            out_ref[z, 0, 0:HEAD_DIM, lanes] = jnp.transpose(query)
            out_ref[z, 0, HEAD_DIM : 2 * HEAD_DIM, lanes] = jnp.transpose(grad)
            product = grad.astype(jnp.float32) * fwd.astype(jnp.float32)
            high = product.astype(jnp.bfloat16)
            low = (product - high.astype(jnp.float32)).astype(jnp.bfloat16)
            delta = dot(pick, high, 1, 1) + dot(pick, low, 1, 1)
            high = delta.astype(jnp.bfloat16).astype(jnp.float32)
            out_ref[z, 0, 2 * HEAD_DIM : PACKED, lanes] = jnp.where(row < 1, high, delta - high).astype(jnp.bfloat16)


def unpack_q_kernel(in_ref, out_ref):
    for z in range(4):
        for pair in range(2):
            part = jnp.transpose(in_ref[z, 0, :, pair * HEAD_DIM : (pair + 1) * HEAD_DIM])
            for i in range(2):
                head = z * 4 + 2 * pair + i
                out_ref[:, head * HEAD_DIM : (head + 1) * HEAD_DIM] = part[i * HALF : (i + 1) * HALF]


def add_kernel(terms, *refs):
    count = len(refs) // (terms + 1)
    for i in range(count):
        for t in range(4):
            total = refs[i * terms][t].astype(jnp.float32)
            for k in range(1, terms):
                total = total + refs[i * terms + k][t].astype(jnp.float32)
            refs[count * terms + i][t] = total.astype(jnp.bfloat16)


def final_kernel(keep_ref, got_ref, last_a_ref, last_b_ref, next_a_ref, next_b_ref, out_ref):
    for t in range(8):
        last_ref, next_ref = ((last_a_ref, next_a_ref), (last_b_ref, next_b_ref))[t // 4]
        for i in range(2):
            total = keep_ref[t, i].astype(jnp.float32) + got_ref[t, i].astype(jnp.float32)
            total = total + last_ref[t % 4, i].astype(jnp.float32) + next_ref[t % 4, i].astype(jnp.float32)
            rows = jnp.transpose(total).astype(jnp.bfloat16)
            out_ref[2 * t, i] = rows[:HALF]
            out_ref[2 * t + 1, i] = rows[HALF:]


def unpack_kv_kernel(in_ref, keys_ref, values_ref):
    for g in range(8):
        cols = slice(g * HEAD_DIM, (g + 1) * HEAD_DIM)
        y, z = g // 2, 2 * (g % 2)
        for i, out_ref in ((0, keys_ref), (1, values_ref)):
            total = in_ref[z, y, i].astype(jnp.float32) + in_ref[z + 1, y, i].astype(jnp.float32)
            out_ref[:, cols] = total.astype(jnp.bfloat16)


PIECES = ((0, 0, 8), (1, 0, 8), (2, 0, 4), (2, 4, 4), (3, 0, 8))
GROUP = 2
QUERY, BEGIN, TABLE = 64, 72, 80


def tiles_kernel(plan_in, bounds_in, packed_ref, lse_ref, *rest):
    mine, other, dq_ref, keep, send, rest = rest[:5], rest[5:10], rest[10], rest[11:15], rest[15:19], rest[19:]
    plan_ref, bounds_ref, table_ref, kv_ref, dkv_ref, dq_sum, dq_out, keep_out, lanes_ref, sums_ref, *buffers, sems = rest
    z, x, c = lax.axis_index("z"), lax.axis_index("x"), lax.axis_index("c")
    factor = HEAD_DIM ** (-0.5)

    small = [
        pltpu.make_async_copy(plan_in, plan_ref, sems.at[10]),
        pltpu.make_async_copy(bounds_in, bounds_ref, sems.at[11]),
    ]
    for copy in small:
        copy.start()
    copies = []
    for i, (slab, tile, count) in enumerate(PIECES):
        for core, sources in enumerate((mine, other)):
            rows = pl.ds(slab * 16 + core * 8 + tile, count)
            copies.append(pltpu.make_async_copy(sources[i], kv_ref.at[rows], sems.at[2 * i + core]))
    for copy in copies:
        copy.start()

    dkv_ref[...] = jnp.zeros_like(dkv_ref)
    dq_sum[...] = jnp.zeros_like(dq_sum)
    for buffer in buffers[2:]:
        buffer[...] = jnp.zeros_like(buffer)
    for copy in small:
        copy.wait()
    slabs = [((i - x) & 3) * 16 for i in range(4)]
    cores = [c * 8, (1 - c) * 8]
    for slot in range(64):
        place = slabs[slot // 4 % 4] + cores[slot // 2 % 2] + slot // 16 * 2 + slot % 2
        table_ref[plan_ref[slot // 2, slot % 2]] = place
    row = lax.broadcasted_iota(jnp.int32, (SPAN, LANES), 0)
    lane = lax.broadcasted_iota(jnp.int32, (1, LANES), 1)
    within = (lane // 256) * HALF + lane % HALF
    bounds = [bounds_ref[i] for i in range(1, 12)]
    steps = jnp.int32(0)
    for s in range(8):
        span = plan_ref[(s // 2) * 8 + x * 2 + c, s % 2]
        last = span * SPAN + within
        first = jnp.zeros_like(last)
        first_doc = jnp.int32(0)
        for bound in bounds:
            first = jnp.where(bound <= last, jnp.maximum(first, bound), first)
            first_doc = jnp.where(bound <= span * SPAN, jnp.maximum(first_doc, bound), first_doc)
        begin = lax.shift_right_logical(first_doc, 7)
        table_ref[QUERY + s] = span
        table_ref[BEGIN + s] = begin
        steps = steps + lax.shift_right_logical(span - begin + GROUP, 1)
        lanes_ref[s, 0:1] = first
        lanes_ref[s, 1:2] = last
        sums_ref[s, 0:1] = lse_ref[pl.ds(((s // 2 - z) & 3) * 2 + s % 2, 1), :]
        parts = [packed_ref[2 * s + i, 2 * HEAD_DIM : PACKED].astype(jnp.float32) for i in range(2)]
        sums_ref[s, 1:2] = jnp.concatenate([part[0:1] + part[1:2] for part in parts], axis=1)
    for copy in copies:
        copy.wait()

    def operand(s, start):
        return jnp.concatenate([packed_ref[2 * s + i, start : start + HEAD_DIM] for i in range(2)], axis=1)

    def tiles_of(item):
        s, span = item
        return [table_ref[jnp.minimum(span + j, table_ref[QUERY + s])] for j in range(GROUP)]

    def tile(item, i):
        return jnp.concatenate([kv_ref[t, :, i].reshape(SPAN, HEAD_DIM) for t in tiles_of(item)], axis=0)

    def scores_stage(item, live, probs_ref, dscore_ref):
        s, span = item
        first, last = lanes_ref[s, 0:1], lanes_ref[s, 1:2]
        lse, delta = sums_ref[s, 0:1], sums_ref[s, 1:2]
        masks = []
        for j in range(GROUP):
            base = jnp.where(live & (span + j <= table_ref[QUERY + s]), (span + j) * SPAN, 8192)
            masks.append((row >= first - base) & (row <= last - base))
        allowed = jnp.concatenate(masks, axis=0)
        scores = dot(tile(item, 0), operand(s, 0), 1, 0)
        probs = jnp.where(allowed, jnp.exp(scores * factor - lse), 0.0)
        dprob = dot(tile(item, 1), operand(s, HEAD_DIM), 1, 0)
        probs_ref[...] = probs.astype(jnp.bfloat16)
        dscore_ref[...] = (probs * (dprob - delta)).astype(jnp.bfloat16)

    def sums_stage(item, probs_ref, dscore_ref):
        s, span = item
        probs, dscore = probs_ref[...], dscore_ref[...]
        part_v = dot(operand(s, HEAD_DIM), probs, 1, 1)
        part_k = dot(operand(s, 0), dscore, 1, 1)
        dq_sum[s] += dot(tile(item, 0), dscore, 0, 0)
        for i, part in ((0, part_k), (1, part_v)):
            for j, t in enumerate(tiles_of(item)):
                dkv_ref[t, i] += part[:, j * SPAN : (j + 1) * SPAN]

    def advance(item):
        s, span = item
        done = span + GROUP > table_ref[QUERY + s]
        following = jnp.where(done, jnp.minimum(s + 1, 7), s)
        return following, jnp.where(done, table_ref[BEGIN + following], span + GROUP)

    def two_steps(i, carry):
        before, item = carry
        scores_stage(item, True, buffers[0], buffers[1])
        sums_stage(before, buffers[2], buffers[3])
        following = advance(item)
        scores_stage(following, 2 * i + 1 < steps, buffers[2], buffers[3])
        sums_stage(item, buffers[0], buffers[1])
        return following, advance(following)

    start = (jnp.int32(0), table_ref[BEGIN])
    final, _ = lax.fori_loop(0, lax.shift_right_logical(steps + 1, 1), two_steps, (start, start))
    sums_stage(final, buffers[2], buffers[3])

    leaving = []

    def leave(source, target, sem):
        leaving.append(pltpu.make_async_copy(source, target, sem))
        leaving[-1].start()

    for i in range(16):
        lanes = slice((i % 2) * 256, (i % 2) * 256 + 256)
        dq_out[i] = (dq_sum[i // 2, :, lanes] * factor).astype(jnp.bfloat16)
    leave(dq_out, dq_ref, sems.at[12])
    for core in range(2):
        for slab in (2, 1, 3, 0):
            for t in range(8):
                start = slab * 16 + core * 8 + t
                key = (dkv_ref[start, 0] * factor).astype(jnp.bfloat16)
                value = dkv_ref[start, 1].astype(jnp.bfloat16)
                if core == 0:
                    keep_out[slab, t, 0], keep_out[slab, t, 1] = key, value
                else:
                    send[slab][t, 0], send[slab][t, 1] = key, value
            if core == 0:
                leave(keep_out.at[slab], keep[slab], sems.at[13 + slab])
    for copy in leaving:
        copy.wait()


VMEM = pl.BlockSpec(memory_space=pltpu.VMEM)
HBM = pl.BlockSpec(memory_space=pltpu.HBM)


def tiles(plan, bounds, packed, lse, mine, other):
    bf16, f32 = jnp.bfloat16, jnp.float32
    parts = [jax.ShapeDtypeStruct((8, 2, HEAD_DIM, SPAN), bf16)] * 4
    outs = pl.pallas_call(
        tiles_kernel,
        out_shape=[pltpu.HBM((16, HEAD_DIM, 256), bf16)] + [pltpu.HBM((8, 2, HEAD_DIM, SPAN), bf16)] * 4 + parts,
        in_specs=[HBM] * 2 + [VMEM] * 2 + [pl.BlockSpec(memory_space=pl.ANY)] * 10,
        out_specs=[HBM] * 5 + [VMEM] * 4,
        scratch_shapes=[
            pltpu.SMEM((32, 2), jnp.int32),
            pltpu.SMEM((12,), jnp.int32),
            pltpu.SMEM((TABLE,), jnp.int32),
            pltpu.VMEM((64, 2, 2, HALF, HEAD_DIM), bf16),
            pltpu.VMEM((64, 2, HEAD_DIM, SPAN), f32),
            pltpu.VMEM((8, HEAD_DIM, LANES), f32),
            pltpu.VMEM((16, HEAD_DIM, 256), bf16),
            pltpu.VMEM((4, 8, 2, HEAD_DIM, SPAN), bf16),
            pltpu.VMEM((8, 2, LANES), jnp.int32),
            pltpu.VMEM((8, 2, LANES), f32),
        ]
        + [pltpu.VMEM((GROUP * SPAN, LANES), bf16)] * 4
        + [pltpu.SemaphoreType.DMA((17,))],
        compiler_params=pltpu.CompilerParams(vmem_limit_bytes=26 * MIB),
        name="tiles",
    )(plan, bounds, packed, lse, *[part.reshape(-1, 2, 2, HALF, HEAD_DIM) for part in (*mine, *other)])
    return outs[0], outs[1:5], outs[5:9]


def shift(array, axis, by):
    return lax.ppermute(array, axis, [(i, (i + by) % 4) for i in range(4)])


def in_hbm(array):
    return pltpu.with_memory_space_constraint(array, pltpu.HBM)


def swap(array):
    return lax.ppermute(array, "c", [(0, 1), (1, 0)])


def exchange(array):
    return lax.all_to_all(array, ("z", "y"), 0, 0, tiled=True)


def shards(queries, keys, values, fwd_out, out_grad, log_norm, doc_bounds, span_plan, read_lists):
    bf16 = jnp.bfloat16
    f32 = jnp.float32
    z = lax.axis_index("z")

    kv_out = pl.pallas_call(
        pack_kv_kernel,
        out_shape=jax.ShapeDtypeStruct((4, 4, 2, HALF, HEAD_DIM), bf16),
        in_specs=[VMEM, VMEM],
        out_specs=VMEM,
        name="pack_kv",
    )(keys, values)
    block = exchange(kv_out.reshape(16, 2, HALF, HEAD_DIM))

    wide = pl.BlockSpec((HALF, 16 * HEAD_DIM), lambda y: (0, y))
    q_out = pl.pallas_call(
        pack_q_kernel,
        grid=(4,),
        out_shape=jax.ShapeDtypeStruct((4, 4, PACKED, 256), bf16),
        in_specs=[wide, wide, wide],
        out_specs=pl.BlockSpec((4, 1, PACKED, 256), lambda y: (0, y, 0, 0)),
        name="pack_q",
    )(queries, out_grad, fwd_out)
    norms = log_norm.reshape(2, 2, HALF, 4, 4).transpose(3, 0, 1, 4, 2).reshape(4, 2, LANES)
    to = [lax.dynamic_index_in_dim(norms, (z + k) % 4, 0, keepdims=False) for k in range(4)]
    lse = jnp.concatenate(
        [to[0], shift(to[3], "z", -1), shift(to[2], "z", 2), shift(to[1], "z", 1)], axis=0
    )
    q_out, lse = lax.optimization_barrier((q_out, lse))
    packed = exchange(q_out.reshape(16, PACKED, 256))

    from_next = shift(block, "x", -1)
    from_last = shift(block, "x", 1)
    far_a = shift(from_next[:8], "x", -1)
    far_b = shift(from_last[8:], "x", 1)

    plan, bounds = in_hbm(span_plan), in_hbm(doc_bounds)
    mine = [block, from_next, far_a, far_b, from_last]
    other = [swap(part) for part in mine]
    dq, keep, send = tiles(plan, bounds, packed, lse, mine, other)

    got = {k: in_hbm(swap(send[k])) for k in (2, 1, 3, 0)}
    keep = [in_hbm(part) for part in keep]
    half = [pl.BlockSpec((4, 2, HEAD_DIM, SPAN), lambda _, i=i: (i, 0, 0, 0)) for i in range(2)]
    piece = jax.ShapeDtypeStruct((4, 2, HEAD_DIM, SPAN), bf16)
    via_next, via_last, last_b, next_a = pl.pallas_call(
        functools.partial(add_kernel, 2),
        grid=(1,),
        out_shape=[piece] * 4,
        in_specs=[half[0]] * 2 + [half[1]] * 4 + [half[0]] * 2,
        out_specs=[half[0]] * 4,
        compiler_params=pltpu.CompilerParams(vmem_limit_bytes=8 * MIB),
        name="first_sums",
    )(keep[2], got[2], keep[2], got[2], keep[1], got[1], keep[3], got[3])
    via_next, via_last = shift(via_next, "x", 1), shift(via_last, "x", -1)
    last_b, next_a = shift(last_b, "x", 1), shift(next_a, "x", -1)
    last_a, next_b = pl.pallas_call(
        functools.partial(add_kernel, 3),
        grid=(1,),
        out_shape=[piece] * 2,
        in_specs=[half[0]] * 3 + [half[1]] * 2 + [half[0]],
        out_specs=[half[0]] * 2,
        compiler_params=pltpu.CompilerParams(vmem_limit_bytes=6 * MIB),
        name="second_sums",
    )(keep[1], got[1], via_next, keep[3], got[3], via_last)
    last_a, next_b = shift(last_a, "x", 1), shift(next_b, "x", -1)
    dq_back = exchange(dq).reshape(4, 4, HEAD_DIM, 256)
    total = pl.pallas_call(
        final_kernel,
        out_shape=jax.ShapeDtypeStruct((16, 2, HALF, HEAD_DIM), bf16),
        in_specs=[VMEM] * 6,
        out_specs=VMEM,
        compiler_params=pltpu.CompilerParams(vmem_limit_bytes=6 * MIB),
        name="own_slab",
    )(keep[0], got[0], last_a, last_b, next_a, next_b)
    total, dq_back = lax.optimization_barrier((total, dq_back))
    kv_back = exchange(total)
    grad_queries = pl.pallas_call(
        unpack_q_kernel,
        grid=(4,),
        out_shape=jax.ShapeDtypeStruct((HALF, 64 * HEAD_DIM), bf16),
        in_specs=[pl.BlockSpec((4, 1, HEAD_DIM, 256), lambda y: (0, y, 0, 0))],
        out_specs=wide,
        compiler_params=pltpu.CompilerParams(vmem_limit_bytes=6 * MIB),
        name="unpack_q",
    )(dq_back)
    grad_keys, grad_values = pl.pallas_call(
        unpack_kv_kernel,
        out_shape=[jax.ShapeDtypeStruct((HALF, 8 * HEAD_DIM), bf16)] * 2,
        in_specs=[VMEM],
        out_specs=[VMEM, VMEM],
        compiler_params=pltpu.CompilerParams(vmem_limit_bytes=4 * MIB),
        name="unpack_kv",
    )(kv_back.reshape(4, 4, 2, HALF, HEAD_DIM))
    return (grad_queries, grad_keys, grad_values)


def solution(mesh):
    fine = Mesh(mesh.devices.reshape(4, 4, 2, 4), ROWS)
    rows = P(ROWS, None)
    cp = ("z", "x", "c")
    in_specs = (rows, rows, rows, rows, rows, P(cp, "y"), P(), P(), P(cp, None, None))
    return jax.shard_map(shards, mesh=fine, in_specs=in_specs, out_specs=(rows, rows, rows), check_vma=False)
```

time: 126 us -> 123 us (0.976)
  waiting for transfers between devices: 46.9 us -> 39.7 us
  Pallas kernels: 25.4 us -> 30.2 us
  other arithmetic: 4.74 us -> 0.02 us
  local copies, waits for them, and re-layouts: 2.21 us -> 5.18 us
  starting transfers between devices: 44 us -> 46.4 us
    pallas_call x1 -> x4, Pallas kernels: 16.3 us -> 21.1 us  [the longest x1 15.6 us: tiles(): pl.pallas_call(tiles_kernel, out_shape=[pltpu.HBM((16, HEAD_DIM, 256), bf...]
    ppermute x11 -> x13, waiting for transfers between devices: 29.6 us -> 26 us  [shift(): return lax.ppermute(array, axis, [(i, (i + by) % 4) for i in range(4)])]
    ppermute x11 -> x13, starting transfers between devices: 19.4 us -> 22.6 us  [shift(): return lax.ppermute(array, axis, [(i, (i + by) % 4) for i in range(4)])]
    unnamed x11 -> x13, local copies, waits for them, and re-layouts: 0.11 us -> 3.27 us
    convert_element_type x3 -> x0, other arithmetic: 2.33 us -> none  [the longest x1 2.18 us: shards(): kv_back = exchange((sums[0] + near).astype(bf16))]
    all_to_all x4, waiting for transfers between devices: 15.2 us -> 13.2 us  [exchange(): return lax.all_to_all(array, ('z', 'y'), 0, 0, tiled=True)]
    ppermute x10 -> x9, waiting for transfers between devices: 2.03 us -> 0.52 us  [swap(): return lax.ppermute(array, 'c', [(0, 1), (1, 0)])]
  transfers between devices with their start and end apart: 25 -> 26, of which waited for: 12 -> 11; matrix products, arithmetic and copies ran while one was open for 6% -> 3% of each run, Pallas kernels for 5% -> 10%
where the time goes in v3:
time: 123 us; the launch traced here: 122 us
  starting transfers between devices  46.4 us (38%)
  waiting for transfers between devices  39.7 us (32%)
  Pallas kernels  30.2 us (25%)
  local copies, waits for them, and re-layouts  5.18 us (4%)
    ppermute x13, waiting for transfers between devices, shift(): return lax.ppermute(array, axis, [(i, (i + by) % 4) for i in range(4)])  26 us
    all_to_all x4, starting transfers between devices, exchange(): return lax.all_to_all(array, ('z', 'y'), 0, 0, tiled=True)  23 us
    ppermute x13, starting transfers between devices, shift(): return lax.ppermute(array, axis, [(i, (i + by) % 4) for i in range(4)])  22.6 us
    pallas_call x1, Pallas kernels, tiles(): pl.pallas_call(tiles_kernel, out_shape=[pltpu.HBM((16, HEAD_DIM, 256), bf...  15.6 us
    all_to_all x4, waiting for transfers between devices, exchange(): return lax.all_to_all(array, ('z', 'y'), 0, 0, tiled=True)  13.2 us
    pallas_call x1, Pallas kernels, shards(): pl.pallas_call(pack_q_kernel, grid=(4,), out_shape=jax.ShapeDtypeStruct((...  4.7 us
    unnamed x13, local copies, waits for them, and re-layouts  3.27 us
  transfers between devices with their start and end apart: 26, of which 11 were waited for; matrix products, arithmetic and copies ran while one was open for 3% of the time, Pallas kernels for 10%

profile of v3, /device:TPU:0, one launch (start us, length us, event | category | flops | bytes accessed | tf_op | source)
XLA Modules:
  0.0 122.4 jit_solution(9795052055207496362)
XLA Ops:
  0.6 1.8 %pack_kv.1 = bf16[4,4,2,64,128]{4,3,2,1,0:T(8,128)(2,1)} custom-call(bf16[64,1024]{1,0:T(8,128)(2,1)} %keys_ref.1, bf16[64,1024]{1,0:T(8,128)(2,1)} %values_ref.1), custom_call_target="tpu_custom_call" | custom-call | tf_op jit(solution)/shard_map/pack_kv/pallas_call | solution.py:284
  2.5 8.1 %all-to-all-start.1 = ((bf16[16,2,64,128]{3,2,1,0:T(8,128)(2,1)}), bf16[16,2,64,128]{3,2,1,0:T(8,128)(2,1)S(1)}, u32[]{:S(2)}, u32[]{:S(2)}) async-start(bf16[16,2,64,128]{3,2,1,0:T(8,128)(2,1)} %bitcast.31), calls=%async_computation.1 | async-start | bytes 1048576 | tf_op jit(solution)/shard_map/all_to_all | solution.py:276
  11.6 1.9 %collective-permute-start.2 = (f32[2,512]{1,0:T(2,128)S(1)}, f32[2,512]{1,0:T(2,128)S(1)}, u32[]{:S(2)}, u32[]{:S(2)}) collective-permute-start(f32[2,512]{1,0:T(2,128)S(1)} %get-tuple-element.46), channel_id=1, source_target_pairs={{0,32},{32,64},{64,96},{96,0},{1,33},{33,65},{65,97},{97,1},{2,34}... | collective-permute-start | bytes 12296 | tf_op jit(solution)/shard_map/ppermute | solution.py:264
  13.6 2.7 %collective-permute-start.1 = (f32[2,512]{1,0:T(2,128)S(1)}, f32[2,512]{1,0:T(2,128)S(1)}, u32[]{:S(2)}, u32[]{:S(2)}) collective-permute-start(f32[2,512]{1,0:T(2,128)S(1)} %get-tuple-element.47), channel_id=1, source_target_pairs={{0,64},{32,96},{64,0},{96,32},{1,65},{33,97},{65,1},{97,33},{2,66}... | collective-permute-start | bytes 12296 | tf_op jit(solution)/shard_map/ppermute | solution.py:264
  17.7 4.7 %pack_q.1 = bf16[4,4,272,256]{3,2,1,0:T(8,128)(2,1)} custom-call(bf16[64,8192]{1,0:T(8,128)(2,1)} %queries_ref.1, bf16[64,8192]{1,0:T(8,128)(2,1)} %grad_ref.1, bf16[64,8192]{1,0:T(8,128)(2,1)} %fwd_ref.1), custom_call_target="tpu_custom_call" | custom-call | tf_op jit(solution)/shard_map/pack_q/pallas_call | solution.py:294
  22.4 4.4 %all-to-all-start = ((bf16[16,272,256]{2,1,0:T(8,128)(2,1)}), bf16[16,272,256]{2,1,0:T(8,128)(2,1)S(1)}, u32[]{:S(2)}, u32[]{:S(2)}) async-start(bf16[16,272,256]{2,1,0:T(8,128)(2,1)} %bitcast.30), calls=%async_computation | async-start | bytes 4456448 | tf_op jit(solution)/shard_map/all_to_all | solution.py:276
  28.4 1.7 %collective-permute-start.3 = (bf16[16,2,64,128]{3,2,1,0:T(8,128)(2,1)S(1)}, bf16[16,2,64,128]{3,2,1,0:T(8,128)(2,1)}, u32[]{:S(2)}, u32[]{:S(2)}) collective-permute-start(bf16[16,2,64,128]{3,2,1,0:T(8,128)(2,1)S(1)} %all-to-all-done.1), channel_id=1, source_target_pairs={{0,24},{8,0},{16,8},{24,16},{1,25},{9,1},{17,9},{25,17},{2,26},{10... | collective-permute-start | bytes 1572872 | tf_op jit(solution)/shard_map/ppermute | solution.py:264
  30.1 10.0 %collective-permute-done.5 = bf16[16,2,64,128]{3,2,1,0:T(8,128)(2,1)S(1)} collective-permute-done((bf16[16,2,64,128]{3,2,1,0:T(8,128)(2,1)S(1)}, bf16[16,2,64,128]{3,2,1,0:T(8,128)(2,1)S(1)}, u32[]{:S(2)}, u32[]{:S(2)}) %collective-permute-start.5) | collective-permute-done | bytes 524320 | tf_op jit(solution)/shard_map/ppermute | solution.py:264
  41.4 3.0 %collective-permute-start.4 = (bf16[8,2,64,128]{3,2,1,0:T(8,128)(2,1)S(1)}, bf16[8,2,64,128]{3,2,1,0:T(8,128)(2,1)}, u32[]{:S(2)}, u32[]{:S(2)}) collective-permute-start(bf16[8,2,64,128]{3,2,1,0:T(8,128)(2,1)S(1)} %slice.8), channel_id=1, source_target_pairs={{0,24},{8,0},{16,8},{24,16},{1,25},{9,1},{17,9},{25,17},{2,26},{10... | collective-permute-start | bytes 786440 | tf_op jit(solution)/shard_map/ppermute | solution.py:264
  44.7 3.1 %collective-permute-done.6 = bf16[8,2,64,128]{3,2,1,0:T(8,128)(2,1)S(1)} collective-permute-done((bf16[8,2,64,128]{3,2,1,0:T(8,128)(2,1)S(1)}, bf16[8,2,64,128]{3,2,1,0:T(8,128)(2,1)S(1)}, u32[]{:S(2)}, u32[]{:S(2)}) %collective-permute-start.6) | collective-permute-done | bytes 262176 | tf_op jit(solution)/shard_map/ppermute | solution.py:264
  47.8 2.9 %collective-permute-done.4 = bf16[8,2,64,128]{3,2,1,0:T(8,128)(2,1)} collective-permute-done((bf16[8,2,64,128]{3,2,1,0:T(8,128)(2,1)S(1)}, bf16[8,2,64,128]{3,2,1,0:T(8,128)(2,1)}, u32[]{:S(2)}, u32[]{:S(2)}) %collective-permute-start.4) | collective-permute-done | bytes 262176 | tf_op jit(solution)/shard_map/ppermute | solution.py:264
  52.6 4.9 %all-to-all-done.packed_ref = bf16[16,272,256]{2,1,0:T(8,128)(2,1)S(1)} async-done(((bf16[16,272,256]{2,1,0:T(8,128)(2,1)}), bf16[16,272,256]{2,1,0:T(8,128)(2,1)S(1)}, u32[]{:S(2)}, u32[]{:S(2)}) %all-to-all-start) | async-done | bytes 2228256 | tf_op jit(solution)/shard_map/all_to_all | solution.py:276
  57.5 15.6 %tiles.1 = (bf16[16,128,256]{2,1,0:T(8,128)(2,1)}, bf16[8,2,128,128]{3,2,1,0:T(8,128)(2,1)}, bf16[8,2,128,128]{3,2,1,0:T(8,128)(2,1)}, bf16[8,2,128,128]{3,2,1,0...) custom-call(s32[32,2]{1,0:T(8,128)} %copy.12.plan_in, ...), custom_call_target="tpu_custom_call" | custom-call | tf_op jit(solution)/shard_map/tiles/pallas_call | solution.py:238
  74.5 3.7 %all-to-all-start.2 = ((bf16[16,128,256]{2,1,0:T(8,128)(2,1)}), bf16[16,128,256]{2,1,0:T(8,128)(2,1)S(1)}, u32[]{:S(2)}, u32[]{:S(2)}) async-start(bf16[16,128,256]{2,1,0:T(8,128)(2,1)} %get-tuple-element.40), calls=%async_computation.2 | async-start | bytes 2097152 | tf_op jit(solution)/shard_map/all_to_all | solution.py:276
  79.3 1.7 %first_sums.1 = (bf16[4,2,128,128]{3,2,1,0:T(8,128)(2,1)S(1)}, bf16[4,2,128,128]{3,2,1,0:T(8,128)(2,1)S(1)}, bf16[4,2,128,128]{3,2,1,0:T(8,128)(2,1)S(1)}, bf16[4,2,128,128]{3,2,1,0:T(8,128)(2,1)S(1)}) custom-call(bf16[8,2,128,128]{3,2,1,0:T(8,128)(2,1)} %get-tuple-element.30.refs_0_.refs_2_, bf16[8,2,128,128]{3,2,1,0:T(8,128)(2,1)} %copy-done.4, ...), custom_call_target="tpu_custom_call" | custom-call | tf_op jit(solution)/shard_map/first_sums/pallas_call | solution.py:324
  82.6 1.7 %collective-permute-start.17 = (bf16[4,2,128,128]{3,2,1,0:T(8,128)(2,1)S(1)}, bf16[4,2,128,128]{3,2,1,0:T(8,128)(2,1)S(1)}, u32[]{:S(2)}, u32[]{:S(2)}) collective-permute-start(bf16[4,2,128,128]{3,2,1,0:T(8,128)(2,1)S(1)} %get-tuple-element.35), channel_id=1, source_target_pairs={{0,24},{8,0},{16,8},{24,16},{1,25},{9,1},{17,9},{25,17},{2,26},{10... | collective-permute-start | bytes 786440 | tf_op jit(solution)/shard_map/ppermute | solution.py:264
  84.6 2.9 %collective-permute-start.20 = (bf16[4,2,128,128]{3,2,1,0:T(8,128)(2,1)S(1)}, bf16[4,2,128,128]{3,2,1,0:T(8,128)(2,1)S(1)}, u32[]{:S(2)}, u32[]{:S(2)}) collective-permute-start(bf16[4,2,128,128]{3,2,1,0:T(8,128)(2,1)S(1)} %get-tuple-element.38), channel_id=1, source_target_pairs={{0,24},{8,0},{16,8},{24,16},{1,25},{9,1},{17,9},{25,17},{2,26},{10... | collective-permute-start | bytes 786440 | tf_op jit(solution)/shard_map/ppermute | solution.py:264
  87.6 3.8 %collective-permute-done.16.refs_2_ = bf16[4,2,128,128]{3,2,1,0:T(8,128)(2,1)S(1)} collective-permute-done((bf16[4,2,128,128]{3,2,1,0:T(8,128)(2,1)S(1)}, bf16[4,2,128,128]{3,2,1,0:T(8,128)(2,1)S(1)}, u32[]{:S(2)}, u32[]{:S(2)}) %collective-permute-start.16) | collective-permute-done | bytes 262176 | tf_op jit(solution)/shard_map/ppermute | solution.py:264
  94.7 1.7 %collective-permute-start.21 = (bf16[4,2,128,128]{3,2,1,0:T(8,128)(2,1)S(1)}, bf16[4,2,128,128]{3,2,1,0:T(8,128)(2,1)S(1)}, u32[]{:S(2)}, u32[]{:S(2)}) collective-permute-start(bf16[4,2,128,128]{3,2,1,0:T(8,128)(2,1)S(1)} %get-tuple-element.39), channel_id=1, source_target_pairs={{0,24},{8,0},{16,8},{24,16},{1,25},{9,1},{17,9},{25,17},{2,26},{10... | collective-permute-start | bytes 786440 | tf_op jit(solution)/shard_map/ppermute | solution.py:264
  97.3 4.9 %collective-permute-done.18.last_a_ref = bf16[4,2,128,128]{3,2,1,0:T(8,128)(2,1)S(1)} collective-permute-done((bf16[4,2,128,128]{3,2,1,0:T(8,128)(2,1)S(1)}, bf16[4,2,128,128]{3,2,1,0:T(8,128)(2,1)S(1)}, u32[]{:S(2)}, u32[]{:S(2)}) %collective-permute-start.18) | collective-permute-done | bytes 262176 | tf_op jit(solution)/shard_map/ppermute | solution.py:264
  102.3 2.3 %own_slab.1 = bf16[16,2,64,128]{3,2,1,0:T(8,128)(2,1)} custom-call(bf16[8,2,128,128]{3,2,1,0:T(8,128)(2,1)} %get-tuple-element.26.keep_ref, bf16[8,2,128,128]{3,2,1,0:T(8,128)(2,1)} %copy-done.5, bf16[4,2,128,128]{3,2,1,0:T(8,128)(2,1)S(1)} %collective-permute-done.18.last_a_ref, bf16[4,2,128,128]{3,2,1,0:T(8,128)(2,1)S(1)} %collective-permute-done.19.last_b_ref, ...), custom_call_target="tpu_custom_call" | custom-call | tf_op jit(solution)/shard_map/own_slab/pallas_call | solution.py:346
  104.6 6.9 %all-to-all-start.3 = ((bf16[16,2,64,128]{3,2,1,0:T(8,128)(2,1)}), bf16[16,2,64,128]{3,2,1,0:T(8,128)(2,1)S(1)}, u32[]{:S(2)}, u32[]{:S(2)}) async-start(bf16[16,2,64,128]{3,2,1,0:T(8,128)(2,1)} %own_slab.1), calls=%async_computation.3 | async-start | bytes 1048576 | tf_op jit(solution)/shard_map/all_to_all | solution.py:276
  111.5 1.9 %unpack_q.1 = bf16[64,8192]{1,0:T(8,128)(2,1)} custom-call(bf16[4,4,128,256]{3,2,1,0:T(8,128)(2,1)S(1)} %bitcast.25), custom_call_target="tpu_custom_call" | custom-call | tf_op jit(solution)/shard_map/unpack_q/pallas_call | solution.py:356
  113.4 8.2 %all-to-all-done.3 = bf16[16,2,64,128]{3,2,1,0:T(8,128)(2,1)S(1)} async-done(((bf16[16,2,64,128]{3,2,1,0:T(8,128)(2,1)}), bf16[16,2,64,128]{3,2,1,0:T(8,128)(2,1)S(1)}, u32[]{:S(2)}, u32[]{:S(2)}) %all-to-all-start.3) | async-done | bytes 524320 | tf_op jit(solution)/shard_map/all_to_all | solution.py:276
  (56 shorter events, 16.7 us)
Async XLA Ops:
  2.5 20.0 %all-to-all-start.1 = ((bf16[16,2,64,128]{3,2,1,0:T(8,128)(2,1)}), bf16[16,2,64,128]{3,2,1,0:T(8,128)(2,1)S(1)}, u32[]{:S(2)}, u32[]{:S(2)}) async-start(bf16[16,2,64,128]{3,2,1,0:T(8,128)(2,1)} %bitcast.31), calls=%async_computation.1 | async-start | bytes 1048576 | tf_op jit(solution)/shard_map/all_to_all | solution.py:276
  11.6 10.8 %collective-permute-start.2 = (f32[2,512]{1,0:T(2,128)S(1)}, f32[2,512]{1,0:T(2,128)S(1)}, u32[]{:S(2)}, u32[]{:S(2)}) collective-permute-start(f32[2,512]{1,0:T(2,128)S(1)} %get-tuple-element.46), channel_id=1, source_target_pairs={{0,32},{32,64},{64,96},{96,0},{1,33},{33,65},{65,97},{97,1},{2,34}... | collective-permute-start | bytes 12296 | tf_op jit(solution)/shard_map/ppermute | solution.py:264
  13.6 8.8 %collective-permute-start.1 = (f32[2,512]{1,0:T(2,128)S(1)}, f32[2,512]{1,0:T(2,128)S(1)}, u32[]{:S(2)}, u32[]{:S(2)}) collective-permute-start(f32[2,512]{1,0:T(2,128)S(1)} %get-tuple-element.47), channel_id=1, source_target_pairs={{0,64},{32,96},{64,0},{96,32},{1,65},{33,97},{65,1},{97,33},{2,66}... | collective-permute-start | bytes 12296 | tf_op jit(solution)/shard_map/ppermute | solution.py:264
  16.2 6.2 %collective-permute-start = (f32[2,512]{1,0:T(2,128)S(1)}, f32[2,512]{1,0:T(2,128)S(1)}, u32[]{:S(2)}, u32[]{:S(2)}) collective-permute-start(f32[2,512]{1,0:T(2,128)S(1)} %get-tuple-element.48), channel_id=1, source_target_pairs={{0,96},{32,0},{64,32},{96,64},{1,97},{33,1},{65,33},{97,65},{2,98}... | collective-permute-start | bytes 12296 | tf_op jit(solution)/shard_map/ppermute | solution.py:264
  22.4 35.1 %all-to-all-start = ((bf16[16,272,256]{2,1,0:T(8,128)(2,1)}), bf16[16,272,256]{2,1,0:T(8,128)(2,1)S(1)}, u32[]{:S(2)}, u32[]{:S(2)}) async-start(bf16[16,272,256]{2,1,0:T(8,128)(2,1)} %bitcast.30), calls=%async_computation | async-start | bytes 4456448 | tf_op jit(solution)/shard_map/all_to_all | solution.py:276
  26.8 13.3 %collective-permute-start.5 = (bf16[16,2,64,128]{3,2,1,0:T(8,128)(2,1)S(1)}, bf16[16,2,64,128]{3,2,1,0:T(8,128)(2,1)S(1)}, u32[]{:S(2)}, u32[]{:S(2)}) collective-permute-start(bf16[16,2,64,128]{3,2,1,0:T(8,128)(2,1)S(1)} %all-to-all-done.1), channel_id=1, source_target_pairs={{0,8},{8,16},{16,24},{24,0},{1,9},{9,17},{17,25},{25,1},{2,10},{10... | collective-permute-start | bytes 1572872 | tf_op jit(solution)/shard_map/ppermute | solution.py:264
  28.4 12.1 %collective-permute-start.3 = (bf16[16,2,64,128]{3,2,1,0:T(8,128)(2,1)S(1)}, bf16[16,2,64,128]{3,2,1,0:T(8,128)(2,1)}, u32[]{:S(2)}, u32[]{:S(2)}) collective-permute-start(bf16[16,2,64,128]{3,2,1,0:T(8,128)(2,1)S(1)} %all-to-all-done.1), channel_id=1, source_target_pairs={{0,24},{8,0},{16,8},{24,16},{1,25},{9,1},{17,9},{25,17},{2,26},{10... | collective-permute-start | bytes 1572872 | tf_op jit(solution)/shard_map/ppermute | solution.py:264
  30.1 21.9 %collective-permute-start.7 = (bf16[16,2,64,128]{3,2,1,0:T(8,128)(2,1)S(1)}, bf16[16,2,64,128]{3,2,1,0:T(8,128)(2,1)}, u32[]{:S(2)}, u32[]{:S(2)}) collective-permute-start(bf16[16,2,64,128]{3,2,1,0:T(8,128)(2,1)S(1)} %all-to-all-done.1), channel_id=1, source_target_pairs={{0,4},{4,0},{1,5},{5,1},{2,6},{6,2},{3,7},{7,3},{8,12},{12,8},{9,1... | collective-permute-start | bytes 1572872 | tf_op jit(solution)/shard_map/ppermute | solution.py:272
  40.1 7.7 %collective-permute-start.6 = (bf16[8,2,64,128]{3,2,1,0:T(8,128)(2,1)S(1)}, bf16[8,2,64,128]{3,2,1,0:T(8,128)(2,1)S(1)}, u32[]{:S(2)}, u32[]{:S(2)}) collective-permute-start(bf16[8,2,64,128]{3,2,1,0:T(8,128)(2,1)S(1)} %slice.9), channel_id=1, source_target_pairs={{0,8},{8,16},{16,24},{24,0},{1,9},{9,17},{17,25},{25,1},{2,10},{10... | collective-permute-start | bytes 786440 | tf_op jit(solution)/shard_map/ppermute | solution.py:264
  40.5 11.6 %collective-permute-start.11 = (bf16[16,2,64,128]{3,2,1,0:T(8,128)(2,1)S(1)}, bf16[16,2,64,128]{3,2,1,0:T(8,128)(2,1)}, u32[]{:S(2)}, u32[]{:S(2)}) collective-permute-start(bf16[16,2,64,128]{3,2,1,0:T(8,128)(2,1)S(1)} %collective-permute-done.5), channel_id=1, source_target_pairs={{0,4},{4,0},{1,5},{5,1},{2,6},{6,2},{3,7},{7,3},{8,12},{12,8},{9,1... | collective-permute-start | bytes 1572872 | tf_op jit(solution)/shard_map/ppermute | solution.py:272
  41.4 9.3 %collective-permute-start.4 = (bf16[8,2,64,128]{3,2,1,0:T(8,128)(2,1)S(1)}, bf16[8,2,64,128]{3,2,1,0:T(8,128)(2,1)}, u32[]{:S(2)}, u32[]{:S(2)}) collective-permute-start(bf16[8,2,64,128]{3,2,1,0:T(8,128)(2,1)S(1)} %slice.8), channel_id=1, source_target_pairs={{0,24},{8,0},{16,8},{24,16},{1,25},{9,1},{17,9},{25,17},{2,26},{10... | collective-permute-start | bytes 786440 | tf_op jit(solution)/shard_map/ppermute | solution.py:264
  44.5 8.1 %collective-permute-start.8 = (bf16[16,2,64,128]{3,2,1,0:T(8,128)(2,1)}, bf16[16,2,64,128]{3,2,1,0:T(8,128)(2,1)}, u32[]{:S(2)}, u32[]{:S(2)}) collective-permute-start(bf16[16,2,64,128]{3,2,1,0:T(8,128)(2,1)} %collective-permute-done.3), channel_id=1, source_target_pairs={{0,4},{4,0},{1,5},{5,1},{2,6},{6,2},{3,7},{7,3},{8,12},{12,8},{9,1... | collective-permute-start | bytes 1572872 | tf_op jit(solution)/shard_map/ppermute | solution.py:272
  47.8 4.3 %collective-permute-start.10 = (bf16[8,2,64,128]{3,2,1,0:T(8,128)(2,1)S(1)}, bf16[8,2,64,128]{3,2,1,0:T(8,128)(2,1)}, u32[]{:S(2)}, u32[]{:S(2)}) collective-permute-start(bf16[8,2,64,128]{3,2,1,0:T(8,128)(2,1)S(1)} %collective-permute-done.6), channel_id=1, source_target_pairs={{0,4},{4,0},{1,5},{5,1},{2,6},{6,2},{3,7},{7,3},{8,12},{12,8},{9,1... | collective-permute-start | bytes 786440 | tf_op jit(solution)/shard_map/ppermute | solution.py:272
  73.9 4.2 %collective-permute-start.13 = (bf16[8,2,128,128]{3,2,1,0:T(8,128)(2,1)}, bf16[8,2,128,128]{3,2,1,0:T(8,128)(2,1)S(1)}, u32[]{:S(2)}, u32[]{:S(2)}) collective-permute-start(bf16[8,2,128,128]{3,2,1,0:T(8,128)(2,1)} %get-tuple-element.29), channel_id=1, source_target_pairs={{0,4},{4,0},{1,5},{5,1},{2,6},{6,2},{3,7},{7,3},{8,12},{12,8},{9,1... | collective-permute-start | bytes 1572872 | tf_op jit(solution)/shard_map/ppermute | solution.py:272
  73.9 4.2 %collective-permute-start.14 = (bf16[8,2,128,128]{3,2,1,0:T(8,128)(2,1)}, bf16[8,2,128,128]{3,2,1,0:T(8,128)(2,1)S(1)}, u32[]{:S(2)}, u32[]{:S(2)}) collective-permute-start(bf16[8,2,128,128]{3,2,1,0:T(8,128)(2,1)} %get-tuple-element.31), channel_id=1, source_target_pairs={{0,4},{4,0},{1,5},{5,1},{2,6},{6,2},{3,7},{7,3},{8,12},{12,8},{9,1... | collective-permute-start | bytes 1572872 | tf_op jit(solution)/shard_map/ppermute | solution.py:272
  74.5 30.2 %all-to-all-start.2 = ((bf16[16,128,256]{2,1,0:T(8,128)(2,1)}), bf16[16,128,256]{2,1,0:T(8,128)(2,1)S(1)}, u32[]{:S(2)}, u32[]{:S(2)}) async-start(bf16[16,128,256]{2,1,0:T(8,128)(2,1)} %get-tuple-element.40), calls=%async_computation.2 | async-start | bytes 2097152 | tf_op jit(solution)/shard_map/all_to_all | solution.py:276
  81.0 10.4 %collective-permute-start.16 = (bf16[4,2,128,128]{3,2,1,0:T(8,128)(2,1)S(1)}, bf16[4,2,128,128]{3,2,1,0:T(8,128)(2,1)S(1)}, u32[]{:S(2)}, u32[]{:S(2)}) collective-permute-start(bf16[4,2,128,128]{3,2,1,0:T(8,128)(2,1)S(1)} %get-tuple-element.34), channel_id=1, source_target_pairs={{0,8},{8,16},{16,24},{24,0},{1,9},{9,17},{17,25},{25,1},{2,10},{10... | collective-permute-start | bytes 786440 | tf_op jit(solution)/shard_map/ppermute | solution.py:264
  82.6 9.1 %collective-permute-start.17 = (bf16[4,2,128,128]{3,2,1,0:T(8,128)(2,1)S(1)}, bf16[4,2,128,128]{3,2,1,0:T(8,128)(2,1)S(1)}, u32[]{:S(2)}, u32[]{:S(2)}) collective-permute-start(bf16[4,2,128,128]{3,2,1,0:T(8,128)(2,1)S(1)} %get-tuple-element.35), channel_id=1, source_target_pairs={{0,24},{8,0},{16,8},{24,16},{1,25},{9,1},{17,9},{25,17},{2,26},{10... | collective-permute-start | bytes 786440 | tf_op jit(solution)/shard_map/ppermute | solution.py:264
  84.3 12.1 %collective-permute-start.12 = (bf16[8,2,128,128]{3,2,1,0:T(8,128)(2,1)S(1)}, bf16[8,2,128,128]{3,2,1,0:T(8,128)(2,1)S(1)}, u32[]{:S(2)}, u32[]{:S(2)}) collective-permute-start(bf16[8,2,128,128]{3,2,1,0:T(8,128)(2,1)S(1)} %copy-done.1), channel_id=1, source_target_pairs={{0,4},{4,0},{1,5},{5,1},{2,6},{6,2},{3,7},{7,3},{8,12},{12,8},{9,1... | collective-permute-start | bytes 1572872 | tf_op jit(solution)/shard_map/ppermute | solution.py:272
  84.3 12.7 %collective-permute-start.19 = (bf16[4,2,128,128]{3,2,1,0:T(8,128)(2,1)S(1)}, bf16[4,2,128,128]{3,2,1,0:T(8,128)(2,1)S(1)}, u32[]{:S(2)}, u32[]{:S(2)}) collective-permute-start(bf16[4,2,128,128]{3,2,1,0:T(8,128)(2,1)S(1)} %get-tuple-element.37), channel_id=1, source_target_pairs={{0,8},{8,16},{16,24},{24,0},{1,9},{9,17},{17,25},{25,1},{2,10},{10... | collective-permute-start | bytes 786440 | tf_op jit(solution)/shard_map/ppermute | solution.py:264
  84.6 12.7 %collective-permute-start.20 = (bf16[4,2,128,128]{3,2,1,0:T(8,128)(2,1)S(1)}, bf16[4,2,128,128]{3,2,1,0:T(8,128)(2,1)S(1)}, u32[]{:S(2)}, u32[]{:S(2)}) collective-permute-start(bf16[4,2,128,128]{3,2,1,0:T(8,128)(2,1)S(1)} %get-tuple-element.38), channel_id=1, source_target_pairs={{0,24},{8,0},{16,8},{24,16},{1,25},{9,1},{17,9},{25,17},{2,26},{10... | collective-permute-start | bytes 786440 | tf_op jit(solution)/shard_map/ppermute | solution.py:264
  93.1 9.1 %collective-permute-start.18 = (bf16[4,2,128,128]{3,2,1,0:T(8,128)(2,1)S(1)}, bf16[4,2,128,128]{3,2,1,0:T(8,128)(2,1)S(1)}, u32[]{:S(2)}, u32[]{:S(2)}) collective-permute-start(bf16[4,2,128,128]{3,2,1,0:T(8,128)(2,1)S(1)} %get-tuple-element.36), channel_id=1, source_target_pairs={{0,8},{8,16},{16,24},{24,0},{1,9},{9,17},{17,25},{25,1},{2,10},{10... | collective-permute-start | bytes 786440 | tf_op jit(solution)/shard_map/ppermute | solution.py:264
  94.7 7.6 %collective-permute-start.21 = (bf16[4,2,128,128]{3,2,1,0:T(8,128)(2,1)S(1)}, bf16[4,2,128,128]{3,2,1,0:T(8,128)(2,1)S(1)}, u32[]{:S(2)}, u32[]{:S(2)}) collective-permute-start(bf16[4,2,128,128]{3,2,1,0:T(8,128)(2,1)S(1)} %get-tuple-element.39), channel_id=1, source_target_pairs={{0,24},{8,0},{16,8},{24,16},{1,25},{9,1},{17,9},{25,17},{2,26},{10... | collective-permute-start | bytes 786440 | tf_op jit(solution)/shard_map/ppermute | solution.py:264
  104.6 17.0 %all-to-all-start.3 = ((bf16[16,2,64,128]{3,2,1,0:T(8,128)(2,1)}), bf16[16,2,64,128]{3,2,1,0:T(8,128)(2,1)S(1)}, u32[]{:S(2)}, u32[]{:S(2)}) async-start(bf16[16,2,64,128]{3,2,1,0:T(8,128)(2,1)} %own_slab.1), calls=%async_computation.3 | async-start | bytes 1048576 | tf_op jit(solution)/shard_map/all_to_all | solution.py:276
  (8 other events, 21.3 us)

commit v4 on v3

--- a/solution.py
+++ b/solution.py
@@ -10,6 +10,7 @@
 HEAD_DIM = 128
 SPAN = 128
 HALF = 64
+LOG2E = 1.4426950408889634
 LANES = 512
 PACKED = 272
 ROWS = ("z", "x", "c", "y")
@@ -28,7 +29,7 @@
             out_ref[z, y, 1] = values_ref[:, cols]
 
 
-def pack_q_kernel(queries_ref, grad_ref, fwd_ref, out_ref):
+def pack_q_kernel(queries_ref, grad_ref, fwd_ref, norms_ref, out_ref):
     row = lax.broadcasted_iota(jnp.int32, (16, HEAD_DIM), 0)
     pick = (row < 2).astype(jnp.bfloat16)
     for z in range(4):
@@ -45,7 +46,12 @@
             low = (product - high.astype(jnp.float32)).astype(jnp.bfloat16)
             delta = dot(pick, high, 1, 1) + dot(pick, low, 1, 1)
             high = delta.astype(jnp.bfloat16).astype(jnp.float32)
-            out_ref[z, 0, 2 * HEAD_DIM : PACKED, lanes] = jnp.where(row < 1, high, delta - high).astype(jnp.bfloat16)
+            pieces, rest = [], norms_ref[z, :, lanes]
+            for _ in range(3):
+                pieces.append(rest.astype(jnp.bfloat16).astype(jnp.float32))
+                rest = rest - pieces[-1]
+            tail = jnp.concatenate([high[0:1], (delta - high)[1:2], *pieces, high[0:2]], axis=0)
+            out_ref[z, 0, 2 * HEAD_DIM : PACKED, lanes] = tail.astype(jnp.bfloat16)
 
 
 def unpack_q_kernel(in_ref, out_ref):
@@ -61,18 +67,18 @@
     count = len(refs) // (terms + 1)
     for i in range(count):
         for t in range(4):
-            total = refs[i * terms][t].astype(jnp.float32)
+            total = refs[i * terms][0, t].astype(jnp.float32)
             for k in range(1, terms):
-                total = total + refs[i * terms + k][t].astype(jnp.float32)
-            refs[count * terms + i][t] = total.astype(jnp.bfloat16)
+                total = total + refs[i * terms + k][0, t].astype(jnp.float32)
+            refs[count * terms + i][0, t] = total.astype(jnp.bfloat16)
 
 
 def final_kernel(keep_ref, got_ref, last_a_ref, last_b_ref, next_a_ref, next_b_ref, out_ref):
     for t in range(8):
         last_ref, next_ref = ((last_a_ref, next_a_ref), (last_b_ref, next_b_ref))[t // 4]
         for i in range(2):
-            total = keep_ref[t, i].astype(jnp.float32) + got_ref[t, i].astype(jnp.float32)
-            total = total + last_ref[t % 4, i].astype(jnp.float32) + next_ref[t % 4, i].astype(jnp.float32)
+            total = keep_ref[0, t, i].astype(jnp.float32) + got_ref[0, t, i].astype(jnp.float32)
+            total = total + last_ref[0, t % 4, i].astype(jnp.float32) + next_ref[0, t % 4, i].astype(jnp.float32)
             rows = jnp.transpose(total).astype(jnp.bfloat16)
             out_ref[2 * t, i] = rows[:HALF]
             out_ref[2 * t + 1, i] = rows[HALF:]
@@ -92,10 +98,10 @@
 QUERY, BEGIN, TABLE = 64, 72, 80
 
 
-def tiles_kernel(plan_in, bounds_in, packed_ref, lse_ref, *rest):
-    mine, other, dq_ref, keep, send, rest = rest[:5], rest[5:10], rest[10], rest[11:15], rest[15:19], rest[19:]
+def tiles_kernel(plan_in, bounds_in, packed_ref, *rest):
+    mine, other, (dq_ref, keep_ref, send_ref), rest = rest[:5], rest[5:10], rest[10:13], rest[13:]
     plan_ref, bounds_ref, table_ref, kv_ref, dkv_ref, dq_sum, dq_out, keep_out, lanes_ref, sums_ref, *buffers, sems = rest
-    z, x, c = lax.axis_index("z"), lax.axis_index("x"), lax.axis_index("c")
+    y, x, c = lax.axis_index("y"), lax.axis_index("x"), lax.axis_index("c")
     factor = HEAD_DIM ** (-0.5)
 
     small = [
@@ -142,7 +148,10 @@
         steps = steps + lax.shift_right_logical(span - begin + GROUP, 1)
         lanes_ref[s, 0:1] = first
         lanes_ref[s, 1:2] = last
-        sums_ref[s, 0:1] = lse_ref[pl.ds(((s // 2 - z) & 3) * 2 + s % 2, 1), :]
+        norms = packed_ref[s // 2 * 4 + y, 2 * HEAD_DIM : PACKED].astype(jnp.float32)
+        rows = [slice(2 + s % 2 * 2 + i, 3 + s % 2 * 2 + i) for i in range(2)]
+        norms = [norms[r] + norms[r.start + 4 : r.stop + 4] + norms[r.start + 8 : r.stop + 8] for r in rows]
+        sums_ref[s, 0:1] = jnp.concatenate(norms, axis=1) * LOG2E
         parts = [packed_ref[2 * s + i, 2 * HEAD_DIM : PACKED].astype(jnp.float32) for i in range(2)]
         sums_ref[s, 1:2] = jnp.concatenate([part[0:1] + part[1:2] for part in parts], axis=1)
     for copy in copies:
@@ -162,13 +171,14 @@
         s, span = item
         first, last = lanes_ref[s, 0:1], lanes_ref[s, 1:2]
         lse, delta = sums_ref[s, 0:1], sums_ref[s, 1:2]
+        width = (last - first).astype(jnp.uint32)
         masks = []
         for j in range(GROUP):
             base = jnp.where(live & (span + j <= table_ref[QUERY + s]), (span + j) * SPAN, 8192)
-            masks.append((row >= first - base) & (row <= last - base))
+            masks.append((row + (base - first)).astype(jnp.uint32) <= width)
         allowed = jnp.concatenate(masks, axis=0)
         scores = dot(tile(item, 0), operand(s, 0), 1, 0)
-        probs = jnp.where(allowed, jnp.exp(scores * factor - lse), 0.0)
+        probs = jnp.where(allowed, jnp.exp2(scores * (factor * LOG2E) - lse), 0.0)
         dprob = dot(tile(item, 1), operand(s, HEAD_DIM), 1, 0)
         probs_ref[...] = probs.astype(jnp.bfloat16)
         dscore_ref[...] = (probs * (dprob - delta)).astype(jnp.bfloat16)
@@ -221,9 +231,9 @@
                 if core == 0:
                     keep_out[slab, t, 0], keep_out[slab, t, 1] = key, value
                 else:
-                    send[slab][t, 0], send[slab][t, 1] = key, value
+                    send_ref[slab, t, 0], send_ref[slab, t, 1] = key, value
             if core == 0:
-                leave(keep_out.at[slab], keep[slab], sems.at[13 + slab])
+                leave(keep_out.at[slab], keep_ref.at[slab], sems.at[13 + slab])
     for copy in leaving:
         copy.wait()
 
@@ -232,14 +242,14 @@
 HBM = pl.BlockSpec(memory_space=pltpu.HBM)
 
 
-def tiles(plan, bounds, packed, lse, mine, other):
+def tiles(plan, bounds, packed, mine, other):
     bf16, f32 = jnp.bfloat16, jnp.float32
-    parts = [jax.ShapeDtypeStruct((8, 2, HEAD_DIM, SPAN), bf16)] * 4
-    outs = pl.pallas_call(
+    sums = (4, 8, 2, HEAD_DIM, SPAN)
+    return pl.pallas_call(
         tiles_kernel,
-        out_shape=[pltpu.HBM((16, HEAD_DIM, 256), bf16)] + [pltpu.HBM((8, 2, HEAD_DIM, SPAN), bf16)] * 4 + parts,
-        in_specs=[HBM] * 2 + [VMEM] * 2 + [pl.BlockSpec(memory_space=pl.ANY)] * 10,
-        out_specs=[HBM] * 5 + [VMEM] * 4,
+        out_shape=[pltpu.HBM((16, HEAD_DIM, 256), bf16), pltpu.HBM(sums, bf16), jax.ShapeDtypeStruct(sums, bf16)],
+        in_specs=[HBM] * 2 + [VMEM] + [pl.BlockSpec(memory_space=pl.ANY)] * 10,
+        out_specs=[HBM, HBM, VMEM],
         scratch_shapes=[
             pltpu.SMEM((32, 2), jnp.int32),
             pltpu.SMEM((12,), jnp.int32),
@@ -256,8 +266,7 @@
         + [pltpu.SemaphoreType.DMA((17,))],
         compiler_params=pltpu.CompilerParams(vmem_limit_bytes=26 * MIB),
         name="tiles",
-    )(plan, bounds, packed, lse, *[part.reshape(-1, 2, 2, HALF, HEAD_DIM) for part in (*mine, *other)])
-    return outs[0], outs[1:5], outs[5:9]
+    )(plan, bounds, packed, *[part.reshape(-1, 2, 2, HALF, HEAD_DIM) for part in (*mine, *other)])
 
 
 def shift(array, axis, by):
@@ -279,7 +288,6 @@
 def shards(queries, keys, values, fwd_out, out_grad, log_norm, doc_bounds, span_plan, read_lists):
     bf16 = jnp.bfloat16
     f32 = jnp.float32
-    z = lax.axis_index("z")
 
     kv_out = pl.pallas_call(
         pack_kv_kernel,
@@ -290,21 +298,16 @@
     )(keys, values)
     block = exchange(kv_out.reshape(16, 2, HALF, HEAD_DIM))
 
+    norms = log_norm.reshape(4, HALF, 4, 4).transpose(2, 0, 3, 1).reshape(4, 4, 256)
     wide = pl.BlockSpec((HALF, 16 * HEAD_DIM), lambda y: (0, y))
     q_out = pl.pallas_call(
         pack_q_kernel,
         grid=(4,),
         out_shape=jax.ShapeDtypeStruct((4, 4, PACKED, 256), bf16),
-        in_specs=[wide, wide, wide],
+        in_specs=[wide, wide, wide, pl.BlockSpec((4, 4, 256), lambda y: (0, 0, 0))],
         out_specs=pl.BlockSpec((4, 1, PACKED, 256), lambda y: (0, y, 0, 0)),
         name="pack_q",
-    )(queries, out_grad, fwd_out)
-    norms = log_norm.reshape(2, 2, HALF, 4, 4).transpose(3, 0, 1, 4, 2).reshape(4, 2, LANES)
-    to = [lax.dynamic_index_in_dim(norms, (z + k) % 4, 0, keepdims=False) for k in range(4)]
-    lse = jnp.concatenate(
-        [to[0], shift(to[3], "z", -1), shift(to[2], "z", 2), shift(to[1], "z", 1)], axis=0
-    )
-    q_out, lse = lax.optimization_barrier((q_out, lse))
+    )(queries, out_grad, fwd_out, norms)
     packed = exchange(q_out.reshape(16, PACKED, 256))
 
     from_next = shift(block, "x", -1)
@@ -315,42 +318,46 @@
     plan, bounds = in_hbm(span_plan), in_hbm(doc_bounds)
     mine = [block, from_next, far_a, far_b, from_last]
     other = [swap(part) for part in mine]
-    dq, keep, send = tiles(plan, bounds, packed, lse, mine, other)
-
-    got = {k: in_hbm(swap(send[k])) for k in (2, 1, 3, 0)}
-    keep = [in_hbm(part) for part in keep]
-    half = [pl.BlockSpec((4, 2, HEAD_DIM, SPAN), lambda _, i=i: (i, 0, 0, 0)) for i in range(2)]
-    piece = jax.ShapeDtypeStruct((4, 2, HEAD_DIM, SPAN), bf16)
+    dq, keep, send = tiles(plan, bounds, packed, mine, other)
+
+    got = swap(send)
+
+    def block_of(slab, half):
+        return pl.BlockSpec((1, 4, 2, HEAD_DIM, SPAN), lambda _: (slab, half, 0, 0, 0))
+
+    piece = jax.ShapeDtypeStruct((1, 4, 2, HEAD_DIM, SPAN), bf16)
     via_next, via_last, last_b, next_a = pl.pallas_call(
         functools.partial(add_kernel, 2),
         grid=(1,),
         out_shape=[piece] * 4,
-        in_specs=[half[0]] * 2 + [half[1]] * 4 + [half[0]] * 2,
-        out_specs=[half[0]] * 4,
+        in_specs=[block_of(*place) for place in ((2, 0), (2, 1), (1, 1), (3, 0)) for _ in range(2)],
+        out_specs=[block_of(0, 0)] * 4,
         compiler_params=pltpu.CompilerParams(vmem_limit_bytes=8 * MIB),
         name="first_sums",
-    )(keep[2], got[2], keep[2], got[2], keep[1], got[1], keep[3], got[3])
+    )(*[keep, got] * 4)
     via_next, via_last = shift(via_next, "x", 1), shift(via_last, "x", -1)
     last_b, next_a = shift(last_b, "x", 1), shift(next_a, "x", -1)
     last_a, next_b = pl.pallas_call(
         functools.partial(add_kernel, 3),
         grid=(1,),
         out_shape=[piece] * 2,
-        in_specs=[half[0]] * 3 + [half[1]] * 2 + [half[0]],
-        out_specs=[half[0]] * 2,
+        in_specs=[block_of(1, 0)] * 2 + [block_of(0, 0)] + [block_of(3, 1)] * 2 + [block_of(0, 0)],
+        out_specs=[block_of(0, 0)] * 2,
         compiler_params=pltpu.CompilerParams(vmem_limit_bytes=6 * MIB),
         name="second_sums",
-    )(keep[1], got[1], via_next, keep[3], got[3], via_last)
+    )(keep, got, via_next, keep, got, via_last)
     last_a, next_b = shift(last_a, "x", 1), shift(next_b, "x", -1)
     dq_back = exchange(dq).reshape(4, 4, HEAD_DIM, 256)
+    slab = pl.BlockSpec((1, 8, 2, HEAD_DIM, SPAN), lambda _: (0, 0, 0, 0, 0))
     total = pl.pallas_call(
         final_kernel,
+        grid=(1,),
         out_shape=jax.ShapeDtypeStruct((16, 2, HALF, HEAD_DIM), bf16),
-        in_specs=[VMEM] * 6,
-        out_specs=VMEM,
-        compiler_params=pltpu.CompilerParams(vmem_limit_bytes=6 * MIB),
+        in_specs=[slab] * 2 + [block_of(0, 0)] * 4,
+        out_specs=pl.BlockSpec((16, 2, HALF, HEAD_DIM), lambda _: (0, 0, 0, 0)),
+        compiler_params=pltpu.CompilerParams(vmem_limit_bytes=8 * MIB),
         name="own_slab",
-    )(keep[0], got[0], last_a, last_b, next_a, next_b)
+    )(keep, got, last_a, last_b, next_a, next_b)
     total, dq_back = lax.optimization_barrier((total, dq_back))
     kv_back = exchange(total)
     grad_queries = pl.pallas_call(

time: 123 us -> 120 us (0.976)
  waiting for transfers between devices: 39.7 us -> 46.9 us
  starting transfers between devices: 46.4 us -> 39.3 us
  Pallas kernels: 30.2 us -> 28.5 us
    all_to_all x4, waiting for transfers between devices: 13.2 us -> 21.5 us  [exchange(): return lax.all_to_all(array, ('z', 'y'), 0, 0, tiled=True)]
    ppermute x13 -> x10, starting transfers between devices: 22.6 us -> 16.5 us  [shift(): return lax.ppermute(array, axis, [(i, (i + by) % 4) for i in range(4)])]
    ppermute x13 -> x10, waiting for transfers between devices: 26 us -> 23.5 us  [shift(): return lax.ppermute(array, axis, [(i, (i + by) % 4) for i in range(4)])]
    unnamed x13 -> x7, local copies, waits for them, and re-layouts: 3.27 us -> 1.52 us
    ppermute x9 -> x6, waiting for transfers between devices: 0.52 us -> 1.86 us  [swap(): return lax.ppermute(array, 'c', [(0, 1), (1, 0)])]
  transfers between devices with their start and end apart: 26 -> 20, of which waited for: 11 -> 14; matrix products, arithmetic and copies ran while one was open for 3% -> 3% of each run, Pallas kernels for 10% -> 9%
where the time goes in v4:
time: 120 us; the launch traced here: 119 us
  waiting for transfers between devices  46.9 us (39%)
  starting transfers between devices  39.3 us (33%)
  Pallas kernels  28.5 us (24%)
  local copies, waits for them, and re-layouts  4.01 us (3%)
    ppermute x10, waiting for transfers between devices, shift(): return lax.ppermute(array, axis, [(i, (i + by) % 4) for i in range(4)])  23.5 us
    all_to_all x4, starting transfers between devices, exchange(): return lax.all_to_all(array, ('z', 'y'), 0, 0, tiled=True)  22.2 us
    all_to_all x4, waiting for transfers between devices, exchange(): return lax.all_to_all(array, ('z', 'y'), 0, 0, tiled=True)  21.5 us
    ppermute x10, starting transfers between devices, shift(): return lax.ppermute(array, axis, [(i, (i + by) % 4) for i in range(4)])  16.5 us
    pallas_call x1, Pallas kernels, tiles(): pl.pallas_call(tiles_kernel, out_shape=[pltpu.HBM((16, HEAD_DIM, 256), bf...  15.3 us
    pallas_call x1, Pallas kernels, shards(): pl.pallas_call(pack_q_kernel, grid=(4,), out_shape=jax.ShapeDtypeStruct((...  4.71 us
  transfers between devices with their start and end apart: 20, of which 14 were waited for; matrix products, arithmetic and copies ran while one was open for 3% of the time, Pallas kernels for 9%

profile of v4, /device:TPU:0, one launch (start us, length us, event | category | flops | bytes accessed | tf_op | source)
XLA Modules:
  0.0 119.5 jit_solution(10424002468072329867)
XLA Ops:
  0.6 1.8 %pack_kv.1 = bf16[4,4,2,64,128]{4,3,2,1,0:T(8,128)(2,1)} custom-call(bf16[64,1024]{1,0:T(8,128)(2,1)} %keys_ref.1, bf16[64,1024]{1,0:T(8,128)(2,1)} %values_ref.1), custom_call_target="tpu_custom_call" | custom-call | tf_op jit(solution)/shard_map/pack_kv/pallas_call | solution.py:292
  2.5 8.1 %all-to-all-start.1 = ((bf16[16,2,64,128]{3,2,1,0:T(8,128)(2,1)}), bf16[16,2,64,128]{3,2,1,0:T(8,128)(2,1)S(1)}, u32[]{:S(2)}, u32[]{:S(2)}) async-start(bf16[16,2,64,128]{3,2,1,0:T(8,128)(2,1)} %bitcast.25), calls=%async_computation.1 | async-start | bytes 1048576 | tf_op jit(solution)/shard_map/all_to_all | solution.py:285
  12.1 4.7 %pack_q.1 = bf16[4,4,272,256]{3,2,1,0:T(8,128)(2,1)} custom-call(bf16[64,8192]{1,0:T(8,128)(2,1)} %queries_ref.1, bf16[64,8192]{1,0:T(8,128)(2,1)} %grad_ref.1, bf16[64,8192]{1,0:T(8,128)(2,1)} %fwd_ref.1, f32[4,4,256]{2,1,0:T(4,128)} %reshape.55.norms_ref), custom_call_target="tpu_custom_call" | custom-call | tf_op jit(solution)/shard_map/pack_q/pallas_call | solution.py:303
  16.8 5.3 %all-to-all-done.1 = bf16[16,2,64,128]{3,2,1,0:T(8,128)(2,1)S(1)} async-done(((bf16[16,2,64,128]{3,2,1,0:T(8,128)(2,1)}), bf16[16,2,64,128]{3,2,1,0:T(8,128)(2,1)S(1)}, u32[]{:S(2)}, u32[]{:S(2)}) %all-to-all-start.1) | async-done | bytes 524320 | tf_op jit(solution)/shard_map/all_to_all | solution.py:285
  22.1 3.9 %all-to-all-start = ((bf16[16,272,256]{2,1,0:T(8,128)(2,1)}), bf16[16,272,256]{2,1,0:T(8,128)(2,1)S(1)}, u32[]{:S(2)}, u32[]{:S(2)}) async-start(bf16[16,272,256]{2,1,0:T(8,128)(2,1)} %bitcast.24), calls=%async_computation | async-start | bytes 4456448 | tf_op jit(solution)/shard_map/all_to_all | solution.py:285
  26.0 1.6 %collective-permute-start.2 = (bf16[16,2,64,128]{3,2,1,0:T(8,128)(2,1)S(1)}, bf16[16,2,64,128]{3,2,1,0:T(8,128)(2,1)S(1)}, u32[]{:S(2)}, u32[]{:S(2)}) collective-permute-start(bf16[16,2,64,128]{3,2,1,0:T(8,128)(2,1)S(1)} %all-to-all-done.1), channel_id=1, source_target_pairs={{0,8},{8,16},{16,24},{24,0},{1,9},{9,17},{17,25},{25,1},{2,10},{10... | collective-permute-start | bytes 1572872 | tf_op jit(solution)/shard_map/ppermute | solution.py:273
  27.6 1.7 %collective-permute-start = (bf16[16,2,64,128]{3,2,1,0:T(8,128)(2,1)S(1)}, bf16[16,2,64,128]{3,2,1,0:T(8,128)(2,1)}, u32[]{:S(2)}, u32[]{:S(2)}) collective-permute-start(bf16[16,2,64,128]{3,2,1,0:T(8,128)(2,1)S(1)} %all-to-all-done.1), channel_id=1, source_target_pairs={{0,24},{8,0},{16,8},{24,16},{1,25},{9,1},{17,9},{25,17},{2,26},{10... | collective-permute-start | bytes 1572872 | tf_op jit(solution)/shard_map/ppermute | solution.py:273
  29.3 10.3 %collective-permute-done.2 = bf16[16,2,64,128]{3,2,1,0:T(8,128)(2,1)S(1)} collective-permute-done((bf16[16,2,64,128]{3,2,1,0:T(8,128)(2,1)S(1)}, bf16[16,2,64,128]{3,2,1,0:T(8,128)(2,1)S(1)}, u32[]{:S(2)}, u32[]{:S(2)}) %collective-permute-start.2) | collective-permute-done | bytes 524320 | tf_op jit(solution)/shard_map/ppermute | solution.py:273
  41.0 3.0 %collective-permute-start.1 = (bf16[8,2,64,128]{3,2,1,0:T(8,128)(2,1)S(1)}, bf16[8,2,64,128]{3,2,1,0:T(8,128)(2,1)}, u32[]{:S(2)}, u32[]{:S(2)}) collective-permute-start(bf16[8,2,64,128]{3,2,1,0:T(8,128)(2,1)S(1)} %slice.8), channel_id=1, source_target_pairs={{0,24},{8,0},{16,8},{24,16},{1,25},{9,1},{17,9},{25,17},{2,26},{10... | collective-permute-start | bytes 786440 | tf_op jit(solution)/shard_map/ppermute | solution.py:273
  44.5 2.8 %collective-permute-done.3 = bf16[8,2,64,128]{3,2,1,0:T(8,128)(2,1)S(1)} collective-permute-done((bf16[8,2,64,128]{3,2,1,0:T(8,128)(2,1)S(1)}, bf16[8,2,64,128]{3,2,1,0:T(8,128)(2,1)S(1)}, u32[]{:S(2)}, u32[]{:S(2)}) %collective-permute-start.3) | collective-permute-done | bytes 262176 | tf_op jit(solution)/shard_map/ppermute | solution.py:273
  49.8 7.4 %all-to-all-done.packed_ref = bf16[16,272,256]{2,1,0:T(8,128)(2,1)S(1)} async-done(((bf16[16,272,256]{2,1,0:T(8,128)(2,1)}), bf16[16,272,256]{2,1,0:T(8,128)(2,1)S(1)}, u32[]{:S(2)}, u32[]{:S(2)}) %all-to-all-start) | async-done | bytes 2228256 | tf_op jit(solution)/shard_map/all_to_all | solution.py:285
  57.2 15.3 %tiles.1 = (bf16[16,128,256]{2,1,0:T(8,128)(2,1)}, bf16[4,8,2,128,128]{4,3,2,1,0:T(8,128)(2,1)}, bf16[4,8,2,128,128]{4,3,2,1,0:T(8,128)(2,1)}) custom-call(s32[32,2]{1,0:T(8,128)} %copy.12.plan_in, s32[12]{0:T(128)} %bounds_in.1, bf16[16,272,256]{2,1,0:T(8,128)(2,1)S(1)} %all-to-all-done.packed_ref, bf16[8,2,2,64,128]{4,3,2,1,0:T(8,128)(2,1)S(1)} %bitcast.20, ...), custom_call_target="tpu_custom_call" | custom-call | tf_op jit(solution)/shard_map/tiles/pallas_call | solution.py:248
  72.6 3.8 %all-to-all-start.2 = ((bf16[16,128,256]{2,1,0:T(8,128)(2,1)}), bf16[16,128,256]{2,1,0:T(8,128)(2,1)S(1)}, u32[]{:S(2)}, u32[]{:S(2)}) async-start(bf16[16,128,256]{2,1,0:T(8,128)(2,1)} %get-tuple-element.24), calls=%async_computation.2 | async-start | bytes 2097152 | tf_op jit(solution)/shard_map/all_to_all | solution.py:285
  77.1 1.4 %first_sums.1 = (bf16[1,4,2,128,128]{4,3,2,1,0:T(8,128)(2,1)S(1)}, bf16[1,4,2,128,128]{4,3,2,1,0:T(8,128)(2,1)S(1)}, bf16[1,4,2,128,128]{4,3,2,1,0:T(8,128)(2,1)S(1)}, bf16[1,4,2,128,128]{4,3,2,1,0:T(8,128)(2,1)S(1)}) custom-call(bf16[4,8,2,128,128]{4,3,2,1,0:T(8,128)(2,1)S(1)} %copy-done, ...), custom_call_target="tpu_custom_call" | custom-call | tf_op jit(solution)/shard_map/first_sums/pallas_call | solution.py:329
  78.5 1.6 %collective-permute-start.10 = (bf16[1,4,2,128,128]{4,3,2,1,0:T(8,128)(2,1)S(1)}, bf16[1,4,2,128,128]{4,3,2,1,0:T(8,128)(2,1)S(1)}, u32[]{:S(2)}, u32[]{:S(2)}) collective-permute-start(bf16[1,4,2,128,128]{4,3,2,1,0:T(8,128)(2,1)S(1)} %get-tuple-element.18), channel_id=1, source_target_pairs={{0,8},{8,16},{16,24},{24,0},{1,9},{9,17},{17,25},{25,1},{2,10},{10... | collective-permute-start | bytes 786440 | tf_op jit(solution)/shard_map/ppermute | solution.py:273
  80.1 1.7 %collective-permute-start.11 = (bf16[1,4,2,128,128]{4,3,2,1,0:T(8,128)(2,1)S(1)}, bf16[1,4,2,128,128]{4,3,2,1,0:T(8,128)(2,1)S(1)}, u32[]{:S(2)}, u32[]{:S(2)}) collective-permute-start(bf16[1,4,2,128,128]{4,3,2,1,0:T(8,128)(2,1)S(1)} %get-tuple-element.19), channel_id=1, source_target_pairs={{0,24},{8,0},{16,8},{24,16},{1,25},{9,1},{17,9},{25,17},{2,26},{10... | collective-permute-start | bytes 786440 | tf_op jit(solution)/shard_map/ppermute | solution.py:273
  82.1 2.9 %collective-permute-start.14 = (bf16[1,4,2,128,128]{4,3,2,1,0:T(8,128)(2,1)S(1)}, bf16[1,4,2,128,128]{4,3,2,1,0:T(8,128)(2,1)S(1)}, u32[]{:S(2)}, u32[]{:S(2)}) collective-permute-start(bf16[1,4,2,128,128]{4,3,2,1,0:T(8,128)(2,1)S(1)} %get-tuple-element.22), channel_id=1, source_target_pairs={{0,24},{8,0},{16,8},{24,16},{1,25},{9,1},{17,9},{25,17},{2,26},{10... | collective-permute-start | bytes 786440 | tf_op jit(solution)/shard_map/ppermute | solution.py:273
  85.1 3.9 %collective-permute-done.10.refs_2_ = bf16[1,4,2,128,128]{4,3,2,1,0:T(8,128)(2,1)S(1)} collective-permute-done((bf16[1,4,2,128,128]{4,3,2,1,0:T(8,128)(2,1)S(1)}, bf16[1,4,2,128,128]{4,3,2,1,0:T(8,128)(2,1)S(1)}, u32[]{:S(2)}, u32[]{:S(2)}) %collective-permute-start.10) | collective-permute-done | bytes 262176 | tf_op jit(solution)/shard_map/ppermute | solution.py:273
  91.2 2.6 %collective-permute-start.15 = (bf16[1,4,2,128,128]{4,3,2,1,0:T(8,128)(2,1)S(1)}, bf16[1,4,2,128,128]{4,3,2,1,0:T(8,128)(2,1)S(1)}, u32[]{:S(2)}, u32[]{:S(2)}) collective-permute-start(bf16[1,4,2,128,128]{4,3,2,1,0:T(8,128)(2,1)S(1)} %get-tuple-element.23), channel_id=1, source_target_pairs={{0,24},{8,0},{16,8},{24,16},{1,25},{9,1},{17,9},{25,17},{2,26},{10... | collective-permute-start | bytes 786440 | tf_op jit(solution)/shard_map/ppermute | solution.py:273
  94.9 4.5 %collective-permute-done.12.last_a_ref = bf16[1,4,2,128,128]{4,3,2,1,0:T(8,128)(2,1)S(1)} collective-permute-done((bf16[1,4,2,128,128]{4,3,2,1,0:T(8,128)(2,1)S(1)}, bf16[1,4,2,128,128]{4,3,2,1,0:T(8,128)(2,1)S(1)}, u32[]{:S(2)}, u32[]{:S(2)}) %collective-permute-start.12) | collective-permute-done | bytes 262176 | tf_op jit(solution)/shard_map/ppermute | solution.py:273
  99.4 1.4 %own_slab.1 = bf16[16,2,64,128]{3,2,1,0:T(8,128)(2,1)S(1)} custom-call(bf16[4,8,2,128,128]{4,3,2,1,0:T(8,128)(2,1)S(1)} %copy-done, bf16[4,8,2,128,128]{4,3,2,1,0:T(8,128)(2,1)} %collective-permute-done.9.refs_1_.refs_3_.refs_5_.refs_7_.refs_4_.got_ref, bf16[1,4,2,128,128]{4,3,2,1,0:T(8,128)(2,1)S(1)} %collective-permute-done.12.last_a_ref, ...), custom_call_target="tpu_custom_call" | custom-call | tf_op jit(solution)/shard_map/own_slab/pallas_call | solution.py:352
  101.6 6.4 %all-to-all-start.3 = ((bf16[16,2,64,128]{3,2,1,0:T(8,128)(2,1)}), bf16[16,2,64,128]{3,2,1,0:T(8,128)(2,1)S(1)}, u32[]{:S(2)}, u32[]{:S(2)}) async-start(bf16[16,2,64,128]{3,2,1,0:T(8,128)(2,1)} %copy-done.1), calls=%async_computation.3 | async-start | bytes 1048576 | tf_op jit(solution)/shard_map/all_to_all | solution.py:285
  108.1 1.9 %unpack_q.1 = bf16[64,8192]{1,0:T(8,128)(2,1)} custom-call(bf16[4,4,128,256]{3,2,1,0:T(8,128)(2,1)S(1)} %bitcast.19), custom_call_target="tpu_custom_call" | custom-call | tf_op jit(solution)/shard_map/unpack_q/pallas_call | solution.py:363
  109.9 8.8 %all-to-all-done.3 = bf16[16,2,64,128]{3,2,1,0:T(8,128)(2,1)S(1)} async-done(((bf16[16,2,64,128]{3,2,1,0:T(8,128)(2,1)}), bf16[16,2,64,128]{3,2,1,0:T(8,128)(2,1)S(1)}, u32[]{:S(2)}, u32[]{:S(2)}) %all-to-all-start.3) | async-done | bytes 524320 | tf_op jit(solution)/shard_map/all_to_all | solution.py:285
  (36 shorter events, 11.9 us)
Async XLA Ops:
  2.5 19.7 %all-to-all-start.1 = ((bf16[16,2,64,128]{3,2,1,0:T(8,128)(2,1)}), bf16[16,2,64,128]{3,2,1,0:T(8,128)(2,1)S(1)}, u32[]{:S(2)}, u32[]{:S(2)}) async-start(bf16[16,2,64,128]{3,2,1,0:T(8,128)(2,1)} %bitcast.25), calls=%async_computation.1 | async-start | bytes 1048576 | tf_op jit(solution)/shard_map/all_to_all | solution.py:285
  22.1 25.8 %copy-start.2 = (s32[32,2]{0,1:T(2,128)S(1)}, s32[32,2]{0,1:T(2,128)}, u32[]{:S(2)}) copy-start(s32[32,2]{0,1:T(2,128)} %param.16) | copy-start | bytes 772
  22.1 35.1 %all-to-all-start = ((bf16[16,272,256]{2,1,0:T(8,128)(2,1)}), bf16[16,272,256]{2,1,0:T(8,128)(2,1)S(1)}, u32[]{:S(2)}, u32[]{:S(2)}) async-start(bf16[16,272,256]{2,1,0:T(8,128)(2,1)} %bitcast.24), calls=%async_computation | async-start | bytes 4456448 | tf_op jit(solution)/shard_map/all_to_all | solution.py:285
  26.0 13.6 %collective-permute-start.2 = (bf16[16,2,64,128]{3,2,1,0:T(8,128)(2,1)S(1)}, bf16[16,2,64,128]{3,2,1,0:T(8,128)(2,1)S(1)}, u32[]{:S(2)}, u32[]{:S(2)}) collective-permute-start(bf16[16,2,64,128]{3,2,1,0:T(8,128)(2,1)S(1)} %all-to-all-done.1), channel_id=1, source_target_pairs={{0,8},{8,16},{16,24},{24,0},{1,9},{9,17},{17,25},{25,1},{2,10},{10... | collective-permute-start | bytes 1572872 | tf_op jit(solution)/shard_map/ppermute | solution.py:273
  27.6 12.5 %collective-permute-start = (bf16[16,2,64,128]{3,2,1,0:T(8,128)(2,1)S(1)}, bf16[16,2,64,128]{3,2,1,0:T(8,128)(2,1)}, u32[]{:S(2)}, u32[]{:S(2)}) collective-permute-start(bf16[16,2,64,128]{3,2,1,0:T(8,128)(2,1)S(1)} %all-to-all-done.1), channel_id=1, source_target_pairs={{0,24},{8,0},{16,8},{24,16},{1,25},{9,1},{17,9},{25,17},{2,26},{10... | collective-permute-start | bytes 1572872 | tf_op jit(solution)/shard_map/ppermute | solution.py:273
  29.3 19.3 %collective-permute-start.4 = (bf16[16,2,64,128]{3,2,1,0:T(8,128)(2,1)S(1)}, bf16[16,2,64,128]{3,2,1,0:T(8,128)(2,1)}, u32[]{:S(2)}, u32[]{:S(2)}) collective-permute-start(bf16[16,2,64,128]{3,2,1,0:T(8,128)(2,1)S(1)} %all-to-all-done.1), channel_id=1, source_target_pairs={{0,4},{4,0},{1,5},{5,1},{2,6},{6,2},{3,7},{7,3},{8,12},{12,8},{9,1... | collective-permute-start | bytes 1572872 | tf_op jit(solution)/shard_map/ppermute | solution.py:281
  39.7 7.7 %collective-permute-start.3 = (bf16[8,2,64,128]{3,2,1,0:T(8,128)(2,1)S(1)}, bf16[8,2,64,128]{3,2,1,0:T(8,128)(2,1)S(1)}, u32[]{:S(2)}, u32[]{:S(2)}) collective-permute-start(bf16[8,2,64,128]{3,2,1,0:T(8,128)(2,1)S(1)} %slice.9), channel_id=1, source_target_pairs={{0,8},{8,16},{16,24},{24,0},{1,9},{9,17},{17,25},{25,1},{2,10},{10... | collective-permute-start | bytes 786440 | tf_op jit(solution)/shard_map/ppermute | solution.py:273
  41.0 6.9 %collective-permute-start.1 = (bf16[8,2,64,128]{3,2,1,0:T(8,128)(2,1)S(1)}, bf16[8,2,64,128]{3,2,1,0:T(8,128)(2,1)}, u32[]{:S(2)}, u32[]{:S(2)}) collective-permute-start(bf16[8,2,64,128]{3,2,1,0:T(8,128)(2,1)S(1)} %slice.8), channel_id=1, source_target_pairs={{0,24},{8,0},{16,8},{24,16},{1,25},{9,1},{17,9},{25,17},{2,26},{10... | collective-permute-start | bytes 786440 | tf_op jit(solution)/shard_map/ppermute | solution.py:273
  44.0 5.0 %collective-permute-start.8 = (bf16[16,2,64,128]{3,2,1,0:T(8,128)(2,1)S(1)}, bf16[16,2,64,128]{3,2,1,0:T(8,128)(2,1)}, u32[]{:S(2)}, u32[]{:S(2)}) collective-permute-start(bf16[16,2,64,128]{3,2,1,0:T(8,128)(2,1)S(1)} %collective-permute-done.2), channel_id=1, source_target_pairs={{0,4},{4,0},{1,5},{5,1},{2,6},{6,2},{3,7},{7,3},{8,12},{12,8},{9,1... | collective-permute-start | bytes 1572872 | tf_op jit(solution)/shard_map/ppermute | solution.py:281
  44.0 5.8 %collective-permute-start.5 = (bf16[16,2,64,128]{3,2,1,0:T(8,128)(2,1)}, bf16[16,2,64,128]{3,2,1,0:T(8,128)(2,1)}, u32[]{:S(2)}, u32[]{:S(2)}) collective-permute-start(bf16[16,2,64,128]{3,2,1,0:T(8,128)(2,1)} %collective-permute-done), channel_id=1, source_target_pairs={{0,4},{4,0},{1,5},{5,1},{2,6},{6,2},{3,7},{7,3},{8,12},{12,8},{9,1... | collective-permute-start | bytes 1572872 | tf_op jit(solution)/shard_map/ppermute | solution.py:281
  47.3 1.7 %collective-permute-start.7 = (bf16[8,2,64,128]{3,2,1,0:T(8,128)(2,1)S(1)}, bf16[8,2,64,128]{3,2,1,0:T(8,128)(2,1)}, u32[]{:S(2)}, u32[]{:S(2)}) collective-permute-start(bf16[8,2,64,128]{3,2,1,0:T(8,128)(2,1)S(1)} %collective-permute-done.3), channel_id=1, source_target_pairs={{0,4},{4,0},{1,5},{5,1},{2,6},{6,2},{3,7},{7,3},{8,12},{12,8},{9,1... | collective-permute-start | bytes 786440 | tf_op jit(solution)/shard_map/ppermute | solution.py:281
  47.9 1.9 %collective-permute-start.6 = (bf16[8,2,64,128]{3,2,1,0:T(8,128)(2,1)}, bf16[8,2,64,128]{3,2,1,0:T(8,128)(2,1)}, u32[]{:S(2)}, u32[]{:S(2)}) collective-permute-start(bf16[8,2,64,128]{3,2,1,0:T(8,128)(2,1)} %collective-permute-done.1), channel_id=1, source_target_pairs={{0,4},{4,0},{1,5},{5,1},{2,6},{6,2},{3,7},{7,3},{8,12},{12,8},{9,1... | collective-permute-start | bytes 786440 | tf_op jit(solution)/shard_map/ppermute | solution.py:281
  72.5 4.6 %copy-start = (bf16[4,8,2,128,128]{4,3,2,1,0:T(8,128)(2,1)S(1)}, bf16[4,8,2,128,128]{4,3,2,1,0:T(8,128)(2,1)}, u32[]{:S(2)}) copy-start(bf16[4,8,2,128,128]{4,3,2,1,0:T(8,128)(2,1)} %get-tuple-element.16.refs_0_.refs_2_.refs_4_.refs_6_.refs_3_.keep_ref) | copy-start | bytes 6291460
  72.5 4.6 %collective-permute-start.9 = (bf16[4,8,2,128,128]{4,3,2,1,0:T(8,128)(2,1)}, bf16[4,8,2,128,128]{4,3,2,1,0:T(8,128)(2,1)}, u32[]{:S(2)}, u32[]{:S(2)}) collective-permute-start(bf16[4,8,2,128,128]{4,3,2,1,0:T(8,128)(2,1)} %get-tuple-element.17), channel_id=1, source_target_pairs={{0,4},{4,0},{1,5},{5,1},{2,6},{6,2},{3,7},{7,3},{8,12},{12,8},{9,1... | collective-permute-start | bytes 6291464 | tf_op jit(solution)/shard_map/ppermute | solution.py:281
  72.6 29.0 %all-to-all-start.2 = ((bf16[16,128,256]{2,1,0:T(8,128)(2,1)}), bf16[16,128,256]{2,1,0:T(8,128)(2,1)S(1)}, u32[]{:S(2)}, u32[]{:S(2)}) async-start(bf16[16,128,256]{2,1,0:T(8,128)(2,1)} %get-tuple-element.24), calls=%async_computation.2 | async-start | bytes 2097152 | tf_op jit(solution)/shard_map/all_to_all | solution.py:285
  78.5 10.4 %collective-permute-start.10 = (bf16[1,4,2,128,128]{4,3,2,1,0:T(8,128)(2,1)S(1)}, bf16[1,4,2,128,128]{4,3,2,1,0:T(8,128)(2,1)S(1)}, u32[]{:S(2)}, u32[]{:S(2)}) collective-permute-start(bf16[1,4,2,128,128]{4,3,2,1,0:T(8,128)(2,1)S(1)} %get-tuple-element.18), channel_id=1, source_target_pairs={{0,8},{8,16},{16,24},{24,0},{1,9},{9,17},{17,25},{25,1},{2,10},{10... | collective-permute-start | bytes 786440 | tf_op jit(solution)/shard_map/ppermute | solution.py:273
  80.1 9.2 %collective-permute-start.11 = (bf16[1,4,2,128,128]{4,3,2,1,0:T(8,128)(2,1)S(1)}, bf16[1,4,2,128,128]{4,3,2,1,0:T(8,128)(2,1)S(1)}, u32[]{:S(2)}, u32[]{:S(2)}) collective-permute-start(bf16[1,4,2,128,128]{4,3,2,1,0:T(8,128)(2,1)S(1)} %get-tuple-element.19), channel_id=1, source_target_pairs={{0,24},{8,0},{16,8},{24,16},{1,25},{9,1},{17,9},{25,17},{2,26},{10... | collective-permute-start | bytes 786440 | tf_op jit(solution)/shard_map/ppermute | solution.py:273
  81.8 12.7 %collective-permute-start.13 = (bf16[1,4,2,128,128]{4,3,2,1,0:T(8,128)(2,1)S(1)}, bf16[1,4,2,128,128]{4,3,2,1,0:T(8,128)(2,1)S(1)}, u32[]{:S(2)}, u32[]{:S(2)}) collective-permute-start(bf16[1,4,2,128,128]{4,3,2,1,0:T(8,128)(2,1)S(1)} %get-tuple-element.21), channel_id=1, source_target_pairs={{0,8},{8,16},{16,24},{24,0},{1,9},{9,17},{17,25},{25,1},{2,10},{10... | collective-permute-start | bytes 786440 | tf_op jit(solution)/shard_map/ppermute | solution.py:273
  82.1 12.8 %collective-permute-start.14 = (bf16[1,4,2,128,128]{4,3,2,1,0:T(8,128)(2,1)S(1)}, bf16[1,4,2,128,128]{4,3,2,1,0:T(8,128)(2,1)S(1)}, u32[]{:S(2)}, u32[]{:S(2)}) collective-permute-start(bf16[1,4,2,128,128]{4,3,2,1,0:T(8,128)(2,1)S(1)} %get-tuple-element.22), channel_id=1, source_target_pairs={{0,24},{8,0},{16,8},{24,16},{1,25},{9,1},{17,9},{25,17},{2,26},{10... | collective-permute-start | bytes 786440 | tf_op jit(solution)/shard_map/ppermute | solution.py:273
  90.5 8.9 %collective-permute-start.12 = (bf16[1,4,2,128,128]{4,3,2,1,0:T(8,128)(2,1)S(1)}, bf16[1,4,2,128,128]{4,3,2,1,0:T(8,128)(2,1)S(1)}, u32[]{:S(2)}, u32[]{:S(2)}) collective-permute-start(bf16[1,4,2,128,128]{4,3,2,1,0:T(8,128)(2,1)S(1)} %get-tuple-element.20), channel_id=1, source_target_pairs={{0,8},{8,16},{16,24},{24,0},{1,9},{9,17},{17,25},{25,1},{2,10},{10... | collective-permute-start | bytes 786440 | tf_op jit(solution)/shard_map/ppermute | solution.py:273
  91.2 8.2 %collective-permute-start.15 = (bf16[1,4,2,128,128]{4,3,2,1,0:T(8,128)(2,1)S(1)}, bf16[1,4,2,128,128]{4,3,2,1,0:T(8,128)(2,1)S(1)}, u32[]{:S(2)}, u32[]{:S(2)}) collective-permute-start(bf16[1,4,2,128,128]{4,3,2,1,0:T(8,128)(2,1)S(1)} %get-tuple-element.23), channel_id=1, source_target_pairs={{0,24},{8,0},{16,8},{24,16},{1,25},{9,1},{17,9},{25,17},{2,26},{10... | collective-permute-start | bytes 786440 | tf_op jit(solution)/shard_map/ppermute | solution.py:273
  100.8 0.8 copy-start.1
  101.6 17.1 %all-to-all-start.3 = ((bf16[16,2,64,128]{3,2,1,0:T(8,128)(2,1)}), bf16[16,2,64,128]{3,2,1,0:T(8,128)(2,1)S(1)}, u32[]{:S(2)}, u32[]{:S(2)}) async-start(bf16[16,2,64,128]{3,2,1,0:T(8,128)(2,1)} %copy-done.1), calls=%async_computation.3 | async-start | bytes 1048576 | tf_op jit(solution)/shard_map/all_to_all | solution.py:285

commit v5 on v4

--- a/solution.py
+++ b/solution.py
@@ -25,8 +25,8 @@
     for z in range(4):
         for y in range(4):
             cols = slice((2 * y + z // 2) * HEAD_DIM, (2 * y + z // 2 + 1) * HEAD_DIM)
-            out_ref[z, y, 0] = keys_ref[:, cols]
-            out_ref[z, y, 1] = values_ref[:, cols]
+            out_ref[y, z, 0] = keys_ref[:, cols]
+            out_ref[y, z, 1] = values_ref[:, cols]
 
 
 def pack_q_kernel(queries_ref, grad_ref, fwd_ref, norms_ref, out_ref):
@@ -39,8 +39,8 @@
             query = jnp.concatenate([queries_ref[:, col] for col in cols], axis=0)
             grad = jnp.concatenate([grad_ref[:, col] for col in cols], axis=0)
             fwd = jnp.concatenate([fwd_ref[:, col] for col in cols], axis=0)
-            out_ref[z, 0, 0:HEAD_DIM, lanes] = jnp.transpose(query)
-            out_ref[z, 0, HEAD_DIM : 2 * HEAD_DIM, lanes] = jnp.transpose(grad)
+            out_ref[0, z, 0:HEAD_DIM, lanes] = jnp.transpose(query)
+            out_ref[0, z, HEAD_DIM : 2 * HEAD_DIM, lanes] = jnp.transpose(grad)
             product = grad.astype(jnp.float32) * fwd.astype(jnp.float32)
             high = product.astype(jnp.bfloat16)
             low = (product - high.astype(jnp.float32)).astype(jnp.bfloat16)
@@ -51,13 +51,13 @@
                 pieces.append(rest.astype(jnp.bfloat16).astype(jnp.float32))
                 rest = rest - pieces[-1]
             tail = jnp.concatenate([high[0:1], (delta - high)[1:2], *pieces, high[0:2]], axis=0)
-            out_ref[z, 0, 2 * HEAD_DIM : PACKED, lanes] = tail.astype(jnp.bfloat16)
+            out_ref[0, z, 2 * HEAD_DIM : PACKED, lanes] = tail.astype(jnp.bfloat16)
 
 
 def unpack_q_kernel(in_ref, out_ref):
     for z in range(4):
         for pair in range(2):
-            part = jnp.transpose(in_ref[z, 0, :, pair * HEAD_DIM : (pair + 1) * HEAD_DIM])
+            part = jnp.transpose(in_ref[0, z, :, pair * HEAD_DIM : (pair + 1) * HEAD_DIM])
             for i in range(2):
                 head = z * 4 + 2 * pair + i
                 out_ref[:, head * HEAD_DIM : (head + 1) * HEAD_DIM] = part[i * HALF : (i + 1) * HALF]
@@ -80,8 +80,9 @@
             total = keep_ref[0, t, i].astype(jnp.float32) + got_ref[0, t, i].astype(jnp.float32)
             total = total + last_ref[0, t % 4, i].astype(jnp.float32) + next_ref[0, t % 4, i].astype(jnp.float32)
             rows = jnp.transpose(total).astype(jnp.bfloat16)
-            out_ref[2 * t, i] = rows[:HALF]
-            out_ref[2 * t + 1, i] = rows[HALF:]
+            first = t // 4 * 8 + t % 4
+            out_ref[first, i] = rows[:HALF]
+            out_ref[first + 4, i] = rows[HALF:]
 
 
 def unpack_kv_kernel(in_ref, keys_ref, values_ref):
@@ -89,7 +90,7 @@
         cols = slice(g * HEAD_DIM, (g + 1) * HEAD_DIM)
         y, z = g // 2, 2 * (g % 2)
         for i, out_ref in ((0, keys_ref), (1, values_ref)):
-            total = in_ref[z, y, i].astype(jnp.float32) + in_ref[z + 1, y, i].astype(jnp.float32)
+            total = in_ref[y, z, i].astype(jnp.float32) + in_ref[y, z + 1, i].astype(jnp.float32)
             out_ref[:, cols] = total.astype(jnp.bfloat16)
 
 
@@ -113,7 +114,7 @@
     copies = []
     for i, (slab, tile, count) in enumerate(PIECES):
         for core, sources in enumerate((mine, other)):
-            rows = pl.ds(slab * 16 + core * 8 + tile, count)
+            rows = pl.ds((slab * 16 + core * 8 + tile) // 4, count // 4)
             copies.append(pltpu.make_async_copy(sources[i], kv_ref.at[rows], sems.at[2 * i + core]))
     for copy in copies:
         copy.start()
@@ -127,7 +128,7 @@
     slabs = [((i - x) & 3) * 16 for i in range(4)]
     cores = [c * 8, (1 - c) * 8]
     for slot in range(64):
-        place = slabs[slot // 4 % 4] + cores[slot // 2 % 2] + slot // 16 * 2 + slot % 2
+        place = slabs[slot // 4 % 4] + cores[slot // 2 % 2] + slot % 2 * 4 + slot // 16
         table_ref[plan_ref[slot // 2, slot % 2]] = place
     row = lax.broadcasted_iota(jnp.int32, (SPAN, LANES), 0)
     lane = lax.broadcasted_iota(jnp.int32, (1, LANES), 1)
@@ -148,24 +149,25 @@
         steps = steps + lax.shift_right_logical(span - begin + GROUP, 1)
         lanes_ref[s, 0:1] = first
         lanes_ref[s, 1:2] = last
-        norms = packed_ref[s // 2 * 4 + y, 2 * HEAD_DIM : PACKED].astype(jnp.float32)
+        norms = packed_ref[y * 4 + s // 2, 2 * HEAD_DIM : PACKED].astype(jnp.float32)
         rows = [slice(2 + s % 2 * 2 + i, 3 + s % 2 * 2 + i) for i in range(2)]
         norms = [norms[r] + norms[r.start + 4 : r.stop + 4] + norms[r.start + 8 : r.stop + 8] for r in rows]
         sums_ref[s, 0:1] = jnp.concatenate(norms, axis=1) * LOG2E
-        parts = [packed_ref[2 * s + i, 2 * HEAD_DIM : PACKED].astype(jnp.float32) for i in range(2)]
+        parts = [packed_ref[(s % 2 * 2 + i) * 4 + s // 2, 2 * HEAD_DIM : PACKED].astype(jnp.float32) for i in range(2)]
         sums_ref[s, 1:2] = jnp.concatenate([part[0:1] + part[1:2] for part in parts], axis=1)
     for copy in copies:
         copy.wait()
 
     def operand(s, start):
-        return jnp.concatenate([packed_ref[2 * s + i, start : start + HEAD_DIM] for i in range(2)], axis=1)
+        first = (s & 1) * 8 + lax.shift_right_logical(s, 1)
+        return jnp.concatenate([packed_ref[first + 4 * i, start : start + HEAD_DIM] for i in range(2)], axis=1)
 
     def tiles_of(item):
         s, span = item
         return [table_ref[jnp.minimum(span + j, table_ref[QUERY + s])] for j in range(GROUP)]
 
     def tile(item, i):
-        return jnp.concatenate([kv_ref[t, :, i].reshape(SPAN, HEAD_DIM) for t in tiles_of(item)], axis=0)
+        return jnp.concatenate([kv_ref[lax.shift_right_logical(t, 2), :, t & 3, i].reshape(SPAN, HEAD_DIM) for t in tiles_of(item)], axis=0)
 
     def scores_stage(item, live, probs_ref, dscore_ref):
         s, span = item
@@ -220,7 +222,7 @@
 
     for i in range(16):
         lanes = slice((i % 2) * 256, (i % 2) * 256 + 256)
-        dq_out[i] = (dq_sum[i // 2, :, lanes] * factor).astype(jnp.bfloat16)
+        dq_out[(i // 2 % 2 * 2 + i % 2) * 4 + i // 4] = (dq_sum[i // 2, :, lanes] * factor).astype(jnp.bfloat16)
     leave(dq_out, dq_ref, sems.at[12])
     for core in range(2):
         for slab in (2, 1, 3, 0):
@@ -254,7 +256,7 @@
             pltpu.SMEM((32, 2), jnp.int32),
             pltpu.SMEM((12,), jnp.int32),
             pltpu.SMEM((TABLE,), jnp.int32),
-            pltpu.VMEM((64, 2, 2, HALF, HEAD_DIM), bf16),
+            pltpu.VMEM((16, 2, 4, 2, HALF, HEAD_DIM), bf16),
             pltpu.VMEM((64, 2, HEAD_DIM, SPAN), f32),
             pltpu.VMEM((8, HEAD_DIM, LANES), f32),
             pltpu.VMEM((16, HEAD_DIM, 256), bf16),
@@ -266,7 +268,7 @@
         + [pltpu.SemaphoreType.DMA((17,))],
         compiler_params=pltpu.CompilerParams(vmem_limit_bytes=26 * MIB),
         name="tiles",
-    )(plan, bounds, packed, *[part.reshape(-1, 2, 2, HALF, HEAD_DIM) for part in (*mine, *other)])
+    )(plan, bounds, packed, *[part.reshape(-1, 2, 4, 2, HALF, HEAD_DIM) for part in (*mine, *other)])
 
 
 def shift(array, axis, by):
@@ -282,7 +284,7 @@
 
 
 def exchange(array):
-    return lax.all_to_all(array, ("z", "y"), 0, 0, tiled=True)
+    return lax.all_to_all(array, ("y", "z"), 0, 0, tiled=True)
 
 
 def shards(queries, keys, values, fwd_out, out_grad, log_norm, doc_bounds, span_plan, read_lists):
@@ -305,7 +307,7 @@
         grid=(4,),
         out_shape=jax.ShapeDtypeStruct((4, 4, PACKED, 256), bf16),
         in_specs=[wide, wide, wide, pl.BlockSpec((4, 4, 256), lambda y: (0, 0, 0))],
-        out_specs=pl.BlockSpec((4, 1, PACKED, 256), lambda y: (0, y, 0, 0)),
+        out_specs=pl.BlockSpec((1, 4, PACKED, 256), lambda y: (y, 0, 0, 0)),
         name="pack_q",
     )(queries, out_grad, fwd_out, norms)
     packed = exchange(q_out.reshape(16, PACKED, 256))
@@ -364,7 +366,7 @@
         unpack_q_kernel,
         grid=(4,),
         out_shape=jax.ShapeDtypeStruct((HALF, 64 * HEAD_DIM), bf16),
-        in_specs=[pl.BlockSpec((4, 1, HEAD_DIM, 256), lambda y: (0, y, 0, 0))],
+        in_specs=[pl.BlockSpec((1, 4, HEAD_DIM, 256), lambda y: (y, 0, 0, 0))],
         out_specs=wide,
         compiler_params=pltpu.CompilerParams(vmem_limit_bytes=6 * MIB),
         name="unpack_q",

time: 120 us -> 119 us (level)
  waiting for transfers between devices: 46.9 us -> 45 us
    all_to_all x4, waiting for transfers between devices: 21.5 us -> 19.9 us  [exchange(): return lax.all_to_all(array, ('y', 'z'), 0, 0, tiled=True)]
where the time goes in v5:
time: 119 us; the launch traced here: 118 us
  waiting for transfers between devices  45 us (38%)
  starting transfers between devices  39.5 us (33%)
  Pallas kernels  28.6 us (24%)
  local copies, waits for them, and re-layouts  4.01 us (3%)
    ppermute x10, waiting for transfers between devices, shift(): return lax.ppermute(array, axis, [(i, (i + by) % 4) for i in range(4)])  23.3 us
    all_to_all x4, starting transfers between devices, exchange(): return lax.all_to_all(array, ('y', 'z'), 0, 0, tiled=True)  22.3 us
    all_to_all x4, waiting for transfers between devices, exchange(): return lax.all_to_all(array, ('y', 'z'), 0, 0, tiled=True)  19.9 us
    ppermute x10, starting transfers between devices, shift(): return lax.ppermute(array, axis, [(i, (i + by) % 4) for i in range(4)])  16.5 us
    pallas_call x1, Pallas kernels, tiles(): pl.pallas_call(tiles_kernel, out_shape=[pltpu.HBM((16, HEAD_DIM, 256), bf...  15.5 us
    pallas_call x1, Pallas kernels, shards(): pl.pallas_call(pack_q_kernel, grid=(4,), out_shape=jax.ShapeDtypeStruct((...  4.72 us
  transfers between devices with their start and end apart: 20, of which 14 were waited for; matrix products, arithmetic and copies ran while one was open for 3% of the time, Pallas kernels for 9%

profile of v5, /device:TPU:0, one launch (start us, length us, event | category | flops | bytes accessed | tf_op | source)
XLA Modules:
  0.0 117.9 jit_solution(16430492762715872831)
XLA Ops:
  0.6 1.8 %pack_kv.1 = bf16[4,4,2,64,128]{4,3,2,1,0:T(8,128)(2,1)} custom-call(bf16[64,1024]{1,0:T(8,128)(2,1)} %keys_ref.1, bf16[64,1024]{1,0:T(8,128)(2,1)} %values_ref.1), custom_call_target="tpu_custom_call" | custom-call | tf_op jit(solution)/shard_map/pack_kv/pallas_call | solution.py:294
  2.5 8.1 %all-to-all-start.1 = ((bf16[16,2,64,128]{3,2,1,0:T(8,128)(2,1)}), bf16[16,2,64,128]{3,2,1,0:T(8,128)(2,1)S(1)}, u32[]{:S(2)}, u32[]{:S(2)}) async-start(bf16[16,2,64,128]{3,2,1,0:T(8,128)(2,1)} %bitcast.25), calls=%async_computation.1 | async-start | bytes 1048576 | tf_op jit(solution)/shard_map/all_to_all | solution.py:287
  12.1 4.7 %pack_q.1 = bf16[4,4,272,256]{3,2,1,0:T(8,128)(2,1)} custom-call(bf16[64,8192]{1,0:T(8,128)(2,1)} %queries_ref.1, bf16[64,8192]{1,0:T(8,128)(2,1)} %grad_ref.1, bf16[64,8192]{1,0:T(8,128)(2,1)} %fwd_ref.1, f32[4,4,256]{2,1,0:T(4,128)} %reshape.55.norms_ref), custom_call_target="tpu_custom_call" | custom-call | tf_op jit(solution)/shard_map/pack_q/pallas_call | solution.py:305
  16.8 5.3 %all-to-all-done.1 = bf16[16,2,64,128]{3,2,1,0:T(8,128)(2,1)S(1)} async-done(((bf16[16,2,64,128]{3,2,1,0:T(8,128)(2,1)}), bf16[16,2,64,128]{3,2,1,0:T(8,128)(2,1)S(1)}, u32[]{:S(2)}, u32[]{:S(2)}) %all-to-all-start.1) | async-done | bytes 524320 | tf_op jit(solution)/shard_map/all_to_all | solution.py:287
  22.1 3.9 %all-to-all-start = ((bf16[16,272,256]{2,1,0:T(8,128)(2,1)}), bf16[16,272,256]{2,1,0:T(8,128)(2,1)S(1)}, u32[]{:S(2)}, u32[]{:S(2)}) async-start(bf16[16,272,256]{2,1,0:T(8,128)(2,1)} %bitcast.24), calls=%async_computation | async-start | bytes 4456448 | tf_op jit(solution)/shard_map/all_to_all | solution.py:287
  26.0 1.6 %collective-permute-start.2 = (bf16[16,2,64,128]{3,2,1,0:T(8,128)(2,1)S(1)}, bf16[16,2,64,128]{3,2,1,0:T(8,128)(2,1)S(1)}, u32[]{:S(2)}, u32[]{:S(2)}) collective-permute-start(bf16[16,2,64,128]{3,2,1,0:T(8,128)(2,1)S(1)} %all-to-all-done.1), channel_id=1, source_target_pairs={{0,8},{8,16},{16,24},{24,0},{1,9},{9,17},{17,25},{25,1},{2,10},{10... | collective-permute-start | bytes 1572872 | tf_op jit(solution)/shard_map/ppermute | solution.py:275
  27.5 1.7 %collective-permute-start = (bf16[16,2,64,128]{3,2,1,0:T(8,128)(2,1)S(1)}, bf16[16,2,64,128]{3,2,1,0:T(8,128)(2,1)}, u32[]{:S(2)}, u32[]{:S(2)}) collective-permute-start(bf16[16,2,64,128]{3,2,1,0:T(8,128)(2,1)S(1)} %all-to-all-done.1), channel_id=1, source_target_pairs={{0,24},{8,0},{16,8},{24,16},{1,25},{9,1},{17,9},{25,17},{2,26},{10... | collective-permute-start | bytes 1572872 | tf_op jit(solution)/shard_map/ppermute | solution.py:275
  29.3 10.2 %collective-permute-done.2 = bf16[16,2,64,128]{3,2,1,0:T(8,128)(2,1)S(1)} collective-permute-done((bf16[16,2,64,128]{3,2,1,0:T(8,128)(2,1)S(1)}, bf16[16,2,64,128]{3,2,1,0:T(8,128)(2,1)S(1)}, u32[]{:S(2)}, u32[]{:S(2)}) %collective-permute-start.2) | collective-permute-done | bytes 524320 | tf_op jit(solution)/shard_map/ppermute | solution.py:275
  40.8 3.0 %collective-permute-start.1 = (bf16[8,2,64,128]{3,2,1,0:T(8,128)(2,1)S(1)}, bf16[8,2,64,128]{3,2,1,0:T(8,128)(2,1)}, u32[]{:S(2)}, u32[]{:S(2)}) collective-permute-start(bf16[8,2,64,128]{3,2,1,0:T(8,128)(2,1)S(1)} %slice.8), channel_id=1, source_target_pairs={{0,24},{8,0},{16,8},{24,16},{1,25},{9,1},{17,9},{25,17},{2,26},{10... | collective-permute-start | bytes 786440 | tf_op jit(solution)/shard_map/ppermute | solution.py:275
  44.3 2.8 %collective-permute-done.3 = bf16[8,2,64,128]{3,2,1,0:T(8,128)(2,1)S(1)} collective-permute-done((bf16[8,2,64,128]{3,2,1,0:T(8,128)(2,1)S(1)}, bf16[8,2,64,128]{3,2,1,0:T(8,128)(2,1)S(1)}, u32[]{:S(2)}, u32[]{:S(2)}) %collective-permute-start.3) | collective-permute-done | bytes 262176 | tf_op jit(solution)/shard_map/ppermute | solution.py:275
  49.6 6.4 %all-to-all-done.packed_ref = bf16[16,272,256]{2,1,0:T(8,128)(2,1)S(1)} async-done(((bf16[16,272,256]{2,1,0:T(8,128)(2,1)}), bf16[16,272,256]{2,1,0:T(8,128)(2,1)S(1)}, u32[]{:S(2)}, u32[]{:S(2)}) %all-to-all-start) | async-done | bytes 2228256 | tf_op jit(solution)/shard_map/all_to_all | solution.py:287
  56.0 15.5 %tiles.1 = (bf16[16,128,256]{2,1,0:T(8,128)(2,1)}, bf16[4,8,2,128,128]{4,3,2,1,0:T(8,128)(2,1)}, bf16[4,8,2,128,128]{4,3,2,1,0:T(8,128)(2,1)}) custom-call(s32[32,2]{1,0:T(8,128)} %copy.12.plan_in, s32[12]{0:T(128)} %bounds_in.1, bf16[16,272,256]{2,1,0:T(8,128)(2,1)S(1)} %all-to-all-done.packed_ref, bf16[2,2,4,2,64,128]{5,4,3,2,1,0:T(8,128)(2,1)S(1)} %bitcast.20, ...), custom_call_target="tpu_custom_call" | custom-call | tf_op jit(solution)/shard_map/tiles/pallas_call | solution.py:250
  71.5 3.9 %all-to-all-start.2 = ((bf16[16,128,256]{2,1,0:T(8,128)(2,1)}), bf16[16,128,256]{2,1,0:T(8,128)(2,1)S(1)}, u32[]{:S(2)}, u32[]{:S(2)}) async-start(bf16[16,128,256]{2,1,0:T(8,128)(2,1)} %get-tuple-element.24), calls=%async_computation.2 | async-start | bytes 2097152 | tf_op jit(solution)/shard_map/all_to_all | solution.py:287
  76.0 1.4 %first_sums.1 = (bf16[1,4,2,128,128]{4,3,2,1,0:T(8,128)(2,1)S(1)}, bf16[1,4,2,128,128]{4,3,2,1,0:T(8,128)(2,1)S(1)}, bf16[1,4,2,128,128]{4,3,2,1,0:T(8,128)(2,1)S(1)}, bf16[1,4,2,128,128]{4,3,2,1,0:T(8,128)(2,1)S(1)}) custom-call(bf16[4,8,2,128,128]{4,3,2,1,0:T(8,128)(2,1)S(1)} %copy-done, ...), custom_call_target="tpu_custom_call" | custom-call | tf_op jit(solution)/shard_map/first_sums/pallas_call | solution.py:331
  77.5 1.6 %collective-permute-start.10 = (bf16[1,4,2,128,128]{4,3,2,1,0:T(8,128)(2,1)S(1)}, bf16[1,4,2,128,128]{4,3,2,1,0:T(8,128)(2,1)S(1)}, u32[]{:S(2)}, u32[]{:S(2)}) collective-permute-start(bf16[1,4,2,128,128]{4,3,2,1,0:T(8,128)(2,1)S(1)} %get-tuple-element.18), channel_id=1, source_target_pairs={{0,8},{8,16},{16,24},{24,0},{1,9},{9,17},{17,25},{25,1},{2,10},{10... | collective-permute-start | bytes 786440 | tf_op jit(solution)/shard_map/ppermute | solution.py:275
  79.0 1.7 %collective-permute-start.11 = (bf16[1,4,2,128,128]{4,3,2,1,0:T(8,128)(2,1)S(1)}, bf16[1,4,2,128,128]{4,3,2,1,0:T(8,128)(2,1)S(1)}, u32[]{:S(2)}, u32[]{:S(2)}) collective-permute-start(bf16[1,4,2,128,128]{4,3,2,1,0:T(8,128)(2,1)S(1)} %get-tuple-element.19), channel_id=1, source_target_pairs={{0,24},{8,0},{16,8},{24,16},{1,25},{9,1},{17,9},{25,17},{2,26},{10... | collective-permute-start | bytes 786440 | tf_op jit(solution)/shard_map/ppermute | solution.py:275
  81.0 3.0 %collective-permute-start.14 = (bf16[1,4,2,128,128]{4,3,2,1,0:T(8,128)(2,1)S(1)}, bf16[1,4,2,128,128]{4,3,2,1,0:T(8,128)(2,1)S(1)}, u32[]{:S(2)}, u32[]{:S(2)}) collective-permute-start(bf16[1,4,2,128,128]{4,3,2,1,0:T(8,128)(2,1)S(1)} %get-tuple-element.22), channel_id=1, source_target_pairs={{0,24},{8,0},{16,8},{24,16},{1,25},{9,1},{17,9},{25,17},{2,26},{10... | collective-permute-start | bytes 786440 | tf_op jit(solution)/shard_map/ppermute | solution.py:275
  84.0 3.9 %collective-permute-done.10.refs_2_ = bf16[1,4,2,128,128]{4,3,2,1,0:T(8,128)(2,1)S(1)} collective-permute-done((bf16[1,4,2,128,128]{4,3,2,1,0:T(8,128)(2,1)S(1)}, bf16[1,4,2,128,128]{4,3,2,1,0:T(8,128)(2,1)S(1)}, u32[]{:S(2)}, u32[]{:S(2)}) %collective-permute-start.10) | collective-permute-done | bytes 262176 | tf_op jit(solution)/shard_map/ppermute | solution.py:275
  89.4 1.6 %collective-permute-start.12 = (bf16[1,4,2,128,128]{4,3,2,1,0:T(8,128)(2,1)S(1)}, bf16[1,4,2,128,128]{4,3,2,1,0:T(8,128)(2,1)S(1)}, u32[]{:S(2)}, u32[]{:S(2)}) collective-permute-start(bf16[1,4,2,128,128]{4,3,2,1,0:T(8,128)(2,1)S(1)} %get-tuple-element.20), channel_id=1, source_target_pairs={{0,8},{8,16},{16,24},{24,0},{1,9},{9,17},{17,25},{25,1},{2,10},{10... | collective-permute-start | bytes 786440 | tf_op jit(solution)/shard_map/ppermute | solution.py:275
  91.0 1.7 %collective-permute-start.15 = (bf16[1,4,2,128,128]{4,3,2,1,0:T(8,128)(2,1)S(1)}, bf16[1,4,2,128,128]{4,3,2,1,0:T(8,128)(2,1)S(1)}, u32[]{:S(2)}, u32[]{:S(2)}) collective-permute-start(bf16[1,4,2,128,128]{4,3,2,1,0:T(8,128)(2,1)S(1)} %get-tuple-element.23), channel_id=1, source_target_pairs={{0,24},{8,0},{16,8},{24,16},{1,25},{9,1},{17,9},{25,17},{2,26},{10... | collective-permute-start | bytes 786440 | tf_op jit(solution)/shard_map/ppermute | solution.py:275
  93.8 4.5 %collective-permute-done.12.last_a_ref = bf16[1,4,2,128,128]{4,3,2,1,0:T(8,128)(2,1)S(1)} collective-permute-done((bf16[1,4,2,128,128]{4,3,2,1,0:T(8,128)(2,1)S(1)}, bf16[1,4,2,128,128]{4,3,2,1,0:T(8,128)(2,1)S(1)}, u32[]{:S(2)}, u32[]{:S(2)}) %collective-permute-start.12) | collective-permute-done | bytes 262176 | tf_op jit(solution)/shard_map/ppermute | solution.py:275
  100.5 6.4 %all-to-all-start.3 = ((bf16[16,2,64,128]{3,2,1,0:T(8,128)(2,1)}), bf16[16,2,64,128]{3,2,1,0:T(8,128)(2,1)S(1)}, u32[]{:S(2)}, u32[]{:S(2)}) async-start(bf16[16,2,64,128]{3,2,1,0:T(8,128)(2,1)} %copy-done.1), calls=%async_computation.3 | async-start | bytes 1048576 | tf_op jit(solution)/shard_map/all_to_all | solution.py:287
  107.0 1.8 %unpack_q.1 = bf16[64,8192]{1,0:T(8,128)(2,1)} custom-call(bf16[4,4,128,256]{3,2,1,0:T(8,128)(2,1)S(1)} %bitcast.19), custom_call_target="tpu_custom_call" | custom-call | tf_op jit(solution)/shard_map/unpack_q/pallas_call | solution.py:365
  108.8 8.3 %all-to-all-done.3 = bf16[16,2,64,128]{3,2,1,0:T(8,128)(2,1)S(1)} async-done(((bf16[16,2,64,128]{3,2,1,0:T(8,128)(2,1)}), bf16[16,2,64,128]{3,2,1,0:T(8,128)(2,1)S(1)}, u32[]{:S(2)}, u32[]{:S(2)}) %all-to-all-start.3) | async-done | bytes 524320 | tf_op jit(solution)/shard_map/all_to_all | solution.py:287
  (36 shorter events, 12.4 us)
Async XLA Ops:
  2.5 19.6 %all-to-all-start.1 = ((bf16[16,2,64,128]{3,2,1,0:T(8,128)(2,1)}), bf16[16,2,64,128]{3,2,1,0:T(8,128)(2,1)S(1)}, u32[]{:S(2)}, u32[]{:S(2)}) async-start(bf16[16,2,64,128]{3,2,1,0:T(8,128)(2,1)} %bitcast.25), calls=%async_computation.1 | async-start | bytes 1048576 | tf_op jit(solution)/shard_map/all_to_all | solution.py:287
  22.1 25.6 %copy-start.2 = (s32[32,2]{0,1:T(2,128)S(1)}, s32[32,2]{0,1:T(2,128)}, u32[]{:S(2)}) copy-start(s32[32,2]{0,1:T(2,128)} %param.16) | copy-start | bytes 772
  22.1 33.9 %all-to-all-start = ((bf16[16,272,256]{2,1,0:T(8,128)(2,1)}), bf16[16,272,256]{2,1,0:T(8,128)(2,1)S(1)}, u32[]{:S(2)}, u32[]{:S(2)}) async-start(bf16[16,272,256]{2,1,0:T(8,128)(2,1)} %bitcast.24), calls=%async_computation | async-start | bytes 4456448 | tf_op jit(solution)/shard_map/all_to_all | solution.py:287
  26.0 13.5 %collective-permute-start.2 = (bf16[16,2,64,128]{3,2,1,0:T(8,128)(2,1)S(1)}, bf16[16,2,64,128]{3,2,1,0:T(8,128)(2,1)S(1)}, u32[]{:S(2)}, u32[]{:S(2)}) collective-permute-start(bf16[16,2,64,128]{3,2,1,0:T(8,128)(2,1)S(1)} %all-to-all-done.1), channel_id=1, source_target_pairs={{0,8},{8,16},{16,24},{24,0},{1,9},{9,17},{17,25},{25,1},{2,10},{10... | collective-permute-start | bytes 1572872 | tf_op jit(solution)/shard_map/ppermute | solution.py:275
  27.5 12.3 %collective-permute-start = (bf16[16,2,64,128]{3,2,1,0:T(8,128)(2,1)S(1)}, bf16[16,2,64,128]{3,2,1,0:T(8,128)(2,1)}, u32[]{:S(2)}, u32[]{:S(2)}) collective-permute-start(bf16[16,2,64,128]{3,2,1,0:T(8,128)(2,1)S(1)} %all-to-all-done.1), channel_id=1, source_target_pairs={{0,24},{8,0},{16,8},{24,16},{1,25},{9,1},{17,9},{25,17},{2,26},{10... | collective-permute-start | bytes 1572872 | tf_op jit(solution)/shard_map/ppermute | solution.py:275
  29.3 19.1 %collective-permute-start.4 = (bf16[16,2,64,128]{3,2,1,0:T(8,128)(2,1)S(1)}, bf16[16,2,64,128]{3,2,1,0:T(8,128)(2,1)}, u32[]{:S(2)}, u32[]{:S(2)}) collective-permute-start(bf16[16,2,64,128]{3,2,1,0:T(8,128)(2,1)S(1)} %all-to-all-done.1), channel_id=1, source_target_pairs={{0,4},{4,0},{1,5},{5,1},{2,6},{6,2},{3,7},{7,3},{8,12},{12,8},{9,1... | collective-permute-start | bytes 1572872 | tf_op jit(solution)/shard_map/ppermute | solution.py:283
  39.5 7.7 %collective-permute-start.3 = (bf16[8,2,64,128]{3,2,1,0:T(8,128)(2,1)S(1)}, bf16[8,2,64,128]{3,2,1,0:T(8,128)(2,1)S(1)}, u32[]{:S(2)}, u32[]{:S(2)}) collective-permute-start(bf16[8,2,64,128]{3,2,1,0:T(8,128)(2,1)S(1)} %slice.9), channel_id=1, source_target_pairs={{0,8},{8,16},{16,24},{24,0},{1,9},{9,17},{17,25},{25,1},{2,10},{10... | collective-permute-start | bytes 786440 | tf_op jit(solution)/shard_map/ppermute | solution.py:275
  40.8 6.9 %collective-permute-start.1 = (bf16[8,2,64,128]{3,2,1,0:T(8,128)(2,1)S(1)}, bf16[8,2,64,128]{3,2,1,0:T(8,128)(2,1)}, u32[]{:S(2)}, u32[]{:S(2)}) collective-permute-start(bf16[8,2,64,128]{3,2,1,0:T(8,128)(2,1)S(1)} %slice.8), channel_id=1, source_target_pairs={{0,24},{8,0},{16,8},{24,16},{1,25},{9,1},{17,9},{25,17},{2,26},{10... | collective-permute-start | bytes 786440 | tf_op jit(solution)/shard_map/ppermute | solution.py:275
  43.8 5.0 %collective-permute-start.8 = (bf16[16,2,64,128]{3,2,1,0:T(8,128)(2,1)S(1)}, bf16[16,2,64,128]{3,2,1,0:T(8,128)(2,1)}, u32[]{:S(2)}, u32[]{:S(2)}) collective-permute-start(bf16[16,2,64,128]{3,2,1,0:T(8,128)(2,1)S(1)} %collective-permute-done.2), channel_id=1, source_target_pairs={{0,4},{4,0},{1,5},{5,1},{2,6},{6,2},{3,7},{7,3},{8,12},{12,8},{9,1... | collective-permute-start | bytes 1572872 | tf_op jit(solution)/shard_map/ppermute | solution.py:283
  43.8 5.8 %collective-permute-start.5 = (bf16[16,2,64,128]{3,2,1,0:T(8,128)(2,1)}, bf16[16,2,64,128]{3,2,1,0:T(8,128)(2,1)}, u32[]{:S(2)}, u32[]{:S(2)}) collective-permute-start(bf16[16,2,64,128]{3,2,1,0:T(8,128)(2,1)} %collective-permute-done), channel_id=1, source_target_pairs={{0,4},{4,0},{1,5},{5,1},{2,6},{6,2},{3,7},{7,3},{8,12},{12,8},{9,1... | collective-permute-start | bytes 1572872 | tf_op jit(solution)/shard_map/ppermute | solution.py:283
  47.1 1.7 %collective-permute-start.7 = (bf16[8,2,64,128]{3,2,1,0:T(8,128)(2,1)S(1)}, bf16[8,2,64,128]{3,2,1,0:T(8,128)(2,1)}, u32[]{:S(2)}, u32[]{:S(2)}) collective-permute-start(bf16[8,2,64,128]{3,2,1,0:T(8,128)(2,1)S(1)} %collective-permute-done.3), channel_id=1, source_target_pairs={{0,4},{4,0},{1,5},{5,1},{2,6},{6,2},{3,7},{7,3},{8,12},{12,8},{9,1... | collective-permute-start | bytes 786440 | tf_op jit(solution)/shard_map/ppermute | solution.py:283
  47.7 1.9 %collective-permute-start.6 = (bf16[8,2,64,128]{3,2,1,0:T(8,128)(2,1)}, bf16[8,2,64,128]{3,2,1,0:T(8,128)(2,1)}, u32[]{:S(2)}, u32[]{:S(2)}) collective-permute-start(bf16[8,2,64,128]{3,2,1,0:T(8,128)(2,1)} %collective-permute-done.1), channel_id=1, source_target_pairs={{0,4},{4,0},{1,5},{5,1},{2,6},{6,2},{3,7},{7,3},{8,12},{12,8},{9,1... | collective-permute-start | bytes 786440 | tf_op jit(solution)/shard_map/ppermute | solution.py:283
  71.4 4.6 %copy-start = (bf16[4,8,2,128,128]{4,3,2,1,0:T(8,128)(2,1)S(1)}, bf16[4,8,2,128,128]{4,3,2,1,0:T(8,128)(2,1)}, u32[]{:S(2)}) copy-start(bf16[4,8,2,128,128]{4,3,2,1,0:T(8,128)(2,1)} %get-tuple-element.16.refs_0_.refs_2_.refs_4_.refs_6_.refs_3_.keep_ref) | copy-start | bytes 6291460
  71.4 4.6 %collective-permute-start.9 = (bf16[4,8,2,128,128]{4,3,2,1,0:T(8,128)(2,1)}, bf16[4,8,2,128,128]{4,3,2,1,0:T(8,128)(2,1)}, u32[]{:S(2)}, u32[]{:S(2)}) collective-permute-start(bf16[4,8,2,128,128]{4,3,2,1,0:T(8,128)(2,1)} %get-tuple-element.17), channel_id=1, source_target_pairs={{0,4},{4,0},{1,5},{5,1},{2,6},{6,2},{3,7},{7,3},{8,12},{12,8},{9,1... | collective-permute-start | bytes 6291464 | tf_op jit(solution)/shard_map/ppermute | solution.py:283
  71.5 29.0 %all-to-all-start.2 = ((bf16[16,128,256]{2,1,0:T(8,128)(2,1)}), bf16[16,128,256]{2,1,0:T(8,128)(2,1)S(1)}, u32[]{:S(2)}, u32[]{:S(2)}) async-start(bf16[16,128,256]{2,1,0:T(8,128)(2,1)} %get-tuple-element.24), calls=%async_computation.2 | async-start | bytes 2097152 | tf_op jit(solution)/shard_map/all_to_all | solution.py:287
  77.5 10.4 %collective-permute-start.10 = (bf16[1,4,2,128,128]{4,3,2,1,0:T(8,128)(2,1)S(1)}, bf16[1,4,2,128,128]{4,3,2,1,0:T(8,128)(2,1)S(1)}, u32[]{:S(2)}, u32[]{:S(2)}) collective-permute-start(bf16[1,4,2,128,128]{4,3,2,1,0:T(8,128)(2,1)S(1)} %get-tuple-element.18), channel_id=1, source_target_pairs={{0,8},{8,16},{16,24},{24,0},{1,9},{9,17},{17,25},{25,1},{2,10},{10... | collective-permute-start | bytes 786440 | tf_op jit(solution)/shard_map/ppermute | solution.py:275
  79.0 9.2 %collective-permute-start.11 = (bf16[1,4,2,128,128]{4,3,2,1,0:T(8,128)(2,1)S(1)}, bf16[1,4,2,128,128]{4,3,2,1,0:T(8,128)(2,1)S(1)}, u32[]{:S(2)}, u32[]{:S(2)}) collective-permute-start(bf16[1,4,2,128,128]{4,3,2,1,0:T(8,128)(2,1)S(1)} %get-tuple-element.19), channel_id=1, source_target_pairs={{0,24},{8,0},{16,8},{24,16},{1,25},{9,1},{17,9},{25,17},{2,26},{10... | collective-permute-start | bytes 786440 | tf_op jit(solution)/shard_map/ppermute | solution.py:275
  80.8 12.7 %collective-permute-start.13 = (bf16[1,4,2,128,128]{4,3,2,1,0:T(8,128)(2,1)S(1)}, bf16[1,4,2,128,128]{4,3,2,1,0:T(8,128)(2,1)S(1)}, u32[]{:S(2)}, u32[]{:S(2)}) collective-permute-start(bf16[1,4,2,128,128]{4,3,2,1,0:T(8,128)(2,1)S(1)} %get-tuple-element.21), channel_id=1, source_target_pairs={{0,8},{8,16},{16,24},{24,0},{1,9},{9,17},{17,25},{25,1},{2,10},{10... | collective-permute-start | bytes 786440 | tf_op jit(solution)/shard_map/ppermute | solution.py:275
  81.0 12.8 %collective-permute-start.14 = (bf16[1,4,2,128,128]{4,3,2,1,0:T(8,128)(2,1)S(1)}, bf16[1,4,2,128,128]{4,3,2,1,0:T(8,128)(2,1)S(1)}, u32[]{:S(2)}, u32[]{:S(2)}) collective-permute-start(bf16[1,4,2,128,128]{4,3,2,1,0:T(8,128)(2,1)S(1)} %get-tuple-element.22), channel_id=1, source_target_pairs={{0,24},{8,0},{16,8},{24,16},{1,25},{9,1},{17,9},{25,17},{2,26},{10... | collective-permute-start | bytes 786440 | tf_op jit(solution)/shard_map/ppermute | solution.py:275
  89.4 8.9 %collective-permute-start.12 = (bf16[1,4,2,128,128]{4,3,2,1,0:T(8,128)(2,1)S(1)}, bf16[1,4,2,128,128]{4,3,2,1,0:T(8,128)(2,1)S(1)}, u32[]{:S(2)}, u32[]{:S(2)}) collective-permute-start(bf16[1,4,2,128,128]{4,3,2,1,0:T(8,128)(2,1)S(1)} %get-tuple-element.20), channel_id=1, source_target_pairs={{0,8},{8,16},{16,24},{24,0},{1,9},{9,17},{17,25},{25,1},{2,10},{10... | collective-permute-start | bytes 786440 | tf_op jit(solution)/shard_map/ppermute | solution.py:275
  91.0 7.3 %collective-permute-start.15 = (bf16[1,4,2,128,128]{4,3,2,1,0:T(8,128)(2,1)S(1)}, bf16[1,4,2,128,128]{4,3,2,1,0:T(8,128)(2,1)S(1)}, u32[]{:S(2)}, u32[]{:S(2)}) collective-permute-start(bf16[1,4,2,128,128]{4,3,2,1,0:T(8,128)(2,1)S(1)} %get-tuple-element.23), channel_id=1, source_target_pairs={{0,24},{8,0},{16,8},{24,16},{1,25},{9,1},{17,9},{25,17},{2,26},{10... | collective-permute-start | bytes 786440 | tf_op jit(solution)/shard_map/ppermute | solution.py:275
  99.7 0.8 copy-start.1
  100.5 16.5 %all-to-all-start.3 = ((bf16[16,2,64,128]{3,2,1,0:T(8,128)(2,1)}), bf16[16,2,64,128]{3,2,1,0:T(8,128)(2,1)S(1)}, u32[]{:S(2)}, u32[]{:S(2)}) async-start(bf16[16,2,64,128]{3,2,1,0:T(8,128)(2,1)} %copy-done.1), calls=%async_computation.3 | async-start | bytes 1048576 | tf_op jit(solution)/shard_map/all_to_all | solution.py:287

commit v6 on v5

--- a/solution.py
+++ b/solution.py
@@ -23,7 +23,7 @@
 
 def pack_kv_kernel(keys_ref, values_ref, out_ref):
     for z in range(4):
-        for y in range(4):
+        for y in range(2):
             cols = slice((2 * y + z // 2) * HEAD_DIM, (2 * y + z // 2 + 1) * HEAD_DIM)
             out_ref[y, z, 0] = keys_ref[:, cols]
             out_ref[y, z, 1] = values_ref[:, cols]
@@ -74,15 +74,22 @@
 
 
 def final_kernel(keep_ref, got_ref, last_a_ref, last_b_ref, next_a_ref, next_b_ref, out_ref):
-    for t in range(8):
-        last_ref, next_ref = ((last_a_ref, next_a_ref), (last_b_ref, next_b_ref))[t // 4]
-        for i in range(2):
-            total = keep_ref[0, t, i].astype(jnp.float32) + got_ref[0, t, i].astype(jnp.float32)
-            total = total + last_ref[0, t % 4, i].astype(jnp.float32) + next_ref[0, t % 4, i].astype(jnp.float32)
-            rows = jnp.transpose(total).astype(jnp.bfloat16)
-            first = t // 4 * 8 + t % 4
-            out_ref[first, i] = rows[:HALF]
-            out_ref[first + 4, i] = rows[HALF:]
+    def half(last_ref, next_ref):
+        for t in range(4):
+            for i in range(2):
+                total = keep_ref[0, t, i].astype(jnp.float32) + got_ref[0, t, i].astype(jnp.float32)
+                total = total + last_ref[0, t, i].astype(jnp.float32) + next_ref[0, t, i].astype(jnp.float32)
+                rows = jnp.transpose(total).astype(jnp.bfloat16)
+                out_ref[t, i] = rows[:HALF]
+                out_ref[t + 4, i] = rows[HALF:]
+
+    @pl.when(pl.program_id(0) == 0)
+    def _():
+        half(last_a_ref, next_a_ref)
+
+    @pl.when(pl.program_id(0) == 1)
+    def _():
+        half(last_b_ref, next_b_ref)
 
 
 def unpack_kv_kernel(in_ref, keys_ref, values_ref):
@@ -293,9 +300,10 @@
 
     kv_out = pl.pallas_call(
         pack_kv_kernel,
+        grid=(2,),
         out_shape=jax.ShapeDtypeStruct((4, 4, 2, HALF, HEAD_DIM), bf16),
-        in_specs=[VMEM, VMEM],
-        out_specs=VMEM,
+        in_specs=[pl.BlockSpec((HALF, 4 * HEAD_DIM), lambda y: (0, y))] * 2,
+        out_specs=pl.BlockSpec((2, 4, 2, HALF, HEAD_DIM), lambda y: (y, 0, 0, 0, 0)),
         name="pack_kv",
     )(keys, values)
     block = exchange(kv_out.reshape(16, 2, HALF, HEAD_DIM))
@@ -350,13 +358,13 @@
     )(keep, got, via_next, keep, got, via_last)
     last_a, next_b = shift(last_a, "x", 1), shift(next_b, "x", -1)
     dq_back = exchange(dq).reshape(4, 4, HEAD_DIM, 256)
-    slab = pl.BlockSpec((1, 8, 2, HEAD_DIM, SPAN), lambda _: (0, 0, 0, 0, 0))
+    slab = pl.BlockSpec((1, 4, 2, HEAD_DIM, SPAN), lambda j: (0, j, 0, 0, 0))
     total = pl.pallas_call(
         final_kernel,
-        grid=(1,),
-        out_shape=jax.ShapeDtypeStruct((16, 2, HALF, HEAD_DIM), bf16),
+        grid=(2,),
+        out_shape=pltpu.HBM((16, 2, HALF, HEAD_DIM), bf16),
         in_specs=[slab] * 2 + [block_of(0, 0)] * 4,
-        out_specs=pl.BlockSpec((16, 2, HALF, HEAD_DIM), lambda _: (0, 0, 0, 0)),
+        out_specs=pl.BlockSpec((8, 2, HALF, HEAD_DIM), lambda j: (j, 0, 0, 0)),
         compiler_params=pltpu.CompilerParams(vmem_limit_bytes=8 * MIB),
         name="own_slab",
     )(keep, got, last_a, last_b, next_a, next_b)

time: 119 us -> 118 us (level)
  transfers between devices with their start and end apart: 20 -> 20, of which waited for: 14 -> 14; matrix products, arithmetic and copies ran while one was open for 3% -> 3% of each run, Pallas kernels for 9% -> 10%
where the time goes in v6:
time: 118 us
  waiting for transfers between devices  45 us (38%)
  starting transfers between devices  39.5 us (33%)
  Pallas kernels  29.1 us (25%)
  local copies, waits for them, and re-layouts  3.19 us (3%)
    ppermute x10, waiting for transfers between devices, shift(): return lax.ppermute(array, axis, [(i, (i + by) % 4) for i in range(4)])  23.4 us
    all_to_all x4, starting transfers between devices, exchange(): return lax.all_to_all(array, ('y', 'z'), 0, 0, tiled=True)  22.4 us
    all_to_all x4, waiting for transfers between devices, exchange(): return lax.all_to_all(array, ('y', 'z'), 0, 0, tiled=True)  19.9 us
    ppermute x10, starting transfers between devices, shift(): return lax.ppermute(array, axis, [(i, (i + by) % 4) for i in range(4)])  16.5 us
    pallas_call x1, Pallas kernels, tiles(): pl.pallas_call(tiles_kernel, out_shape=[pltpu.HBM((16, HEAD_DIM, 256), bf...  15.4 us
    pallas_call x1, Pallas kernels, shards(): pl.pallas_call(pack_q_kernel, grid=(4,), out_shape=jax.ShapeDtypeStruct((...  4.71 us
  transfers between devices with their start and end apart: 20, of which 14 were waited for; matrix products, arithmetic and copies ran while one was open for 3% of the time, Pallas kernels for 10%

profile of v6, /device:TPU:0, one launch (start us, length us, event | category | flops | bytes accessed | tf_op | source)
XLA Modules:
  0.0 117.6 jit_solution(13457284443734348623)
XLA Ops:
  0.6 1.7 %pack_kv.1 = bf16[4,4,2,64,128]{4,3,2,1,0:T(8,128)(2,1)} custom-call(bf16[64,1024]{1,0:T(8,128)(2,1)} %keys_ref.1, bf16[64,1024]{1,0:T(8,128)(2,1)} %values_ref.1), custom_call_target="tpu_custom_call" | custom-call | tf_op jit(solution)/shard_map/pack_kv/pallas_call | solution.py:301
  2.3 8.1 %all-to-all-start.1 = ((bf16[16,2,64,128]{3,2,1,0:T(8,128)(2,1)}), bf16[16,2,64,128]{3,2,1,0:T(8,128)(2,1)S(1)}, u32[]{:S(2)}, u32[]{:S(2)}) async-start(bf16[16,2,64,128]{3,2,1,0:T(8,128)(2,1)} %bitcast.25), calls=%async_computation.1 | async-start | bytes 1048576 | tf_op jit(solution)/shard_map/all_to_all | solution.py:294
  12.0 4.7 %pack_q.1 = bf16[4,4,272,256]{3,2,1,0:T(8,128)(2,1)} custom-call(bf16[64,8192]{1,0:T(8,128)(2,1)} %queries_ref.1, bf16[64,8192]{1,0:T(8,128)(2,1)} %grad_ref.1, bf16[64,8192]{1,0:T(8,128)(2,1)} %fwd_ref.1, f32[4,4,256]{2,1,0:T(4,128)} %reshape.55.norms_ref), custom_call_target="tpu_custom_call" | custom-call | tf_op jit(solution)/shard_map/pack_q/pallas_call | solution.py:313
  16.7 5.3 %all-to-all-done.1 = bf16[16,2,64,128]{3,2,1,0:T(8,128)(2,1)S(1)} async-done(((bf16[16,2,64,128]{3,2,1,0:T(8,128)(2,1)}), bf16[16,2,64,128]{3,2,1,0:T(8,128)(2,1)S(1)}, u32[]{:S(2)}, u32[]{:S(2)}) %all-to-all-start.1) | async-done | bytes 524320 | tf_op jit(solution)/shard_map/all_to_all | solution.py:294
  22.0 3.9 %all-to-all-start = ((bf16[16,272,256]{2,1,0:T(8,128)(2,1)}), bf16[16,272,256]{2,1,0:T(8,128)(2,1)S(1)}, u32[]{:S(2)}, u32[]{:S(2)}) async-start(bf16[16,272,256]{2,1,0:T(8,128)(2,1)} %bitcast.24), calls=%async_computation | async-start | bytes 4456448 | tf_op jit(solution)/shard_map/all_to_all | solution.py:294
  25.8 1.6 %collective-permute-start.2 = (bf16[16,2,64,128]{3,2,1,0:T(8,128)(2,1)S(1)}, bf16[16,2,64,128]{3,2,1,0:T(8,128)(2,1)S(1)}, u32[]{:S(2)}, u32[]{:S(2)}) collective-permute-start(bf16[16,2,64,128]{3,2,1,0:T(8,128)(2,1)S(1)} %all-to-all-done.1), channel_id=1, source_target_pairs={{0,8},{8,16},{16,24},{24,0},{1,9},{9,17},{17,25},{25,1},{2,10},{10... | collective-permute-start | bytes 1572872 | tf_op jit(solution)/shard_map/ppermute | solution.py:282
  27.4 1.7 %collective-permute-start = (bf16[16,2,64,128]{3,2,1,0:T(8,128)(2,1)S(1)}, bf16[16,2,64,128]{3,2,1,0:T(8,128)(2,1)}, u32[]{:S(2)}, u32[]{:S(2)}) collective-permute-start(bf16[16,2,64,128]{3,2,1,0:T(8,128)(2,1)S(1)} %all-to-all-done.1), channel_id=1, source_target_pairs={{0,24},{8,0},{16,8},{24,16},{1,25},{9,1},{17,9},{25,17},{2,26},{10... | collective-permute-start | bytes 1572872 | tf_op jit(solution)/shard_map/ppermute | solution.py:282
  29.1 10.2 %collective-permute-done.2 = bf16[16,2,64,128]{3,2,1,0:T(8,128)(2,1)S(1)} collective-permute-done((bf16[16,2,64,128]{3,2,1,0:T(8,128)(2,1)S(1)}, bf16[16,2,64,128]{3,2,1,0:T(8,128)(2,1)S(1)}, u32[]{:S(2)}, u32[]{:S(2)}) %collective-permute-start.2) | collective-permute-done | bytes 524320 | tf_op jit(solution)/shard_map/ppermute | solution.py:282
  40.7 3.0 %collective-permute-start.1 = (bf16[8,2,64,128]{3,2,1,0:T(8,128)(2,1)S(1)}, bf16[8,2,64,128]{3,2,1,0:T(8,128)(2,1)}, u32[]{:S(2)}, u32[]{:S(2)}) collective-permute-start(bf16[8,2,64,128]{3,2,1,0:T(8,128)(2,1)S(1)} %slice.8), channel_id=1, source_target_pairs={{0,24},{8,0},{16,8},{24,16},{1,25},{9,1},{17,9},{25,17},{2,26},{10... | collective-permute-start | bytes 786440 | tf_op jit(solution)/shard_map/ppermute | solution.py:282
  44.2 2.8 %collective-permute-done.3 = bf16[8,2,64,128]{3,2,1,0:T(8,128)(2,1)S(1)} collective-permute-done((bf16[8,2,64,128]{3,2,1,0:T(8,128)(2,1)S(1)}, bf16[8,2,64,128]{3,2,1,0:T(8,128)(2,1)S(1)}, u32[]{:S(2)}, u32[]{:S(2)}) %collective-permute-start.3) | collective-permute-done | bytes 262176 | tf_op jit(solution)/shard_map/ppermute | solution.py:282
  49.5 6.4 %all-to-all-done.packed_ref = bf16[16,272,256]{2,1,0:T(8,128)(2,1)S(1)} async-done(((bf16[16,272,256]{2,1,0:T(8,128)(2,1)}), bf16[16,272,256]{2,1,0:T(8,128)(2,1)S(1)}, u32[]{:S(2)}, u32[]{:S(2)}) %all-to-all-start) | async-done | bytes 2228256 | tf_op jit(solution)/shard_map/all_to_all | solution.py:294
  55.8 15.4 %tiles.1 = (bf16[16,128,256]{2,1,0:T(8,128)(2,1)}, bf16[4,8,2,128,128]{4,3,2,1,0:T(8,128)(2,1)}, bf16[4,8,2,128,128]{4,3,2,1,0:T(8,128)(2,1)}) custom-call(s32[32,2]{1,0:T(8,128)} %copy.12.plan_in, s32[12]{0:T(128)} %bounds_in.1, bf16[16,272,256]{2,1,0:T(8,128)(2,1)S(1)} %all-to-all-done.packed_ref, bf16[2,2,4,2,64,128]{5,4,3,2,1,0:T(8,128)(2,1)S(1)} %bitcast.20, ...), custom_call_target="tpu_custom_call" | custom-call | tf_op jit(solution)/shard_map/tiles/pallas_call | solution.py:257
  71.4 4.0 %all-to-all-start.2 = ((bf16[16,128,256]{2,1,0:T(8,128)(2,1)}), bf16[16,128,256]{2,1,0:T(8,128)(2,1)S(1)}, u32[]{:S(2)}, u32[]{:S(2)}) async-start(bf16[16,128,256]{2,1,0:T(8,128)(2,1)} %get-tuple-element.24), calls=%async_computation.2 | async-start | bytes 2097152 | tf_op jit(solution)/shard_map/all_to_all | solution.py:294
  77.3 1.6 %collective-permute-start.10 = (bf16[1,4,2,128,128]{4,3,2,1,0:T(8,128)(2,1)S(1)}, bf16[1,4,2,128,128]{4,3,2,1,0:T(8,128)(2,1)S(1)}, u32[]{:S(2)}, u32[]{:S(2)}) collective-permute-start(bf16[1,4,2,128,128]{4,3,2,1,0:T(8,128)(2,1)S(1)} %get-tuple-element.18), channel_id=1, source_target_pairs={{0,8},{8,16},{16,24},{24,0},{1,9},{9,17},{17,25},{25,1},{2,10},{10... | collective-permute-start | bytes 786440 | tf_op jit(solution)/shard_map/ppermute | solution.py:282
  78.9 1.7 %collective-permute-start.11 = (bf16[1,4,2,128,128]{4,3,2,1,0:T(8,128)(2,1)S(1)}, bf16[1,4,2,128,128]{4,3,2,1,0:T(8,128)(2,1)S(1)}, u32[]{:S(2)}, u32[]{:S(2)}) collective-permute-start(bf16[1,4,2,128,128]{4,3,2,1,0:T(8,128)(2,1)S(1)} %get-tuple-element.19), channel_id=1, source_target_pairs={{0,24},{8,0},{16,8},{24,16},{1,25},{9,1},{17,9},{25,17},{2,26},{10... | collective-permute-start | bytes 786440 | tf_op jit(solution)/shard_map/ppermute | solution.py:282
  80.9 2.9 %collective-permute-start.14 = (bf16[1,4,2,128,128]{4,3,2,1,0:T(8,128)(2,1)S(1)}, bf16[1,4,2,128,128]{4,3,2,1,0:T(8,128)(2,1)S(1)}, u32[]{:S(2)}, u32[]{:S(2)}) collective-permute-start(bf16[1,4,2,128,128]{4,3,2,1,0:T(8,128)(2,1)S(1)} %get-tuple-element.22), channel_id=1, source_target_pairs={{0,24},{8,0},{16,8},{24,16},{1,25},{9,1},{17,9},{25,17},{2,26},{10... | collective-permute-start | bytes 786440 | tf_op jit(solution)/shard_map/ppermute | solution.py:282
  83.8 3.9 %collective-permute-done.10.refs_2_ = bf16[1,4,2,128,128]{4,3,2,1,0:T(8,128)(2,1)S(1)} collective-permute-done((bf16[1,4,2,128,128]{4,3,2,1,0:T(8,128)(2,1)S(1)}, bf16[1,4,2,128,128]{4,3,2,1,0:T(8,128)(2,1)S(1)}, u32[]{:S(2)}, u32[]{:S(2)}) %collective-permute-start.10) | collective-permute-done | bytes 262176 | tf_op jit(solution)/shard_map/ppermute | solution.py:282
  89.3 1.6 %collective-permute-start.12 = (bf16[1,4,2,128,128]{4,3,2,1,0:T(8,128)(2,1)S(1)}, bf16[1,4,2,128,128]{4,3,2,1,0:T(8,128)(2,1)S(1)}, u32[]{:S(2)}, u32[]{:S(2)}) collective-permute-start(bf16[1,4,2,128,128]{4,3,2,1,0:T(8,128)(2,1)S(1)} %get-tuple-element.20), channel_id=1, source_target_pairs={{0,8},{8,16},{16,24},{24,0},{1,9},{9,17},{17,25},{25,1},{2,10},{10... | collective-permute-start | bytes 786440 | tf_op jit(solution)/shard_map/ppermute | solution.py:282
  90.9 1.7 %collective-permute-start.15 = (bf16[1,4,2,128,128]{4,3,2,1,0:T(8,128)(2,1)S(1)}, bf16[1,4,2,128,128]{4,3,2,1,0:T(8,128)(2,1)S(1)}, u32[]{:S(2)}, u32[]{:S(2)}) collective-permute-start(bf16[1,4,2,128,128]{4,3,2,1,0:T(8,128)(2,1)S(1)} %get-tuple-element.23), channel_id=1, source_target_pairs={{0,24},{8,0},{16,8},{24,16},{1,25},{9,1},{17,9},{25,17},{2,26},{10... | collective-permute-start | bytes 786440 | tf_op jit(solution)/shard_map/ppermute | solution.py:282
  93.7 4.5 %collective-permute-done.12.last_a_ref = bf16[1,4,2,128,128]{4,3,2,1,0:T(8,128)(2,1)S(1)} collective-permute-done((bf16[1,4,2,128,128]{4,3,2,1,0:T(8,128)(2,1)S(1)}, bf16[1,4,2,128,128]{4,3,2,1,0:T(8,128)(2,1)S(1)}, u32[]{:S(2)}, u32[]{:S(2)}) %collective-permute-start.12) | collective-permute-done | bytes 262176 | tf_op jit(solution)/shard_map/ppermute | solution.py:282
  98.2 2.1 %own_slab.1 = bf16[16,2,64,128]{3,2,1,0:T(8,128)(2,1)} custom-call(bf16[4,8,2,128,128]{4,3,2,1,0:T(8,128)(2,1)S(1)} %copy-done, bf16[4,8,2,128,128]{4,3,2,1,0:T(8,128)(2,1)} %collective-permute-done.9.refs_1_.refs_3_.refs_5_.refs_7_.refs_4_.got_ref, bf16[1,4,2,128,128]{4,3,2,1,0:T(8,128)(2,1)S(1)} %collective-permute-done.12.last_a_ref, ...), custom_call_target="tpu_custom_call" | custom-call | tf_op jit(solution)/shard_map/own_slab/pallas_call | solution.py:362
  100.3 6.4 %all-to-all-start.3 = ((bf16[16,2,64,128]{3,2,1,0:T(8,128)(2,1)}), bf16[16,2,64,128]{3,2,1,0:T(8,128)(2,1)S(1)}, u32[]{:S(2)}, u32[]{:S(2)}) async-start(bf16[16,2,64,128]{3,2,1,0:T(8,128)(2,1)} %own_slab.1), calls=%async_computation.3 | async-start | bytes 1048576 | tf_op jit(solution)/shard_map/all_to_all | solution.py:294
  106.7 1.8 %unpack_q.1 = bf16[64,8192]{1,0:T(8,128)(2,1)} custom-call(bf16[4,4,128,256]{3,2,1,0:T(8,128)(2,1)S(1)} %bitcast.19), custom_call_target="tpu_custom_call" | custom-call | tf_op jit(solution)/shard_map/unpack_q/pallas_call | solution.py:373
  108.5 8.3 %all-to-all-done.3 = bf16[16,2,64,128]{3,2,1,0:T(8,128)(2,1)S(1)} async-done(((bf16[16,2,64,128]{3,2,1,0:T(8,128)(2,1)}), bf16[16,2,64,128]{3,2,1,0:T(8,128)(2,1)S(1)}, u32[]{:S(2)}, u32[]{:S(2)}) %all-to-all-start.3) | async-done | bytes 524320 | tf_op jit(solution)/shard_map/all_to_all | solution.py:294
  (34 shorter events, 11.6 us)
Async XLA Ops:
  2.3 19.6 %all-to-all-start.1 = ((bf16[16,2,64,128]{3,2,1,0:T(8,128)(2,1)}), bf16[16,2,64,128]{3,2,1,0:T(8,128)(2,1)S(1)}, u32[]{:S(2)}, u32[]{:S(2)}) async-start(bf16[16,2,64,128]{3,2,1,0:T(8,128)(2,1)} %bitcast.25), calls=%async_computation.1 | async-start | bytes 1048576 | tf_op jit(solution)/shard_map/all_to_all | solution.py:294
  22.0 25.6 %copy-start.1 = (s32[32,2]{0,1:T(2,128)S(1)}, s32[32,2]{0,1:T(2,128)}, u32[]{:S(2)}) copy-start(s32[32,2]{0,1:T(2,128)} %param.16) | copy-start | bytes 772
  22.0 33.9 %all-to-all-start = ((bf16[16,272,256]{2,1,0:T(8,128)(2,1)}), bf16[16,272,256]{2,1,0:T(8,128)(2,1)S(1)}, u32[]{:S(2)}, u32[]{:S(2)}) async-start(bf16[16,272,256]{2,1,0:T(8,128)(2,1)} %bitcast.24), calls=%async_computation | async-start | bytes 4456448 | tf_op jit(solution)/shard_map/all_to_all | solution.py:294
  25.8 13.5 %collective-permute-start.2 = (bf16[16,2,64,128]{3,2,1,0:T(8,128)(2,1)S(1)}, bf16[16,2,64,128]{3,2,1,0:T(8,128)(2,1)S(1)}, u32[]{:S(2)}, u32[]{:S(2)}) collective-permute-start(bf16[16,2,64,128]{3,2,1,0:T(8,128)(2,1)S(1)} %all-to-all-done.1), channel_id=1, source_target_pairs={{0,8},{8,16},{16,24},{24,0},{1,9},{9,17},{17,25},{25,1},{2,10},{10... | collective-permute-start | bytes 1572872 | tf_op jit(solution)/shard_map/ppermute | solution.py:282
  27.4 12.3 %collective-permute-start = (bf16[16,2,64,128]{3,2,1,0:T(8,128)(2,1)S(1)}, bf16[16,2,64,128]{3,2,1,0:T(8,128)(2,1)}, u32[]{:S(2)}, u32[]{:S(2)}) collective-permute-start(bf16[16,2,64,128]{3,2,1,0:T(8,128)(2,1)S(1)} %all-to-all-done.1), channel_id=1, source_target_pairs={{0,24},{8,0},{16,8},{24,16},{1,25},{9,1},{17,9},{25,17},{2,26},{10... | collective-permute-start | bytes 1572872 | tf_op jit(solution)/shard_map/ppermute | solution.py:282
  29.1 19.1 %collective-permute-start.4 = (bf16[16,2,64,128]{3,2,1,0:T(8,128)(2,1)S(1)}, bf16[16,2,64,128]{3,2,1,0:T(8,128)(2,1)}, u32[]{:S(2)}, u32[]{:S(2)}) collective-permute-start(bf16[16,2,64,128]{3,2,1,0:T(8,128)(2,1)S(1)} %all-to-all-done.1), channel_id=1, source_target_pairs={{0,4},{4,0},{1,5},{5,1},{2,6},{6,2},{3,7},{7,3},{8,12},{12,8},{9,1... | collective-permute-start | bytes 1572872 | tf_op jit(solution)/shard_map/ppermute | solution.py:290
  39.3 7.7 %collective-permute-start.3 = (bf16[8,2,64,128]{3,2,1,0:T(8,128)(2,1)S(1)}, bf16[8,2,64,128]{3,2,1,0:T(8,128)(2,1)S(1)}, u32[]{:S(2)}, u32[]{:S(2)}) collective-permute-start(bf16[8,2,64,128]{3,2,1,0:T(8,128)(2,1)S(1)} %slice.9), channel_id=1, source_target_pairs={{0,8},{8,16},{16,24},{24,0},{1,9},{9,17},{17,25},{25,1},{2,10},{10... | collective-permute-start | bytes 786440 | tf_op jit(solution)/shard_map/ppermute | solution.py:282
  40.7 6.9 %collective-permute-start.1 = (bf16[8,2,64,128]{3,2,1,0:T(8,128)(2,1)S(1)}, bf16[8,2,64,128]{3,2,1,0:T(8,128)(2,1)}, u32[]{:S(2)}, u32[]{:S(2)}) collective-permute-start(bf16[8,2,64,128]{3,2,1,0:T(8,128)(2,1)S(1)} %slice.8), channel_id=1, source_target_pairs={{0,24},{8,0},{16,8},{24,16},{1,25},{9,1},{17,9},{25,17},{2,26},{10... | collective-permute-start | bytes 786440 | tf_op jit(solution)/shard_map/ppermute | solution.py:282
  43.7 5.0 %collective-permute-start.8 = (bf16[16,2,64,128]{3,2,1,0:T(8,128)(2,1)S(1)}, bf16[16,2,64,128]{3,2,1,0:T(8,128)(2,1)}, u32[]{:S(2)}, u32[]{:S(2)}) collective-permute-start(bf16[16,2,64,128]{3,2,1,0:T(8,128)(2,1)S(1)} %collective-permute-done.2), channel_id=1, source_target_pairs={{0,4},{4,0},{1,5},{5,1},{2,6},{6,2},{3,7},{7,3},{8,12},{12,8},{9,1... | collective-permute-start | bytes 1572872 | tf_op jit(solution)/shard_map/ppermute | solution.py:290
  43.7 5.8 %collective-permute-start.5 = (bf16[16,2,64,128]{3,2,1,0:T(8,128)(2,1)}, bf16[16,2,64,128]{3,2,1,0:T(8,128)(2,1)}, u32[]{:S(2)}, u32[]{:S(2)}) collective-permute-start(bf16[16,2,64,128]{3,2,1,0:T(8,128)(2,1)} %collective-permute-done), channel_id=1, source_target_pairs={{0,4},{4,0},{1,5},{5,1},{2,6},{6,2},{3,7},{7,3},{8,12},{12,8},{9,1... | collective-permute-start | bytes 1572872 | tf_op jit(solution)/shard_map/ppermute | solution.py:290
  47.0 1.7 %collective-permute-start.7 = (bf16[8,2,64,128]{3,2,1,0:T(8,128)(2,1)S(1)}, bf16[8,2,64,128]{3,2,1,0:T(8,128)(2,1)}, u32[]{:S(2)}, u32[]{:S(2)}) collective-permute-start(bf16[8,2,64,128]{3,2,1,0:T(8,128)(2,1)S(1)} %collective-permute-done.3), channel_id=1, source_target_pairs={{0,4},{4,0},{1,5},{5,1},{2,6},{6,2},{3,7},{7,3},{8,12},{12,8},{9,1... | collective-permute-start | bytes 786440 | tf_op jit(solution)/shard_map/ppermute | solution.py:290
  47.6 1.9 %collective-permute-start.6 = (bf16[8,2,64,128]{3,2,1,0:T(8,128)(2,1)}, bf16[8,2,64,128]{3,2,1,0:T(8,128)(2,1)}, u32[]{:S(2)}, u32[]{:S(2)}) collective-permute-start(bf16[8,2,64,128]{3,2,1,0:T(8,128)(2,1)} %collective-permute-done.1), channel_id=1, source_target_pairs={{0,4},{4,0},{1,5},{5,1},{2,6},{6,2},{3,7},{7,3},{8,12},{12,8},{9,1... | collective-permute-start | bytes 786440 | tf_op jit(solution)/shard_map/ppermute | solution.py:290
  71.3 4.6 %copy-start = (bf16[4,8,2,128,128]{4,3,2,1,0:T(8,128)(2,1)S(1)}, bf16[4,8,2,128,128]{4,3,2,1,0:T(8,128)(2,1)}, u32[]{:S(2)}) copy-start(bf16[4,8,2,128,128]{4,3,2,1,0:T(8,128)(2,1)} %get-tuple-element.16.refs_0_.refs_2_.refs_4_.refs_6_.refs_3_.keep_ref) | copy-start | bytes 6291460
  71.3 4.6 %collective-permute-start.9 = (bf16[4,8,2,128,128]{4,3,2,1,0:T(8,128)(2,1)}, bf16[4,8,2,128,128]{4,3,2,1,0:T(8,128)(2,1)}, u32[]{:S(2)}, u32[]{:S(2)}) collective-permute-start(bf16[4,8,2,128,128]{4,3,2,1,0:T(8,128)(2,1)} %get-tuple-element.17), channel_id=1, source_target_pairs={{0,4},{4,0},{1,5},{5,1},{2,6},{6,2},{3,7},{7,3},{8,12},{12,8},{9,1... | collective-permute-start | bytes 6291464 | tf_op jit(solution)/shard_map/ppermute | solution.py:290
  71.4 28.9 %all-to-all-start.2 = ((bf16[16,128,256]{2,1,0:T(8,128)(2,1)}), bf16[16,128,256]{2,1,0:T(8,128)(2,1)S(1)}, u32[]{:S(2)}, u32[]{:S(2)}) async-start(bf16[16,128,256]{2,1,0:T(8,128)(2,1)} %get-tuple-element.24), calls=%async_computation.2 | async-start | bytes 2097152 | tf_op jit(solution)/shard_map/all_to_all | solution.py:294
  77.3 10.4 %collective-permute-start.10 = (bf16[1,4,2,128,128]{4,3,2,1,0:T(8,128)(2,1)S(1)}, bf16[1,4,2,128,128]{4,3,2,1,0:T(8,128)(2,1)S(1)}, u32[]{:S(2)}, u32[]{:S(2)}) collective-permute-start(bf16[1,4,2,128,128]{4,3,2,1,0:T(8,128)(2,1)S(1)} %get-tuple-element.18), channel_id=1, source_target_pairs={{0,8},{8,16},{16,24},{24,0},{1,9},{9,17},{17,25},{25,1},{2,10},{10... | collective-permute-start | bytes 786440 | tf_op jit(solution)/shard_map/ppermute | solution.py:282
  78.9 9.2 %collective-permute-start.11 = (bf16[1,4,2,128,128]{4,3,2,1,0:T(8,128)(2,1)S(1)}, bf16[1,4,2,128,128]{4,3,2,1,0:T(8,128)(2,1)S(1)}, u32[]{:S(2)}, u32[]{:S(2)}) collective-permute-start(bf16[1,4,2,128,128]{4,3,2,1,0:T(8,128)(2,1)S(1)} %get-tuple-element.19), channel_id=1, source_target_pairs={{0,24},{8,0},{16,8},{24,16},{1,25},{9,1},{17,9},{25,17},{2,26},{10... | collective-permute-start | bytes 786440 | tf_op jit(solution)/shard_map/ppermute | solution.py:282
  80.6 12.7 %collective-permute-start.13 = (bf16[1,4,2,128,128]{4,3,2,1,0:T(8,128)(2,1)S(1)}, bf16[1,4,2,128,128]{4,3,2,1,0:T(8,128)(2,1)S(1)}, u32[]{:S(2)}, u32[]{:S(2)}) collective-permute-start(bf16[1,4,2,128,128]{4,3,2,1,0:T(8,128)(2,1)S(1)} %get-tuple-element.21), channel_id=1, source_target_pairs={{0,8},{8,16},{16,24},{24,0},{1,9},{9,17},{17,25},{25,1},{2,10},{10... | collective-permute-start | bytes 786440 | tf_op jit(solution)/shard_map/ppermute | solution.py:282
  80.9 12.8 %collective-permute-start.14 = (bf16[1,4,2,128,128]{4,3,2,1,0:T(8,128)(2,1)S(1)}, bf16[1,4,2,128,128]{4,3,2,1,0:T(8,128)(2,1)S(1)}, u32[]{:S(2)}, u32[]{:S(2)}) collective-permute-start(bf16[1,4,2,128,128]{4,3,2,1,0:T(8,128)(2,1)S(1)} %get-tuple-element.22), channel_id=1, source_target_pairs={{0,24},{8,0},{16,8},{24,16},{1,25},{9,1},{17,9},{25,17},{2,26},{10... | collective-permute-start | bytes 786440 | tf_op jit(solution)/shard_map/ppermute | solution.py:282
  89.3 8.9 %collective-permute-start.12 = (bf16[1,4,2,128,128]{4,3,2,1,0:T(8,128)(2,1)S(1)}, bf16[1,4,2,128,128]{4,3,2,1,0:T(8,128)(2,1)S(1)}, u32[]{:S(2)}, u32[]{:S(2)}) collective-permute-start(bf16[1,4,2,128,128]{4,3,2,1,0:T(8,128)(2,1)S(1)} %get-tuple-element.20), channel_id=1, source_target_pairs={{0,8},{8,16},{16,24},{24,0},{1,9},{9,17},{17,25},{25,1},{2,10},{10... | collective-permute-start | bytes 786440 | tf_op jit(solution)/shard_map/ppermute | solution.py:282
  90.9 7.3 %collective-permute-start.15 = (bf16[1,4,2,128,128]{4,3,2,1,0:T(8,128)(2,1)S(1)}, bf16[1,4,2,128,128]{4,3,2,1,0:T(8,128)(2,1)S(1)}, u32[]{:S(2)}, u32[]{:S(2)}) collective-permute-start(bf16[1,4,2,128,128]{4,3,2,1,0:T(8,128)(2,1)S(1)} %get-tuple-element.23), channel_id=1, source_target_pairs={{0,24},{8,0},{16,8},{24,16},{1,25},{9,1},{17,9},{25,17},{2,26},{10... | collective-permute-start | bytes 786440 | tf_op jit(solution)/shard_map/ppermute | solution.py:282
  100.3 16.5 %all-to-all-start.3 = ((bf16[16,2,64,128]{3,2,1,0:T(8,128)(2,1)}), bf16[16,2,64,128]{3,2,1,0:T(8,128)(2,1)S(1)}, u32[]{:S(2)}, u32[]{:S(2)}) async-start(bf16[16,2,64,128]{3,2,1,0:T(8,128)(2,1)} %own_slab.1), calls=%async_computation.3 | async-start | bytes 1048576 | tf_op jit(solution)/shard_map/all_to_all | solution.py:294
